TPU v7x, 32 devices: a whole 2x2x4 slice. The times are simulated.
32 devices in a mesh: seq: 8 (over z, y), head: 4 (over x, core).
Axes of the slice: x: 2, y: 2, z: 4, core: 2. Of those that a mesh axis runs over, the one named last changes fastest.
Arguments:
- queries: bfloat16 [4096, 4096], P('seq', 'head'), may hold values from -60 to 60
- keys: bfloat16 [4096, 4096], P('seq', 'head'), may hold values from -8 to 8
- values: bfloat16 [4096, 4096], P('seq', 'head'), may hold values from -3000 to 3000
- gain: float32 [4096], P('head'), may hold values from 0.5 to 1.5
- grad_out: bfloat16 [4096, 4096], P('seq', 'head'), may hold values from -6 to 6
- pattern: int32 [32, 10], replicated, may hold values from 0 to 31, as said below
Outputs:
- normed: bfloat16 [4096, 4096], P('seq', 'head')
- grad_queries: bfloat16 [4096, 4096], P('seq', 'head')
- grad_keys: bfloat16 [4096, 4096], P('seq', 'head')
- grad_values: bfloat16 [4096, 4096], P('seq', 'head')
Inputs may be any that keep to these rules, and one draw needn't show every extreme that they name: `pattern`: row g lists 10 distinct blocks: g itself, then 3 - 1 further blocks of g's range, then 7 blocks of other ranges. All blocks of a range s that rows of other ranges list are one block, s's export, and each range's export is listed by some row of another range.
All inputs are finite; a program needn't handle non-finite values.
Results may differ from a plain program's by a relative error of at most 0.012.
Values may be sent and summed in bfloat16 or wider, within the bound.
No kernel may reach another device: no remote copies, remote signals or barrier semaphores. Data moves between devices by JAX's collectives and lax.ppermute only.
A program may use at most 192 MiB of HBM per device.

v0:
```python
import jax
import jax.numpy as jnp
from jax import lax
from jax.sharding import PartitionSpec as P

HEAD_SIZE = 128
BLK = 128
LOC = 3
REM = 7
FEAT = 4096


epsilon = 1e-06


def shards(queries, keys, values, gain, grad_out, pattern):
    n_seq = lax.axis_size("seq")
    myself = lax.axis_index("seq")
    tokens, width = queries.shape
    heads = width // HEAD_SIZE
    nblocks = tokens // BLK
    softmax_scale = 1.0 / HEAD_SIZE**0.5
    owner = pattern // nblocks
    row_range = (jnp.arange(pattern.shape[0], dtype=jnp.int32) // nblocks)[:, None]
    remote = owner != row_range
    mine = jnp.where(remote & (owner == myself), pattern, -1)
    export_block = jnp.max(mine) - myself * nblocks
    my_rows = lax.dynamic_slice_in_dim(pattern, myself * nblocks, nblocks, 0)
    local_index = my_rows[:, :LOC] - myself * nblocks
    remote_owner = my_rows[:, LOC:] // nblocks
    key_export = lax.dynamic_slice_in_dim(keys, export_block * BLK, BLK, 0)
    value_export = lax.dynamic_slice_in_dim(values, export_block * BLK, BLK, 0)
    importer = (jnp.max(mine.reshape(n_seq, -1), axis=1) >= 0)[:, None, None]
    empty = jnp.zeros((), keys.dtype)
    key_send = jnp.where(importer, key_export[None], empty)
    value_send = jnp.where(importer, value_export[None], empty)
    key_remote, value_remote = (
        lax.all_to_all(key_send, "seq", split_axis=0, concat_axis=0, tiled=True),
        lax.all_to_all(value_send, "seq", split_axis=0, concat_axis=0, tiled=True),
    )
    rows_group = min(tokens, 512)
    ngroups = tokens // rows_group
    per_group = rows_group // BLK
    key_import = key_remote[remote_owner].reshape(ngroups, per_group, REM * BLK, heads, HEAD_SIZE)
    value_import = value_remote[remote_owner].reshape(
        ngroups, per_group, REM * BLK, heads, HEAD_SIZE
    )
    block_mask = jnp.any(
        local_index[:, :, None] == jnp.arange(nblocks, dtype=jnp.int32)[None, None, :], axis=1
    )
    token_mask = jnp.repeat(jnp.repeat(block_mask, BLK, axis=0), BLK, axis=1).reshape(
        ngroups, rows_group, tokens
    )
    owner_groups = remote_owner.reshape(ngroups, per_group, REM)
    keys_heads = keys.reshape(tokens, heads, HEAD_SIZE)
    values_heads = values.reshape(tokens, heads, HEAD_SIZE)
    query_groups = queries.reshape(ngroups, rows_group, heads, HEAD_SIZE)

    def probabilities(query_group, mask_group, key_group):
        local_scores = (
            jnp.einsum("qhd,khd->hqk", query_group, keys_heads, preferred_element_type=jnp.float32)
            * softmax_scale
        )
        local_scores = jnp.where(mask_group[None], local_scores, -1e30)
        query_blocks = query_group.reshape(per_group, BLK, heads, HEAD_SIZE)
        far_scores = (
            jnp.einsum(
                "bqhd,bkhd->hbqk", query_blocks, key_group, preferred_element_type=jnp.float32
            )
            * softmax_scale
        )
        far_scores = far_scores.reshape(heads, rows_group, REM * BLK)
        peak = jnp.maximum(
            jnp.max(local_scores, axis=-1, keepdims=True),
            jnp.max(far_scores, axis=-1, keepdims=True),
        )
        local_expo = jnp.exp(local_scores - peak)
        far_expo = jnp.exp(far_scores - peak)
        total = jnp.sum(local_expo, axis=-1, keepdims=True) + jnp.sum(
            far_expo, axis=-1, keepdims=True
        )
        return (local_expo / total, far_expo / total)

    def forward_group(inputs):
        query_group, mask_group, key_group, value_group = inputs
        local_prob, far_prob = probabilities(query_group, mask_group, key_group)
        local_out = jnp.einsum(
            "hqk,khd->qhd",
            local_prob.astype(jnp.bfloat16),
            values_heads,
            preferred_element_type=jnp.float32,
        )
        far_prob16 = far_prob.reshape(heads, per_group, BLK, REM * BLK).astype(jnp.bfloat16)
        far_out = jnp.einsum(
            "hbqk,bkhd->bqhd", far_prob16, value_group, preferred_element_type=jnp.float32
        )
        return (local_out + far_out.reshape(rows_group, heads, HEAD_SIZE)).reshape(
            rows_group, width
        )

    attended = lax.map(forward_group, (query_groups, token_mask, key_import, value_import)).reshape(
        tokens, width
    )
    scaled_grad = gain * grad_out.astype(jnp.float32)
    squares_all, cross_all = lax.psum(
        (jnp.sum(attended * attended, axis=1), jnp.sum(scaled_grad * attended, axis=1)), "head"
    )
    inverse = lax.rsqrt(squares_all / FEAT + epsilon)[:, None]
    normed = (attended * inverse * gain).astype(jnp.bfloat16)
    d_attended = (
        inverse * scaled_grad - attended * inverse**3 * cross_all[:, None] / FEAT
    ).astype(jnp.bfloat16)

    def backward_group(carry, inputs):
        key_local, value_local, key_far, value_far = carry
        query_group, mask_group, key_group, value_group, owners, grad_group, out_group = inputs
        local_prob, far_prob = probabilities(query_group, mask_group, key_group)
        delta = jnp.sum(grad_group.astype(jnp.float32) * out_group, axis=-1).T[:, :, None]
        local_dprob = jnp.einsum(
            "qhd,khd->hqk", grad_group, values_heads, preferred_element_type=jnp.float32
        )
        grad_blocks = grad_group.reshape(per_group, BLK, heads, HEAD_SIZE)
        far_dprob = jnp.einsum(
            "bqhd,bkhd->hbqk", grad_blocks, value_group, preferred_element_type=jnp.float32
        ).reshape(heads, rows_group, REM * BLK)
        local_dscore = (local_prob * (local_dprob - delta)).astype(jnp.bfloat16)
        far_dscore = (
            (far_prob * (far_dprob - delta))
            .astype(jnp.bfloat16)
            .reshape(heads, per_group, BLK, REM * BLK)
        )
        local_dq = jnp.einsum(
            "hqk,khd->qhd", local_dscore, keys_heads, preferred_element_type=jnp.float32
        )
        far_dq = jnp.einsum(
            "hbqk,bkhd->bqhd", far_dscore, key_group, preferred_element_type=jnp.float32
        ).reshape(rows_group, heads, HEAD_SIZE)
        query_gradient = (
            (softmax_scale * (local_dq + far_dq)).astype(jnp.bfloat16).reshape(rows_group, width)
        )
        key_local = key_local + softmax_scale * jnp.einsum(
            "hqk,qhd->khd", local_dscore, query_group, preferred_element_type=jnp.float32
        )
        value_local = value_local + jnp.einsum(
            "hqk,qhd->khd",
            local_prob.astype(jnp.bfloat16),
            grad_group,
            preferred_element_type=jnp.float32,
        )
        query_blocks = query_group.reshape(per_group, BLK, heads, HEAD_SIZE)
        far_prob16 = far_prob.reshape(heads, per_group, BLK, REM * BLK).astype(jnp.bfloat16)
        key_terms = softmax_scale * jnp.einsum(
            "hbqk,bqhd->bkhd", far_dscore, query_blocks, preferred_element_type=jnp.float32
        )
        value_terms = jnp.einsum(
            "hbqk,bqhd->bkhd", far_prob16, grad_blocks, preferred_element_type=jnp.float32
        )
        key_terms = key_terms.reshape(per_group, REM, BLK, width)
        value_terms = value_terms.reshape(per_group, REM, BLK, width)
        selector = (owners[:, :, None] == jnp.arange(n_seq, dtype=jnp.int32)[None, None, :]).astype(
            jnp.float32
        )
        key_far = key_far + jnp.einsum(
            "bjs,bjkw->skw", selector, key_terms, precision=lax.Precision.HIGHEST
        )
        value_far = value_far + jnp.einsum(
            "bjs,bjkw->skw", selector, value_terms, precision=lax.Precision.HIGHEST
        )
        return ((key_local, value_local, key_far, value_far), query_gradient)

    zero_local = jnp.zeros((tokens, heads, HEAD_SIZE), jnp.float32)
    zero_far = jnp.zeros((n_seq, BLK, width), jnp.float32)
    scanned = (
        query_groups,
        token_mask,
        key_import,
        value_import,
        owner_groups,
        d_attended.reshape(ngroups, rows_group, heads, HEAD_SIZE),
        attended.reshape(ngroups, rows_group, heads, HEAD_SIZE),
    )
    (key_local, value_local, key_part, value_part), grad_queries = lax.scan(
        backward_group, (zero_local, zero_local, zero_far, zero_far), scanned
    )
    key_back, value_back = (
        lax.all_to_all(
            key_part.astype(jnp.bfloat16), "seq", split_axis=0, concat_axis=0, tiled=True
        ),
        lax.all_to_all(
            value_part.astype(jnp.bfloat16), "seq", split_axis=0, concat_axis=0, tiled=True
        ),
    )
    key_in = jnp.sum(key_back.astype(jnp.float32), axis=0)
    value_in = jnp.sum(value_back.astype(jnp.float32), axis=0)
    key_own = key_local.reshape(tokens, width)
    value_own = value_local.reshape(tokens, width)
    start = export_block * BLK
    key_own = lax.dynamic_update_slice_in_dim(
        key_own, lax.dynamic_slice_in_dim(key_own, start, BLK, 0) + key_in, start, 0
    )
    value_own = lax.dynamic_update_slice_in_dim(
        value_own, lax.dynamic_slice_in_dim(value_own, start, BLK, 0) + value_in, start, 0
    )
    return (
        normed,
        grad_queries.reshape(tokens, width),
        key_own.astype(jnp.bfloat16),
        value_own.astype(jnp.bfloat16),
    )


def solution(mesh):
    in_specs = (
        P("seq", "head"),
        P("seq", "head"),
        P("seq", "head"),
        P("head"),
        P("seq", "head"),
        P(),
    )
    out_specs = (P("seq", "head"), P("seq", "head"), P("seq", "head"), P("seq", "head"))
    return jax.shard_map(shards, mesh=mesh, in_specs=in_specs, out_specs=out_specs, check_vma=False)
```

profile of v0, /device:TPU:0, one launch (start us, length us, event | category | flops | bytes accessed | tf_op | source)
XLA Modules:
  0.0 425.3 jit_solution(3423532590682811631)
XLA Ops:
  5.7 55.4 %all_to_all.20 = bf16[8,128,1024]{2,1,0:T(8,128)(2,1)} all-to-all(bf16[8,128,1024]{2,1,0:T(8,128)(2,1)S(1)} %get-tuple-element.100), channel_id=1, replica_groups=mesh['seq'=8,'head'=4] {'seq'}, dimensions={0} | all-to-all | bytes 4194304 | tf_op jit(solution)/shard_map/all_to_all | solution.py:38
  70.7 6.7 %fusion.5 = (f32[8,512]{1,0:T(8,128)S(1)}, f32[8,512,512]{1,2,0:T(8,128)}) fusion(pred[512,512]{0,1:T(8,128)(4,1)S(1)} %bitcast.140, bf16[512,8,128]{0,2,1:T(8,128)(2,1)} %bitcast.126, bf16[512,8,128]{0,2,1:T(8,128)(2,1)} %bitcast.128), kind=kOutput, calls=%fused_computation.15 | convolution fusion | flops 543158272 | bytes 10764288 | tf_op jit(solution)/shard_map/while/body/eval_jaxpr/qhd,khd->hqk/dot_general | solution.py:61
  77.3 6.4 %gather_fusion = bf16[28,128,1024]{2,1,0:T(8,128)(2,1)} fusion(bf16[8,128,1024]{2,1,0:T(8,128)(2,1)} %all_to_all.20, s32[1024]{0:T(1024)S(1)} %pad_clamp_fusion), kind=kCustom, calls=%fused_computation | custom fusion | bytes 14680176 | tf_op jit(solution)/shard_map/gather | solution.py:44
  83.7 7.9 %copy.214 = bf16[448,8,8,128]{3,2,1,0:T(8,128)(2,1)} copy(bf16[448,8,8,128]{3,1,2,0:T(8,128)(2,1)} %bitcast.122) | data formatting | bytes 14680064
  91.6 21.0 %all-to-all-done.1 = bf16[8,128,1024]{2,1,0:T(8,128)(2,1)S(1)} async-done(((bf16[8,128,1024]{2,1,0:T(8,128)(2,1)}), bf16[8,128,1024]{2,1,0:T(8,128)(2,1)S(1)}, u32[]{:S(2)}, u32[]{:S(2)}) %all-to-all-start.1) | async-done | bytes 2097184 | tf_op jit(solution)/shard_map/all_to_all | solution.py:39
  117.6 8.2 %copy.218 = bf16[448,8,8,128]{3,2,1,0:T(8,128)(2,1)} copy(bf16[448,8,8,128]{3,1,2,0:T(8,128)(2,1)} %bitcast.121) | data formatting | bytes 14680064
  125.7 10.7 %bitcast_reduce_fusion = (f32[8,4,128]{2,1,0:T(4,128)S(1)}, f32[8,4,896,128]{3,2,1,0:T(8,128)}) fusion(bf16[4,128,8,128]{3,2,1,0:T(8,128)(2,1)S(1)} %bitcast.123, bf16[4,896,8,128]{3,2,1,0:T(8,128)(2,1)} %bitcast.119), kind=kOutput, calls=%fused_computation.5 | convolution fusion | flops 946860032 | bytes 23085056 | tf_op jit(solution)/shard_map/while/body/eval_jaxpr/bqhd,bkhd->hbqk/dot_general | solution.py:67
  136.4 7.7 %fusion.4 = f32[8,4,128]{2,1,0:T(4,128)S(1)} fusion(f32[8,4,896,128]{3,2,1,0:T(8,128)} %get-tuple-element.102, f32[8,4,128]{2,1,0:T(4,128)S(1)} %copy_maximum_fusion), kind=kLoop, calls=%fused_computation.10 | loop fusion | flops 11005952 | bytes 14712832 | tf_op jit(solution)/shard_map/while/body/eval_jaxpr/reduce_sum | solution.py:79
  145.9 11.7 %fusion.19 = bf16[8,4,128,896]{2,3,1,0:T(8,128)(2,1)} fusion(f32[8,4,128]{2,1,0:T(4,128)S(1)} %copy_add_fusion, f32[8,4,128]{2,1,0:T(4,128)S(1)} %copy_maximum_fusion, f32[8,4,896,128]{3,2,1,0:T(8,128)} %get-tuple-element.102), kind=kLoop, calls=%fused_computation.33 | loop fusion | flops 14680064 | bytes 22052864 | tf_op jit(solution)/shard_map/while/body/eval_jaxpr/convert_element_type | solution.py:93
  157.6 10.0 %fusion.30 = f32[4,128,8,128]{3,1,2,0:T(8,128)} fusion(bf16[8,4,128,896]{2,3,1,0:T(8,128)(2,1)} %fusion.19, bf16[4,896,8,128]{3,2,1,0:T(8,128)(2,1)} %bitcast.132), kind=kOutput, calls=%fused_computation.50 | convolution fusion | flops 939524096 | bytes 16777216 | tf_op jit(solution)/shard_map/while/body/eval_jaxpr/hbqk,bkhd->bqhd/dot_general | solution.py:94
  171.5 8.3 %multiply_reduce_fusion.2 = (f32[512]{0:T(512)S(1)}, f32[512,8,128]{0,2,1:T(8,128)}) fusion(f32[512,8,128]{0,2,1:T(8,128)} %reshape.160, f32[8,512]{1,0:T(8,128)S(1)} %bitcast_add_fusion.2, f32[8,512]{1,0:T(8,128)S(1)} %bitcast_maximum_fusion, f32[8,512,512]{1,2,0:T(8,128)} %get-tuple-element.104, pred[512,512]{0,1:T(8,128)(4,1)S(1)} %bitcast.142, ...), kind=kOutput, calls=%fused_computation.43 | convolution fusion | flops 548929024 | bytes 13928448 | tf_op jit(solution)/shard_map/while/body/eval_jaxpr/hqk,khd->qhd/dot_general | solution.py:87
  194.9 10.5 %multiply_convert_fusion = bf16[8,4,128,896]{2,3,1,0:T(8,128)(2,1)S(1)} fusion(bf16[4,896,8,128]{3,2,1,0:T(8,128)(2,1)} %bitcast.133, f32[8,4,128]{2,1,0:T(4,128)S(1)} %copy.169, f32[8,4,128]{2,1,0:T(4,128)S(1)} %copy_add_fusion, f32[8,4,128]{2,1,0:T(4,128)S(1)} %copy_maximum_fusion, f32[8,4,896,128]{3,2,1,0:T(8,128)} %get-tuple-element.102, ...), kind=kOutput, calls=%fused_computation.8 | convolution fusion | flops 961544192 | bytes 30457856 | tf_op jit(solution)/shard_map/while/body/eval_jaxpr/bqhd,bkhd->hbqk/dot_general | solution.py:123
  208.3 7.8 %multiply_bitcast_fusion = f32[4,896,8,128]{3,1,2,0:T(8,128)} fusion(bf16[8,4,128,896]{2,3,1,0:T(8,128)(2,1)S(1)} %multiply_convert_fusion, bf16[4,128,8,128]{3,2,1,0:T(8,128)(2,1)} %bitcast.124), kind=kOutput, calls=%fused_computation.7 | convolution fusion | flops 943194112 | bytes 23068672 | tf_op jit(solution)/shard_map/while/body/eval_jaxpr/hbqk,bqhd->bkhd/dot_general | solution.py:152
  216.1 18.8 %copy.180 = f32[4,896,8,128]{3,2,1,0:T(8,128)} copy(f32[4,896,8,128]{3,1,2,0:T(8,128)} %multiply_bitcast_fusion) | data formatting | bytes 29360128 | tf_op jit(solution)/shard_map/while/body/eval_jaxpr/mul | solution.py:152
  234.9 15.8 %reshape.166 = f32[4,7,128,1024]{3,2,1,0:T(8,128)} reshape(f32[4,896,8,128]{3,2,1,0:T(8,128)} %copy.180) | data formatting | bytes 29360128 | tf_op jit(solution)/shard_map/while/body/eval_jaxpr/reshape | solution.py:158
  250.8 25.8 %bitcast_convert_fusion.1 = bf16[8,128,1024]{2,0,1:T(8,128)(2,1)S(1)} fusion(f32[4,7,128,1024]{3,2,1,0:T(8,128)} %reshape.166, s32[4,7]{1,0:T(4,128)S(1)} %copy.177), kind=kOutput, calls=%fused_computation.30 | convolution fusion | flops 353370336 | bytes 16777328 | tf_op jit(solution)/shard_map/while/body/eval_jaxpr/bjs,bjkw->skw/dot_general | solution.py:163
  284.0 10.0 %fusion.35 = f32[4,128,8,128]{3,1,2,0:T(8,128)} fusion(bf16[8,4,128,896]{2,3,1,0:T(8,128)(2,1)} %copy-done.1, bf16[4,896,8,128]{3,2,1,0:T(8,128)(2,1)} %bitcast.120), kind=kOutput, calls=%fused_computation.51 | convolution fusion | flops 939524096 | bytes 16777216 | tf_op jit(solution)/shard_map/while/body/eval_jaxpr/hbqk,bkhd->bqhd/dot_general | solution.py:135
  300.1 10.6 %convolution_bitcast_fusion = f32[4,896,8,128]{1,3,2,0:T(8,128)} fusion(bf16[8,4,128,896]{2,3,1,0:T(8,128)(2,1)} %fusion.19, bf16[4,128,8,128]{3,2,1,0:T(8,128)(2,1)S(1)} %bitcast.135), kind=kOutput, calls=%fused_computation.14 | convolution fusion | flops 939524096 | bytes 23068672 | tf_op jit(solution)/shard_map/while/body/eval_jaxpr/hbqk,bqhd->bkhd/dot_general | solution.py:155
  310.7 17.0 %reshape.194 = f32[4,7,128,1024]{2,1,3,0:T(8,128)} reshape(f32[4,896,8,128]{1,3,2,0:T(8,128)} %convolution_bitcast_fusion) | data formatting | bytes 29360128 | tf_op jit(solution)/shard_map/while/body/eval_jaxpr/reshape | solution.py:159
  327.8 16.5 %copy.189 = f32[4,7,128,1024]{3,1,0,2:T(8,128)} copy(f32[4,7,128,1024]{2,1,3,0:T(8,128)} %reshape.194) | data formatting | bytes 29360128 | tf_op jit(solution)/shard_map/while/body/eval_jaxpr/reshape | solution.py:159
  344.3 18.1 %bitcast_convert_fusion = bf16[8,128,1024]{2,0,1:T(8,128)(2,1)S(1)} fusion(f32[4,7,128,1024]{3,1,0,2:T(8,128)} %copy.189, s32[4,7]{1,0:T(4,128)S(1)} %copy.177), kind=kOutput, calls=%fused_computation.29 | convolution fusion | flops 353370336 | bytes 16777328 | tf_op jit(solution)/shard_map/while/body/eval_jaxpr/bjs,bjkw->skw/dot_general | solution.py:166
  365.0 6.3 %all-to-all-start.3 = ((bf16[8,128,1024]{2,1,0:T(8,128)(2,1)}), bf16[8,128,1024]{2,1,0:T(8,128)(2,1)}, u32[]{:S(2)}, u32[]{:S(2)}) async-start(bf16[8,128,1024]{2,1,0:T(8,128)(2,1)} %copy.190), calls=%async_computation.3 | async-start | bytes 4194304 | tf_op jit(solution)/shard_map/all_to_all | solution.py:189
  390.6 7.6 %fusion.24 = f32[8,128,512]{2,1,0:T(8,128)} fusion(bf16[512,8,128]{0,2,1:T(8,128)(2,1)} %bitcast.136, f32[8,512,512]{1,2,0:T(8,128)} %get-tuple-element.104, f32[8,512]{1,0:T(8,128)S(1)} %bitcast_add_fusion.2, f32[8,512]{1,0:T(8,128)S(1)} %bitcast_maximum_fusion, pred[512,512]{0,1:T(8,128)(4,1)S(1)} %bitcast.144), kind=kOutput, calls=%fused_computation.44 | convolution fusion | flops 547356672 | bytes 11829248 | tf_op jit(solution)/shard_map/while/body/eval_jaxpr/hqk,qhd->khd/dot_general | solution.py:144
  404.4 13.8 %all-to-all-done.3 = bf16[8,128,1024]{2,1,0:T(8,128)(2,1)} async-done(((bf16[8,128,1024]{2,1,0:T(8,128)(2,1)}), bf16[8,128,1024]{2,1,0:T(8,128)(2,1)}, u32[]{:S(2)}, u32[]{:S(2)}) %all-to-all-start.3) | async-done | bytes 2097184 | tf_op jit(solution)/shard_map/all_to_all | solution.py:189
  (88 shorter events, 90.6 us)
Async XLA Ops:
  3.9 63.1 %copy-start.11 = (s32[32,10]{0,1:T(8,128)S(1)}, s32[32,10]{0,1:T(8,128)}, u32[]{:S(2)}) copy-start(s32[32,10]{0,1:T(8,128)} %param.11) | copy-start | bytes 3844
  4.0 63.8 %copy-start.10 = (bf16[512,1024]{1,0:T(8,128)(2,1)S(1)}, bf16[512,1024]{1,0:T(8,128)(2,1)}, u32[]{:S(2)}) copy-start(bf16[512,1024]{1,0:T(8,128)(2,1)} %param.6) | copy-start | bytes 3145732
  61.1 51.5 %all-to-all-start.1 = ((bf16[8,128,1024]{2,1,0:T(8,128)(2,1)}), bf16[8,128,1024]{2,1,0:T(8,128)(2,1)S(1)}, u32[]{:S(2)}, u32[]{:S(2)}) async-start(bf16[8,128,1024]{2,1,0:T(8,128)(2,1)} %get-tuple-element.99), calls=%async_computation.1 | async-start | bytes 4194304 | tf_op jit(solution)/shard_map/all_to_all | solution.py:39
  70.6 55.2 %copy-start.2 = (bf16[64,8,8,128]{3,2,1,0:T(8,128)(2,1)}, bf16[64,8,8,128]{3,2,1,0:T(8,128)(2,1)S(1)}, u32[]{:S(2)}) copy-start(bf16[64,8,8,128]{3,2,1,0:T(8,128)(2,1)S(1)} %copy.215) | copy-start | bytes 3145732
  117.5 26.6 %slice-start = ((s8[8388608]{0:T(1024)(128)(4,1)}), s8[4194304]{0:T(1024)(128)(4,1)S(1)}, s32[]{:S(2)}) async-start(s8[8388608]{0:T(1024)(128)(4,1)} %bitcast.117), calls=%async_computation.4 | async-start | bytes 8388608
  125.7 18.4 %slice-start.1 = ((s8[8388608]{0:T(1024)(128)(4,1)}), s8[4194304]{0:T(1024)(128)(4,1)S(1)}, s32[]{:S(2)}) async-start(s8[8388608]{0:T(1024)(128)(4,1)} %bitcast.117), calls=%async_computation.5 | async-start | bytes 8388608
  171.5 10.2 %copy-start.7 = (bf16[512,1024]{1,0:T(8,128)(2,1)S(1)}, bf16[512,1024]{1,0:T(8,128)(2,1)}, u32[]{:S(2)}) copy-start(bf16[512,1024]{1,0:T(8,128)(2,1)} %param.10) | copy-start | bytes 3145732
  171.5 10.2 %copy-start.12 = (f32[1024]{0:T(1024)S(1)}, f32[1024]{0:T(1024)}, u32[]{:S(2)}) copy-start(f32[1024]{0:T(1024)} %param.9) | copy-start | bytes 12292
  191.3 3.6 copy-start.8
  205.4 2.9 copy-start.1
  279.1 85.9 %all-to-all-start.2 = ((bf16[8,128,1024]{2,1,0:T(8,128)(2,1)}), bf16[8,128,1024]{2,1,0:T(8,128)(2,1)S(1)}, u32[]{:S(2)}, u32[]{:S(2)}) async-start(bf16[8,128,1024]{2,1,0:T(8,128)(2,1)} %copy.182), calls=%async_computation.2 | async-start | bytes 4194304 | tf_op jit(solution)/shard_map/all_to_all | solution.py:186
  294.0 6.1 %copy-start.6 = (bf16[64,8,8,128]{3,2,1,0:T(8,128)(2,1)S(1)}, bf16[64,8,8,128]{3,2,1,0:T(8,128)(2,1)}, u32[]{:S(2)}) copy-start(bf16[64,8,8,128]{3,2,1,0:T(8,128)(2,1)} %copy.219) | copy-start | bytes 3145732
  362.4 8.9 %copy-start.9 = (bf16[512,1024]{0,1:T(8,128)(2,1)S(1)}, bf16[512,1024]{0,1:T(8,128)(2,1)}, u32[]{:S(2)}) copy-start(bf16[512,1024]{0,1:T(8,128)(2,1)} %copy-done.8) | copy-start | bytes 3145732
  365.0 12.0 %copy-start.5 = (bf16[8,128,1024]{2,1,0:T(8,128)(2,1)}, bf16[8,128,1024]{2,1,0:T(8,128)(2,1)S(1)}, u32[]{:S(2)}) copy-start(bf16[8,128,1024]{2,1,0:T(8,128)(2,1)S(1)} %all-to-all-done.2) | copy-start | bytes 6291460
  365.0 53.1 %all-to-all-start.3 = ((bf16[8,128,1024]{2,1,0:T(8,128)(2,1)}), bf16[8,128,1024]{2,1,0:T(8,128)(2,1)}, u32[]{:S(2)}, u32[]{:S(2)}) async-start(bf16[8,128,1024]{2,1,0:T(8,128)(2,1)} %copy.190), calls=%async_computation.3 | async-start | bytes 4194304 | tf_op jit(solution)/shard_map/all_to_all | solution.py:189
  371.4 7.6 %copy-start.3 = (bf16[512,1024]{0,1:T(8,128)(2,1)S(1)}, bf16[512,1024]{0,1:T(8,128)(2,1)}, u32[]{:S(2)}) copy-start(bf16[512,1024]{0,1:T(8,128)(2,1)} %copy.210) | copy-start | bytes 3145732
  377.0 2.0 copy-start
  379.0 4.8 %copy-start.4 = (bf16[512,1024]{0,1:T(8,128)(2,1)S(1)}, bf16[512,1024]{0,1:T(8,128)(2,1)}, u32[]{:S(2)}) copy-start(bf16[512,1024]{0,1:T(8,128)(2,1)} %copy.211) | copy-start | bytes 3145732
where the time goes:
time: 433 us; the launch traced here: 425 us
  matrix products  139 us (32%)
  local copies, waits for them, and re-layouts  133 us (31%)
  blocking collectives  61.1 us (14%)
  other arithmetic  40.2 us (9%)
  waiting for transfers between devices  34.8 us (8%)
  starting transfers between devices  14.8 us (3%)
    all_to_all x1, blocking collectives, shards(): lax.all_to_all(key_send, 'seq', split_axis=0, concat_axis=0, tiled=True)  55.4 us
    reshape x2, local copies, waits for them, and re-layouts, backward_group(): value_terms = value_terms.reshape(per_group, REM, BLK, width)  33.6 us
    unnamed x37, local copies, waits for them, and re-layouts  26.1 us
    dot_general x1, matrix products, backward_group(): jnp.einsum('bjs,bjkw->skw', selector, key_terms, precision=lax.Precision....  25.8 us
    all_to_all x1, waiting for transfers between devices, shards(): lax.all_to_all(value_send, 'seq', split_axis=0, concat_axis=0, tiled=True)  21 us
    mul x1, local copies, waits for them, and re-layouts, backward_group(): softmax_scale * jnp.einsum('hbqk,bqhd->bkhd', far_dscore, query_blocks, p...  18.8 us
    dot_general x1, matrix products, backward_group(): jnp.einsum('bjs,bjkw->skw', selector, value_terms, precision=lax.Precisio...  18.1 us
    reshape x1, local copies, waits for them, and re-layouts, backward_group(): key_terms = key_terms.reshape(per_group, REM, BLK, width)  15.8 us
  transfers between devices with their start and end apart: 3, of which 2 were waited for; matrix products, arithmetic and copies ran while one was open for 33% of the time, Pallas kernels for 0%

commit v1 on v0

v1 whole, which is shorter than its diff:
```python
import functools

import jax
import jax.numpy as jnp
from jax import lax
from jax.experimental import pallas as pl
from jax.experimental.pallas import tpu as pltpu
from jax.sharding import PartitionSpec as P

HEAD_SIZE = 128
BLK = 128
LOC = 3
REM = 7
FEAT = 4096
LOW = -1e30

epsilon = 1e-06
softmax_scale = 1.0 / HEAD_SIZE**0.5

NT = (((1,), (1,)), ((), ()))
NN = (((1,), (0,)), ((), ()))
TN = (((0,), (0,)), ((), ()))


def dot(a, b, dims):
    return lax.dot_general(a, b, dims, preferred_element_type=jnp.float32)


def softmax_kernel(nblocks, masked, bias_ref, q_ref, local_ref, *refs):
    slots = refs[:-2]
    p_ref, cat_ref = refs[-2:]
    tokens = q_ref.shape[0]
    cat_ref[:tokens] = local_ref[...]
    for j, slot in enumerate(slots):
        cat_ref[tokens + j * BLK : tokens + (j + 1) * BLK] = slot[...]
    for g in range(nblocks):
        rows = slice(g * BLK, (g + 1) * BLK)
        scores = dot(q_ref[rows], cat_ref[...], NT) * softmax_scale
        parts = []
        for j in range(nblocks + len(slots)):
            part = scores[:, j * BLK : (j + 1) * BLK]
            if j < nblocks or masked:
                part = part + bias_ref[g, j]
            parts.append(part)
        scores = jnp.concatenate(parts, axis=1)
        peak = jnp.max(scores, axis=1, keepdims=True)
        expo = jnp.exp(scores - peak)
        total = jnp.sum(expo, axis=1, keepdims=True)
        p_ref[0, rows] = (expo * (1.0 / total)).astype(p_ref.dtype)


def attend_kernel(p_ref, local_ref, grad_ref, gain_ref, *refs):
    slots = refs[:-5]
    o_ref, stat_ref, cat_ref, square_ref, cross_ref = refs[-5:]
    head = pl.program_id(0)
    tokens = local_ref.shape[0]
    cat_ref[:tokens] = local_ref[...]
    for j, slot in enumerate(slots):
        cat_ref[tokens + j * BLK : tokens + (j + 1) * BLK] = slot[...]
    out = dot(p_ref[0], cat_ref[...], NN)
    o_ref[...] = out
    scaled = grad_ref[...].astype(jnp.float32) * gain_ref[...]

    @pl.when(head == 0)
    def _():
        square_ref[...] = jnp.zeros_like(square_ref)
        cross_ref[...] = jnp.zeros_like(cross_ref)

    square_ref[...] += out * out
    cross_ref[...] += scaled * out

    @pl.when(head == pl.num_programs(0) - 1)
    def _():
        ones = jnp.ones((8, HEAD_SIZE), jnp.float32)
        total = functools.partial(
            lax.dot_general,
            ones,
            dimension_numbers=NT,
            precision=lax.Precision.HIGHEST,
            preferred_element_type=jnp.float32,
        )
        row = lax.broadcasted_iota(jnp.int32, stat_ref.shape, 0)
        stat_ref[...] = jnp.where(row == 0, total(square_ref[...]), total(cross_ref[...]))


def value_kernel(nblocks, nslots, start_ref, stat_ref, o_ref, grad_ref, gain_ref, p_ref, *refs):
    normed_ref, d_ref, local_ref, export_ref = refs[:4]
    slots = refs[4 : 4 + nslots]
    inverse_ref, factor_ref, term_ref = refs[4 + nslots :]
    tokens = o_ref.shape[0]

    @pl.when(pl.program_id(0) == 0)
    def _():
        stats = jnp.sum(stat_ref[...], axis=0)
        squares = jnp.broadcast_to(stats[0:1], (HEAD_SIZE, tokens)).T
        cross = jnp.broadcast_to(stats[1:2], (HEAD_SIZE, tokens)).T
        inverse = lax.rsqrt(squares / FEAT + epsilon)
        inverse_ref[...] = inverse
        factor_ref[...] = inverse * inverse * inverse * cross / FEAT

    out = o_ref[...]
    inverse = inverse_ref[...]
    gain = gain_ref[...]
    scaled = grad_ref[...].astype(jnp.float32) * gain
    normed_ref[...] = (out * inverse * gain).astype(normed_ref.dtype)
    d_attended = (inverse * scaled - out * factor_ref[...]).astype(d_ref.dtype)
    d_ref[...] = d_attended
    for j in range(nslots):
        cols = slice(tokens + j * BLK, tokens + (j + 1) * BLK)
        slots[j][...] = dot(p_ref[0, :, cols], d_attended, TN).astype(slots[j].dtype)
    term_ref[...] = dot(p_ref[0, :, :tokens], d_attended, TN)
    local_ref[...] = term_ref[...].astype(local_ref.dtype)
    start = pl.multiple_of(start_ref[0], BLK)
    export_ref[...] = term_ref[pl.ds(start, BLK)]


def key_kernel(nblocks, nslots, start_ref, q_ref, k_ref, v_ref, o_ref, d_ref, p_ref, *refs):
    key_in = refs[:nslots]
    value_in = refs[nslots : 2 * nslots]
    dq_ref, local_ref, export_ref = refs[2 * nslots : 2 * nslots + 3]
    slots = refs[2 * nslots + 3 : 3 * nslots + 3]
    key_cat, value_cat, score_ref, term_ref = refs[3 * nslots + 3 :]
    tokens = q_ref.shape[0]
    key_cat[:tokens] = k_ref[...]
    value_cat[:tokens] = v_ref[...]
    for j in range(nslots):
        rows = slice(tokens + j * BLK, tokens + (j + 1) * BLK)
        key_cat[rows] = key_in[j][...]
        value_cat[rows] = value_in[j][...]
    for g in range(nblocks):
        rows = slice(g * BLK, (g + 1) * BLK)
        d_attended = d_ref[rows]
        delta = jnp.sum(d_attended.astype(jnp.float32) * o_ref[rows], axis=1, keepdims=True)
        dprob = dot(d_attended, value_cat[...], NT)
        dscore = p_ref[0, rows].astype(jnp.float32) * (dprob - delta)
        dscore = dscore.astype(jnp.bfloat16)
        score_ref[rows] = dscore
        dq_ref[rows] = (dot(dscore, key_cat[...], NN) * softmax_scale).astype(dq_ref.dtype)
    for j in range(nslots):
        cols = slice(tokens + j * BLK, tokens + (j + 1) * BLK)
        term = dot(score_ref[:, cols], q_ref[...], TN) * softmax_scale
        slots[j][...] = term.astype(slots[j].dtype)
    term_ref[...] = dot(score_ref[:, :tokens], q_ref[...], TN) * softmax_scale
    local_ref[...] = term_ref[...].astype(local_ref.dtype)
    start = pl.multiple_of(start_ref[0], BLK)
    export_ref[...] = term_ref[pl.ds(start, BLK)]


def column(rows):
    return pl.BlockSpec((rows, HEAD_SIZE), lambda h, *_: (0, h))


def shards(queries, keys, values, gain, grad_out, pattern):
    n_seq = lax.axis_size("seq")
    far = n_seq // 2
    myself = lax.axis_index("seq")
    tokens, width = queries.shape
    heads = width // HEAD_SIZE
    nblocks = tokens // BLK
    nslots = n_seq - 1
    span = tokens + nslots * BLK
    masked = nslots != REM

    def turn(x, k):
        pairs = [
            (a * 2 + b, (a + k) % far * 2 + b) for a in range(far) for b in range(2)
        ]
        return lax.ppermute(x, "seq", pairs)

    def swap(x):
        return lax.ppermute(x, "seq", [(i, i ^ 1) for i in range(n_seq)])

    owner = pattern // nblocks
    row_range = (jnp.arange(pattern.shape[0], dtype=jnp.int32) // nblocks)[:, None]
    mine = jnp.where((owner != row_range) & (owner == myself), pattern, -1)
    start = (jnp.max(mine) - myself * nblocks) * BLK
    key_export = lax.dynamic_slice_in_dim(keys, start, BLK, 0)
    value_export = lax.dynamic_slice_in_dim(values, start, BLK, 0)

    shifts = list(range(1, far))
    mates_k = [swap(key_export)]
    key_near = [turn(key_export, k) for k in shifts]
    value_export, key_near = lax.optimization_barrier((value_export, key_near))
    mates_v = [swap(value_export)]
    value_near = [turn(value_export, k) for k in shifts]
    mates_k += [swap(x) for x in key_near]
    mates_v += [swap(x) for x in value_near]
    key_slots = key_near + mates_k
    value_slots = value_near + mates_v

    a, b = myself // 2, myself % 2
    ranges = [(a - k) % far * 2 + b for k in shifts] + [
        (a - k) % far * 2 + 1 - b for k in range(far)
    ]
    my_rows = lax.dynamic_slice_in_dim(pattern, myself * nblocks, nblocks, 0)
    names = jnp.arange(nblocks, dtype=jnp.int32) + myself * nblocks
    listed = jnp.any(my_rows[:, :LOC, None] == names[None, None], axis=1)
    if masked:
        sources = jnp.stack(ranges)
        listed_far = jnp.any((my_rows[:, LOC:] // nblocks)[:, :, None] == sources, axis=1)
        listed = jnp.concatenate([listed, listed_far], axis=1)
    bias = jnp.where(listed, 0.0, LOW).astype(jnp.float32)

    flops = 2 * heads * tokens * span * HEAD_SIZE
    smem = pl.BlockSpec(memory_space=pltpu.SMEM)
    whole = column(tokens)
    block = column(BLK)
    prob_spec = pl.BlockSpec((1, tokens, span), lambda h, *_: (h, 0, 0))
    gain_spec = pl.BlockSpec((1, HEAD_SIZE), lambda h, *_: (0, h))
    params = pltpu.CompilerParams(vmem_limit_bytes=40 * 1024 * 1024)
    gain_row = gain.reshape(1, width)

    prob = pl.pallas_call(
        functools.partial(softmax_kernel, nblocks, masked),
        grid=(heads,),
        in_specs=[smem, whole, whole] + [block] * nslots,
        out_specs=prob_spec,
        out_shape=jax.ShapeDtypeStruct((heads, tokens, span), jnp.bfloat16),
        scratch_shapes=[pltpu.VMEM((span, HEAD_SIZE), jnp.bfloat16)],
        compiler_params=params,
        cost_estimate=pl.CostEstimate(
            flops=flops, bytes_accessed=16 * tokens * span, transcendentals=heads * tokens * span
        ),
        name="softmax",
    )(bias, queries, keys, *key_slots)

    attended, stats = pl.pallas_call(
        attend_kernel,
        grid=(heads,),
        in_specs=[prob_spec, whole, whole, gain_spec] + [block] * nslots,
        out_specs=[whole, pl.BlockSpec((8, tokens), lambda h: (0, 0))],
        out_shape=[
            jax.ShapeDtypeStruct((tokens, width), jnp.float32),
            jax.ShapeDtypeStruct((8, tokens), jnp.float32),
        ],
        scratch_shapes=[
            pltpu.VMEM((span, HEAD_SIZE), jnp.bfloat16),
            pltpu.VMEM((tokens, HEAD_SIZE), jnp.float32),
            pltpu.VMEM((tokens, HEAD_SIZE), jnp.float32),
        ],
        compiler_params=params,
        cost_estimate=pl.CostEstimate(
            flops=flops, bytes_accessed=16 * tokens * span, transcendentals=0
        ),
        name="attend",
    )(prob, values, grad_out, gain_row, *value_slots)

    stats = lax.all_gather(stats, "head")

    start_vec = start.reshape(1)
    local_shapes = [
        jax.ShapeDtypeStruct((tokens, width), jnp.bfloat16),
        jax.ShapeDtypeStruct((BLK, width), jnp.float32),
    ]
    slot_shapes = [jax.ShapeDtypeStruct((BLK, width), jnp.bfloat16)] * nslots
    normed, d_attended, value_local, value_mine, *value_terms = pl.pallas_call(
        functools.partial(value_kernel, nblocks, nslots),
        grid=(heads,),
        in_specs=[
            smem,
            pl.BlockSpec(stats.shape, lambda h: (0, 0, 0)),
            whole,
            whole,
            gain_spec,
            prob_spec,
        ],
        out_specs=[whole, whole, whole, block] + [block] * nslots,
        out_shape=[jax.ShapeDtypeStruct((tokens, width), jnp.bfloat16)] * 2
        + local_shapes
        + slot_shapes,
        scratch_shapes=[pltpu.VMEM((tokens, HEAD_SIZE), jnp.float32)] * 3,
        compiler_params=params,
        cost_estimate=pl.CostEstimate(
            flops=flops, bytes_accessed=16 * tokens * span, transcendentals=0
        ),
        name="value_terms",
    )(start_vec, stats, attended, grad_out, gain_row, prob)

    grad_queries, key_local, key_mine, *key_terms = pl.pallas_call(
        functools.partial(key_kernel, nblocks, nslots),
        grid=(heads,),
        in_specs=[smem, whole, whole, whole, whole, whole, prob_spec] + [block] * (2 * nslots),
        out_specs=[whole, whole, block] + [block] * nslots,
        out_shape=[jax.ShapeDtypeStruct((tokens, width), jnp.bfloat16)]
        + local_shapes
        + slot_shapes,
        scratch_shapes=[
            pltpu.VMEM((span, HEAD_SIZE), jnp.bfloat16),
            pltpu.VMEM((span, HEAD_SIZE), jnp.bfloat16),
            pltpu.VMEM((tokens, span), jnp.bfloat16),
            pltpu.VMEM((tokens, HEAD_SIZE), jnp.float32),
        ],
        compiler_params=params,
        cost_estimate=pl.CostEstimate(
            flops=3 * flops, bytes_accessed=16 * tokens * span, transcendentals=0
        ),
        name="key_terms",
    )(
        start_vec,
        queries,
        keys,
        values,
        attended,
        d_attended,
        prob,
        *key_slots,
        *value_slots,
    )

    def send_back(terms, own):
        near, mates = terms[: far - 1], terms[far - 1 :]
        total = own
        for k in shifts:
            crossed = swap(mates[k]).astype(jnp.float32) + near[k - 1].astype(jnp.float32)
            total = total + turn(crossed.astype(jnp.bfloat16), -k).astype(jnp.float32)
        return (total + swap(mates[0]).astype(jnp.float32)).astype(jnp.bfloat16)

    grad_values = lax.dynamic_update_slice_in_dim(
        value_local, send_back(value_terms, value_mine), start, 0
    )
    grad_keys = lax.dynamic_update_slice_in_dim(
        key_local, send_back(key_terms, key_mine), start, 0
    )
    return normed, grad_queries, grad_keys, grad_values


def solution(mesh):
    split = P("seq", "head")
    return jax.shard_map(
        shards,
        mesh=mesh,
        in_specs=(split, split, split, P("head"), split, P()),
        out_specs=(split, split, split, split),
        check_vma=False,
    )
```

time: 433 us -> 173 us (0.40); the launches traced: 425 us -> 172 us
  matrix products: 139 us -> 0 us
  local copies, waits for them, and re-layouts: 133 us -> 5.87 us
  blocking collectives: 61.1 us -> 5.25 us
  Pallas kernels: 0 us -> 50.5 us
  other arithmetic: 40.2 us -> 3.73 us
  starting transfers between devices: 14.8 us -> 45.6 us
  waiting for transfers between devices: 34.8 us -> 59.9 us
    dot_general x14 -> x0, matrix products: 139 us -> none  [the longest x1 25.8 us: backward_group(): jnp.einsum('bjs,bjkw->skw', selector, key_terms, precision=lax.Precision....]
    reshape x9 -> x0, local copies, waits for them, and re-layouts: 63.4 us -> none  [the longest x2 33.6 us: backward_group(): value_terms = value_terms.reshape(per_group, REM, BLK, width)]
    ppermute x0 -> x28, waiting for transfers between devices: none -> 59.9 us  [the longest x12 41.3 us: turn(): return lax.ppermute(x, 'seq', pairs)]
    all_to_all x1 -> x0, blocking collectives: 55.4 us -> none  [shards(): lax.all_to_all(key_send, 'seq', split_axis=0, concat_axis=0, tiled=True)]
    pallas_call x0 -> x4, Pallas kernels: none -> 50.5 us  [the longest x1 17.6 us: shards(): pl.pallas_call(functools.partial(key_kernel, nblocks, nslots), grid=(head...]
    ppermute x0 -> x28, starting transfers between devices: none -> 45.6 us  [the longest x12 29.4 us: turn(): return lax.ppermute(x, 'seq', pairs)]
    all_to_all x3 -> x0, waiting for transfers between devices: 34.8 us -> none  [the longest x1 21 us: shards(): lax.all_to_all(value_send, 'seq', split_axis=0, concat_axis=0, tiled=True)]
    unnamed x37 -> x14, local copies, waits for them, and re-layouts: 26.1 us -> 2.47 us
  transfers between devices with their start and end apart: 3 -> 28, of which waited for: 2 -> 11; matrix products, arithmetic and copies ran while one was open for 33% -> 2% of each run, Pallas kernels for 0% -> 17%
where the time goes in v1:
time: 173 us; the launch traced here: 172 us
  waiting for transfers between devices  59.9 us (35%)
  Pallas kernels  50.5 us (29%)
  starting transfers between devices  45.6 us (26%)
  local copies, waits for them, and re-layouts  5.87 us (3%)
  blocking collectives  5.25 us (3%)
  other arithmetic  3.73 us (2%)
    ppermute x12, waiting for transfers between devices, turn(): return lax.ppermute(x, 'seq', pairs)  41.3 us
    ppermute x12, starting transfers between devices, turn(): return lax.ppermute(x, 'seq', pairs)  29.4 us
    ppermute x16, waiting for transfers between devices, swap(): return lax.ppermute(x, 'seq', [(i, i ^ 1) for i in range(n_seq)])  18.5 us
    pallas_call x1, Pallas kernels, shards(): pl.pallas_call(functools.partial(key_kernel, nblocks, nslots), grid=(head...  17.6 us
    ppermute x16, starting transfers between devices, swap(): return lax.ppermute(x, 'seq', [(i, i ^ 1) for i in range(n_seq)])  16.3 us
    pallas_call x1, Pallas kernels, shards(): pl.pallas_call(functools.partial(softmax_kernel, nblocks, masked), grid=(...  12.2 us
    pallas_call x1, Pallas kernels, shards(): pl.pallas_call(functools.partial(value_kernel, nblocks, nslots), grid=(he...  10.6 us
    pallas_call x1, Pallas kernels, shards(): pl.pallas_call(attend_kernel, grid=(heads,), in_specs=[prob_spec, whole,...  10 us
  transfers between devices with their start and end apart: 28, of which 11 were waited for; matrix products, arithmetic and copies ran while one was open for 2% of the time, Pallas kernels for 17%

profile of v1, /device:TPU:0, one launch (start us, length us, event | category | flops | bytes accessed | tf_op | source)
XLA Modules:
  0.0 172.3 jit_solution(11722467276708397869)
XLA Ops:
  3.7 3.1 %collective-permute-start = (bf16[128,1024]{1,0:T(8,128)(2,1)S(1)}, bf16[128,1024]{1,0:T(8,128)(2,1)S(1)}, u32[]{:S(2)}, u32[]{:S(2)}) collective-permute-start(bf16[128,1024]{1,0:T(8,128)(2,1)S(1)} %constant_dynamic-slice_fusion), channel_id=1, source_target_pairs={{0,8},{4,12},{8,16},{12,20},{16,24},{20,28},{24,0},{28,4},{1,9},{5... | collective-permute-start | bytes 786440 | tf_op jit(solution)/shard_map/ppermute | solution.py:168
  6.8 2.6 %collective-permute-start.1 = (bf16[128,1024]{1,0:T(8,128)(2,1)S(1)}, bf16[128,1024]{1,0:T(8,128)(2,1)S(1)}, u32[]{:S(2)}, u32[]{:S(2)}) collective-permute-start(bf16[128,1024]{1,0:T(8,128)(2,1)S(1)} %constant_dynamic-slice_fusion), channel_id=1, source_target_pairs={{0,16},{4,20},{8,24},{12,28},{16,0},{20,4},{24,8},{28,12},{1,17},{... | collective-permute-start | bytes 786440 | tf_op jit(solution)/shard_map/ppermute | solution.py:168
  12.3 1.7 constant_dynamic-slice_fusion.1
  13.9 2.2 %collective-permute-done.refs_0_ = bf16[128,1024]{1,0:T(8,128)(2,1)S(1)} collective-permute-done((bf16[128,1024]{1,0:T(8,128)(2,1)S(1)}, bf16[128,1024]{1,0:T(8,128)(2,1)S(1)}, u32[]{:S(2)}, u32[]{:S(2)}) %collective-permute-start) | collective-permute-done | bytes 262176 | tf_op jit(solution)/shard_map/ppermute | solution.py:168
  16.1 10.4 %collective-permute-done.1.refs_1_ = bf16[128,1024]{1,0:T(8,128)(2,1)S(1)} collective-permute-done((bf16[128,1024]{1,0:T(8,128)(2,1)S(1)}, bf16[128,1024]{1,0:T(8,128)(2,1)S(1)}, u32[]{:S(2)}, u32[]{:S(2)}) %collective-permute-start.1) | collective-permute-done | bytes 262176 | tf_op jit(solution)/shard_map/ppermute | solution.py:168
  28.0 6.1 %collective-permute-start.7 = (bf16[128,1024]{1,0:T(8,128)(2,1)}, bf16[128,1024]{1,0:T(8,128)(2,1)S(1)}, u32[]{:S(2)}, u32[]{:S(2)}) collective-permute-start(bf16[128,1024]{1,0:T(8,128)(2,1)} %constant_dynamic-slice_fusion.1), channel_id=1, source_target_pairs={{0,8},{4,12},{8,16},{12,20},{16,24},{20,28},{24,0},{28,4},{1,9},{5... | collective-permute-start | bytes 786440 | tf_op jit(solution)/shard_map/ppermute | solution.py:168
  34.1 1.6 collective-permute-start.8
  39.4 6.4 %collective-permute-done.5.refs_5_ = bf16[128,1024]{1,0:T(8,128)(2,1)S(1)} collective-permute-done((bf16[128,1024]{1,0:T(8,128)(2,1)S(1)}, bf16[128,1024]{1,0:T(8,128)(2,1)S(1)}, u32[]{:S(2)}, u32[]{:S(2)}) %collective-permute-start.5) | collective-permute-done | bytes 262176 | tf_op jit(solution)/shard_map/ppermute | solution.py:171
  47.8 4.1 %collective-permute-done.8.refs_1_.refs_8_ = bf16[128,1024]{1,0:T(8,128)(2,1)S(1)} collective-permute-done((bf16[128,1024]{1,0:T(8,128)(2,1)}, bf16[128,1024]{1,0:T(8,128)(2,1)S(1)}, u32[]{:S(2)}, u32[]{:S(2)}) %collective-permute-start.8) | collective-permute-done | bytes 262176 | tf_op jit(solution)/shard_map/ppermute | solution.py:168
  56.4 12.2 %softmax.1.p_ref = bf16[8,512,1408]{2,1,0:T(8,128)(2,1)} custom-call(f32[4,4]{1,0:T(4,128)S(1)} %broadcast_select_fusion.bias_ref, bf16[512,1024]{1,0:T(8,128)(2,1)S(1)} %copy-done.4, bf16[512,1024]{1,0:T(8,128)(2,1)S(1)} %copy-done, bf16[128,1024]{1,0:T(8,128)(2,1)S(1)} %collective-permute-done.refs_0_, ...), custom_call_target="tpu_custom_call" | custom-call | flops 1476395008 | bytes 11534336 | tf_op jit(solution)/shard_map/softmax/pallas_call | solution.py:213
  68.6 3.3 %collective-permute-done.13.refs_6_.refs_13_ = bf16[128,1024]{1,0:T(8,128)(2,1)S(1)} collective-permute-done((bf16[128,1024]{1,0:T(8,128)(2,1)S(1)}, bf16[128,1024]{1,0:T(8,128)(2,1)S(1)}, u32[]{:S(2)}, u32[]{:S(2)}) %collective-permute-start.13) | collective-permute-done | bytes 262176 | tf_op jit(solution)/shard_map/ppermute | solution.py:171
  72.0 10.0 %attend.1 = (f32[512,1024]{1,0:T(8,128)S(1)}, f32[8,512]{1,0:T(8,128)S(1)}) custom-call(bf16[8,512,1408]{2,1,0:T(8,128)(2,1)} %softmax.1.p_ref, bf16[512,1024]{1,0:T(8,128)(2,1)S(1)} %copy-done.2, bf16[512,1024]{1,0:T(8,128)(2,1)S(1)} %copy-done.3, f32[1,1024]{1,0:T(1,128)S(1)} %bitcast.4, bf16[128,1024]{1,0:T(8,128)(2,1)S(1)} %collective-permute-done.7.refs_0_.refs_7_, ...), custom_call_target="tpu_custom_call" | custom-call | flops 1476395008 | bytes 11534336 | tf_op jit(solution)/shard_map/attend/pallas_call | solution.py:227
  82.0 5.2 %all-gather = f32[32,512]{1,0:T(8,128)S(1)} all-gather(f32[8,512]{1,0:T(8,128)S(1)} %get-tuple-element.35), channel_id=2, replica_groups=mesh['seq'=8,'head'=4] {'head'}, dimensions={0}, use_global_device_ids=true | all-gather | bytes 81920 | tf_op jit(solution)/shard_map/all_gather | solution.py:248
  87.3 10.6 %value_terms.1 = (bf16[512,1024]{1,0:T(8,128)(2,1)}, bf16[512,1024]{1,0:T(8,128)(2,1)S(1)}, bf16[512,1024]{1,0:T(8,128)(2,1)}, f32[128,1024]{1,0:T(8,128)S(1)}, ...) custom-call(s32[1]{0:T(128)} %bitcast.start_ref, ...), custom_call_target="tpu_custom_call" | custom-call | flops 1476395008 | bytes 11534336 | tf_op jit(solution)/shard_map/value_terms/pallas_call | solution.py:256
  101.9 17.6 %key_terms.1 = (bf16[512,1024]{1,0:T(8,128)(2,1)}, bf16[512,1024]{1,0:T(8,128)(2,1)}, f32[128,1024]{1,0:T(8,128)S(1)}, bf16[128,1024]{1,0:T(8,128)(2,1)S(1)}, bf...) custom-call(s32[1]{0:T(128)} %bitcast.start_ref, ...), custom_call_target="tpu_custom_call" | custom-call | flops 4429185024 | bytes 11534336 | tf_op jit(solution)/shard_map/key_terms/pallas_call | solution.py:279
  122.3 4.7 %collective-permute-start.22 = (bf16[128,1024]{1,0:T(8,128)(2,1)S(1)}, bf16[128,1024]{1,0:T(8,128)(2,1)S(1)}, u32[]{:S(2)}, u32[]{:S(2)}) collective-permute-start(bf16[128,1024]{1,0:T(8,128)(2,1)S(1)} %add_convert_fusion.3), channel_id=1, source_target_pairs={{0,24},{4,28},{8,0},{12,4},{16,8},{20,12},{24,16},{28,20},{1,25},{... | collective-permute-start | bytes 786440 | tf_op jit(solution)/shard_map/ppermute | solution.py:168
  127.1 2.4 %collective-permute-done.14 = bf16[128,1024]{1,0:T(8,128)(2,1)S(1)} collective-permute-done((bf16[128,1024]{1,0:T(8,128)(2,1)S(1)}, bf16[128,1024]{1,0:T(8,128)(2,1)S(1)}, u32[]{:S(2)}, u32[]{:S(2)}) %collective-permute-start.14) | collective-permute-done | bytes 262176 | tf_op jit(solution)/shard_map/ppermute | solution.py:171
  129.5 1.6 collective-permute-start.24
  131.1 4.0 %collective-permute-done.16 = bf16[128,1024]{1,0:T(8,128)(2,1)S(1)} collective-permute-done((bf16[128,1024]{1,0:T(8,128)(2,1)S(1)}, bf16[128,1024]{1,0:T(8,128)(2,1)S(1)}, u32[]{:S(2)}, u32[]{:S(2)}) %collective-permute-start.16) | collective-permute-done | bytes 262176 | tf_op jit(solution)/shard_map/ppermute | solution.py:171
  135.1 2.6 %collective-permute-start.26 = (bf16[128,1024]{1,0:T(8,128)(2,1)S(1)}, bf16[128,1024]{1,0:T(8,128)(2,1)S(1)}, u32[]{:S(2)}, u32[]{:S(2)}) collective-permute-start(bf16[128,1024]{1,0:T(8,128)(2,1)S(1)} %add_convert_fusion.1), channel_id=1, source_target_pairs={{0,8},{4,12},{8,16},{12,20},{16,24},{20,28},{24,0},{28,4},{1,9},{5... | collective-permute-start | bytes 786440 | tf_op jit(solution)/shard_map/ppermute | solution.py:168
  137.7 2.4 %collective-permute-done.18 = bf16[128,1024]{1,0:T(8,128)(2,1)S(1)} collective-permute-done((bf16[128,1024]{1,0:T(8,128)(2,1)S(1)}, bf16[128,1024]{1,0:T(8,128)(2,1)S(1)}, u32[]{:S(2)}, u32[]{:S(2)}) %collective-permute-start.18) | collective-permute-done | bytes 262176 | tf_op jit(solution)/shard_map/ppermute | solution.py:171
  140.7 4.7 %collective-permute-start.15 = (bf16[128,1024]{1,0:T(8,128)(2,1)S(1)}, bf16[128,1024]{1,0:T(8,128)(2,1)S(1)}, u32[]{:S(2)}, u32[]{:S(2)}) collective-permute-start(bf16[128,1024]{1,0:T(8,128)(2,1)S(1)} %add_convert_fusion.7), channel_id=1, source_target_pairs={{0,24},{4,28},{8,0},{12,4},{16,8},{20,12},{24,16},{28,20},{1,25},{... | collective-permute-start | bytes 786440 | tf_op jit(solution)/shard_map/ppermute | solution.py:168
  145.8 6.4 %collective-permute-done.24 = bf16[128,1024]{1,0:T(8,128)(2,1)S(1)} collective-permute-done((bf16[128,1024]{1,0:T(8,128)(2,1)S(1)}, bf16[128,1024]{1,0:T(8,128)(2,1)S(1)}, u32[]{:S(2)}, u32[]{:S(2)}) %collective-permute-start.24) | collective-permute-done | bytes 262176 | tf_op jit(solution)/shard_map/ppermute | solution.py:168
  154.5 16.9 %collective-permute-done.17 = bf16[128,1024]{1,0:T(8,128)(2,1)S(1)} collective-permute-done((bf16[128,1024]{1,0:T(8,128)(2,1)S(1)}, bf16[128,1024]{1,0:T(8,128)(2,1)S(1)}, u32[]{:S(2)}, u32[]{:S(2)}) %collective-permute-start.17) | collective-permute-done | bytes 262176 | tf_op jit(solution)/shard_map/ppermute | solution.py:168
  (67 shorter events, 28.2 us)
Async XLA Ops:
  6.8 19.7 %collective-permute-start.1 = (bf16[128,1024]{1,0:T(8,128)(2,1)S(1)}, bf16[128,1024]{1,0:T(8,128)(2,1)S(1)}, u32[]{:S(2)}, u32[]{:S(2)}) collective-permute-start(bf16[128,1024]{1,0:T(8,128)(2,1)S(1)} %constant_dynamic-slice_fusion), channel_id=1, source_target_pairs={{0,16},{4,20},{8,24},{12,28},{16,0},{20,4},{24,8},{28,12},{1,17},{... | collective-permute-start | bytes 786440 | tf_op jit(solution)/shard_map/ppermute | solution.py:168
  9.4 17.1 %collective-permute-start.2 = (bf16[128,1024]{1,0:T(8,128)(2,1)S(1)}, bf16[128,1024]{1,0:T(8,128)(2,1)S(1)}, u32[]{:S(2)}, u32[]{:S(2)}) collective-permute-start(bf16[128,1024]{1,0:T(8,128)(2,1)S(1)} %constant_dynamic-slice_fusion), channel_id=1, source_target_pairs={{0,24},{4,28},{8,0},{12,4},{16,8},{20,12},{24,16},{28,20},{1,25},{... | collective-permute-start | bytes 786440 | tf_op jit(solution)/shard_map/ppermute | solution.py:168
  10.7 25.7 %collective-permute-start.3 = (bf16[128,1024]{1,0:T(8,128)(2,1)S(1)}, bf16[128,1024]{1,0:T(8,128)(2,1)S(1)}, u32[]{:S(2)}, u32[]{:S(2)}) collective-permute-start(bf16[128,1024]{1,0:T(8,128)(2,1)S(1)} %constant_dynamic-slice_fusion), channel_id=1, source_target_pairs={{0,4},{4,0},{8,12},{12,8},{16,20},{20,16},{24,28},{28,24},{1,5},{5... | collective-permute-start | bytes 786440 | tf_op jit(solution)/shard_map/ppermute | solution.py:171
  28.0 18.2 %collective-permute-start.7 = (bf16[128,1024]{1,0:T(8,128)(2,1)}, bf16[128,1024]{1,0:T(8,128)(2,1)S(1)}, u32[]{:S(2)}, u32[]{:S(2)}) collective-permute-start(bf16[128,1024]{1,0:T(8,128)(2,1)} %constant_dynamic-slice_fusion.1), channel_id=1, source_target_pairs={{0,8},{4,12},{8,16},{12,20},{16,24},{20,28},{24,0},{28,4},{1,9},{5... | collective-permute-start | bytes 786440 | tf_op jit(solution)/shard_map/ppermute | solution.py:168
  34.1 17.8 %collective-permute-start.8 = (bf16[128,1024]{1,0:T(8,128)(2,1)}, bf16[128,1024]{1,0:T(8,128)(2,1)S(1)}, u32[]{:S(2)}, u32[]{:S(2)}) collective-permute-start(bf16[128,1024]{1,0:T(8,128)(2,1)} %constant_dynamic-slice_fusion.1), channel_id=1, source_target_pairs={{0,16},{4,20},{8,24},{12,28},{16,0},{20,4},{24,8},{28,12},{1,17},{... | collective-permute-start | bytes 786440 | tf_op jit(solution)/shard_map/ppermute | solution.py:168
  35.7 16.7 %collective-permute-start.9 = (bf16[128,1024]{1,0:T(8,128)(2,1)}, bf16[128,1024]{1,0:T(8,128)(2,1)S(1)}, u32[]{:S(2)}, u32[]{:S(2)}) collective-permute-start(bf16[128,1024]{1,0:T(8,128)(2,1)} %constant_dynamic-slice_fusion.1), channel_id=1, source_target_pairs={{0,24},{4,28},{8,0},{12,4},{16,8},{20,12},{24,16},{28,20},{1,25},{... | collective-permute-start | bytes 786440 | tf_op jit(solution)/shard_map/ppermute | solution.py:168
  37.8 16.2 %collective-permute-start.6 = (bf16[128,1024]{1,0:T(8,128)(2,1)S(1)}, bf16[128,1024]{1,0:T(8,128)(2,1)S(1)}, u32[]{:S(2)}, u32[]{:S(2)}) collective-permute-start(bf16[128,1024]{1,0:T(8,128)(2,1)S(1)} %collective-permute-done.2.refs_2_), channel_id=1, source_target_pairs={{0,4},{4,0},{8,12},{12,8},{16,20},{20,16},{24,28},{28,24},{1,5},{5... | collective-permute-start | bytes 786440 | tf_op jit(solution)/shard_map/ppermute | solution.py:171
  45.7 22.9 %collective-permute-start.10 = (bf16[128,1024]{1,0:T(8,128)(2,1)}, bf16[128,1024]{1,0:T(8,128)(2,1)S(1)}, u32[]{:S(2)}, u32[]{:S(2)}) collective-permute-start(bf16[128,1024]{1,0:T(8,128)(2,1)} %constant_dynamic-slice_fusion.1), channel_id=1, source_target_pairs={{0,4},{4,0},{8,12},{12,8},{16,20},{20,16},{24,28},{28,24},{1,5},{5... | collective-permute-start | bytes 786440 | tf_op jit(solution)/shard_map/ppermute | solution.py:171
  46.2 22.4 %collective-permute-start.11 = (bf16[128,1024]{1,0:T(8,128)(2,1)S(1)}, bf16[128,1024]{1,0:T(8,128)(2,1)S(1)}, u32[]{:S(2)}, u32[]{:S(2)}) collective-permute-start(bf16[128,1024]{1,0:T(8,128)(2,1)S(1)} %collective-permute-done.7.refs_0_.refs_7_), channel_id=1, source_target_pairs={{0,4},{4,0},{8,12},{12,8},{16,20},{20,16},{24,28},{28,24},{1,5},{5... | collective-permute-start | bytes 786440 | tf_op jit(solution)/shard_map/ppermute | solution.py:171
  51.9 16.7 %collective-permute-start.12 = (bf16[128,1024]{1,0:T(8,128)(2,1)S(1)}, bf16[128,1024]{1,0:T(8,128)(2,1)S(1)}, u32[]{:S(2)}, u32[]{:S(2)}) collective-permute-start(bf16[128,1024]{1,0:T(8,128)(2,1)S(1)} %collective-permute-done.8.refs_1_.refs_8_), channel_id=1, source_target_pairs={{0,4},{4,0},{8,12},{12,8},{16,20},{20,16},{24,28},{28,24},{1,5},{5... | collective-permute-start | bytes 786440 | tf_op jit(solution)/shard_map/ppermute | solution.py:171
  52.4 19.6 %collective-permute-start.13 = (bf16[128,1024]{1,0:T(8,128)(2,1)S(1)}, bf16[128,1024]{1,0:T(8,128)(2,1)S(1)}, u32[]{:S(2)}, u32[]{:S(2)}) collective-permute-start(bf16[128,1024]{1,0:T(8,128)(2,1)S(1)} %collective-permute-done.9.refs_2_.refs_9_), channel_id=1, source_target_pairs={{0,4},{4,0},{8,12},{12,8},{16,20},{20,16},{24,28},{28,24},{1,5},{5... | collective-permute-start | bytes 786440 | tf_op jit(solution)/shard_map/ppermute | solution.py:171
  97.9 22.2 %collective-permute-start.21 = (bf16[128,1024]{1,0:T(8,128)(2,1)S(1)}, bf16[128,1024]{1,0:T(8,128)(2,1)S(1)}, u32[]{:S(2)}, u32[]{:S(2)}) collective-permute-start(bf16[128,1024]{1,0:T(8,128)(2,1)S(1)} %get-tuple-element.51), channel_id=1, source_target_pairs={{0,4},{4,0},{8,12},{12,8},{16,20},{20,16},{24,28},{28,24},{1,5},{5... | collective-permute-start | bytes 786440 | tf_op jit(solution)/shard_map/ppermute | solution.py:171
  98.4 23.3 %collective-permute-start.23 = (bf16[128,1024]{1,0:T(8,128)(2,1)S(1)}, bf16[128,1024]{1,0:T(8,128)(2,1)S(1)}, u32[]{:S(2)}, u32[]{:S(2)}) collective-permute-start(bf16[128,1024]{1,0:T(8,128)(2,1)S(1)} %get-tuple-element.53), channel_id=1, source_target_pairs={{0,4},{4,0},{8,12},{12,8},{16,20},{20,16},{24,28},{28,24},{1,5},{5... | collective-permute-start | bytes 786440 | tf_op jit(solution)/shard_map/ppermute | solution.py:171
  99.9 22.4 %collective-permute-start.25 = (bf16[128,1024]{1,0:T(8,128)(2,1)S(1)}, bf16[128,1024]{1,0:T(8,128)(2,1)S(1)}, u32[]{:S(2)}, u32[]{:S(2)}) collective-permute-start(bf16[128,1024]{1,0:T(8,128)(2,1)S(1)} %get-tuple-element.55), channel_id=1, source_target_pairs={{0,4},{4,0},{8,12},{12,8},{16,20},{20,16},{24,28},{28,24},{1,5},{5... | collective-permute-start | bytes 786440 | tf_op jit(solution)/shard_map/ppermute | solution.py:171
  100.4 40.3 %collective-permute-start.27 = (bf16[128,1024]{1,0:T(8,128)(2,1)S(1)}, bf16[128,1024]{1,0:T(8,128)(2,1)S(1)}, u32[]{:S(2)}, u32[]{:S(2)}) collective-permute-start(bf16[128,1024]{1,0:T(8,128)(2,1)S(1)} %get-tuple-element.57), channel_id=1, source_target_pairs={{0,4},{4,0},{8,12},{12,8},{16,20},{20,16},{24,28},{28,24},{1,5},{5... | collective-permute-start | bytes 786440 | tf_op jit(solution)/shard_map/ppermute | solution.py:171
  120.1 15.0 %collective-permute-start.16 = (bf16[128,1024]{1,0:T(8,128)(2,1)S(1)}, bf16[128,1024]{1,0:T(8,128)(2,1)S(1)}, u32[]{:S(2)}, u32[]{:S(2)}) collective-permute-start(bf16[128,1024]{1,0:T(8,128)(2,1)S(1)} %get-tuple-element.44), channel_id=1, source_target_pairs={{0,4},{4,0},{8,12},{12,8},{16,20},{20,16},{24,28},{28,24},{1,5},{5... | collective-permute-start | bytes 786440 | tf_op jit(solution)/shard_map/ppermute | solution.py:171
  121.7 18.5 %collective-permute-start.18 = (bf16[128,1024]{1,0:T(8,128)(2,1)S(1)}, bf16[128,1024]{1,0:T(8,128)(2,1)S(1)}, u32[]{:S(2)}, u32[]{:S(2)}) collective-permute-start(bf16[128,1024]{1,0:T(8,128)(2,1)S(1)} %get-tuple-element.46), channel_id=1, source_target_pairs={{0,4},{4,0},{8,12},{12,8},{16,20},{20,16},{24,28},{28,24},{1,5},{5... | collective-permute-start | bytes 786440 | tf_op jit(solution)/shard_map/ppermute | solution.py:171
  122.3 23.0 %collective-permute-start.22 = (bf16[128,1024]{1,0:T(8,128)(2,1)S(1)}, bf16[128,1024]{1,0:T(8,128)(2,1)S(1)}, u32[]{:S(2)}, u32[]{:S(2)}) collective-permute-start(bf16[128,1024]{1,0:T(8,128)(2,1)S(1)} %add_convert_fusion.3), channel_id=1, source_target_pairs={{0,24},{4,28},{8,0},{12,4},{16,8},{20,12},{24,16},{28,20},{1,25},{... | collective-permute-start | bytes 786440 | tf_op jit(solution)/shard_map/ppermute | solution.py:168
  129.5 22.7 %collective-permute-start.24 = (bf16[128,1024]{1,0:T(8,128)(2,1)S(1)}, bf16[128,1024]{1,0:T(8,128)(2,1)S(1)}, u32[]{:S(2)}, u32[]{:S(2)}) collective-permute-start(bf16[128,1024]{1,0:T(8,128)(2,1)S(1)} %add_convert_fusion.2), channel_id=1, source_target_pairs={{0,16},{4,20},{8,24},{12,28},{16,0},{20,4},{24,8},{28,12},{1,17},{... | collective-permute-start | bytes 786440 | tf_op jit(solution)/shard_map/ppermute | solution.py:168
  135.1 17.1 %collective-permute-start.26 = (bf16[128,1024]{1,0:T(8,128)(2,1)S(1)}, bf16[128,1024]{1,0:T(8,128)(2,1)S(1)}, u32[]{:S(2)}, u32[]{:S(2)}) collective-permute-start(bf16[128,1024]{1,0:T(8,128)(2,1)S(1)} %add_convert_fusion.1), channel_id=1, source_target_pairs={{0,8},{4,12},{8,16},{12,20},{16,24},{20,28},{24,0},{28,4},{1,9},{5... | collective-permute-start | bytes 786440 | tf_op jit(solution)/shard_map/ppermute | solution.py:168
  140.1 13.0 %collective-permute-start.20 = (bf16[128,1024]{1,0:T(8,128)(2,1)S(1)}, bf16[128,1024]{1,0:T(8,128)(2,1)S(1)}, u32[]{:S(2)}, u32[]{:S(2)}) collective-permute-start(bf16[128,1024]{1,0:T(8,128)(2,1)S(1)} %get-tuple-element.48), channel_id=1, source_target_pairs={{0,4},{4,0},{8,12},{12,8},{16,20},{20,16},{24,28},{28,24},{1,5},{5... | collective-permute-start | bytes 786440 | tf_op jit(solution)/shard_map/ppermute | solution.py:171
  140.7 13.7 %collective-permute-start.15 = (bf16[128,1024]{1,0:T(8,128)(2,1)S(1)}, bf16[128,1024]{1,0:T(8,128)(2,1)S(1)}, u32[]{:S(2)}, u32[]{:S(2)}) collective-permute-start(bf16[128,1024]{1,0:T(8,128)(2,1)S(1)} %add_convert_fusion.7), channel_id=1, source_target_pairs={{0,24},{4,28},{8,0},{12,4},{16,8},{20,12},{24,16},{28,20},{1,25},{... | collective-permute-start | bytes 786440 | tf_op jit(solution)/shard_map/ppermute | solution.py:168
  145.4 26.0 %collective-permute-start.17 = (bf16[128,1024]{1,0:T(8,128)(2,1)S(1)}, bf16[128,1024]{1,0:T(8,128)(2,1)S(1)}, u32[]{:S(2)}, u32[]{:S(2)}) collective-permute-start(bf16[128,1024]{1,0:T(8,128)(2,1)S(1)} %add_convert_fusion.6), channel_id=1, source_target_pairs={{0,16},{4,20},{8,24},{12,28},{16,0},{20,4},{24,8},{28,12},{1,17},{... | collective-permute-start | bytes 786440 | tf_op jit(solution)/shard_map/ppermute | solution.py:168
  152.2 19.2 %collective-permute-start.19 = (bf16[128,1024]{1,0:T(8,128)(2,1)S(1)}, bf16[128,1024]{1,0:T(8,128)(2,1)S(1)}, u32[]{:S(2)}, u32[]{:S(2)}) collective-permute-start(bf16[128,1024]{1,0:T(8,128)(2,1)S(1)} %add_convert_fusion.5), channel_id=1, source_target_pairs={{0,8},{4,12},{8,16},{12,20},{16,24},{20,28},{24,0},{28,4},{1,9},{5... | collective-permute-start | bytes 786440 | tf_op jit(solution)/shard_map/ppermute | solution.py:168
  (11 other events, 263.4 us)

commit v2 on v0

v2 whole, which is shorter than its diff:
```python
import functools

import jax
import jax.numpy as jnp
from jax import lax
from jax.experimental import pallas as pl
from jax.experimental.pallas import tpu as pltpu
from jax.sharding import PartitionSpec as P

HEAD_SIZE = 128
BLK = 128
LOC = 3
REM = 7
FEAT = 4096
LOW = -1e30

epsilon = 1e-06
softmax_scale = 1.0 / HEAD_SIZE**0.5

NT = (((1,), (1,)), ((), ()))
NN = (((1,), (0,)), ((), ()))
TN = (((0,), (0,)), ((), ()))


def dot(a, b, dims):
    return lax.dot_general(a, b, dims, preferred_element_type=jnp.float32)


def head_columns(h):
    return pl.ds(pl.multiple_of(h * HEAD_SIZE, HEAD_SIZE), HEAD_SIZE)


def pick_kernel(nblocks, me_ref, pattern_ref, key_ref, value_ref, key_out, value_out, both_out, start_ref):
    pattern = pattern_ref[...]
    low = me_ref[0] * nblocks
    row = lax.broadcasted_iota(jnp.int32, pattern.shape, 0)
    inside = (pattern >= low) & (pattern < low + nblocks)
    others = (row < low) | (row >= low + nblocks)
    offset = jnp.where(inside & others, pattern - low, 0).astype(jnp.float32)
    start = pl.multiple_of(jnp.max(offset).astype(jnp.int32) * BLK, BLK)
    start_ref[0] = start
    key_out[...] = key_ref[pl.ds(start, BLK)]
    value_out[...] = value_ref[pl.ds(start, BLK)]
    both_out[:BLK] = key_ref[pl.ds(start, BLK)]
    both_out[BLK:] = value_ref[pl.ds(start, BLK)]


def gather_rows(cat_ref, pieces, cols):
    at = 0
    for piece in pieces:
        rows = piece.shape[0]
        cat_ref[at : at + rows] = piece[:, cols]
        at += rows


def softmax_kernel(nblocks, split, ranges_ref, pattern_ref, q_ref, *refs):
    pieces = refs[:-3]
    pa_ref, pb_ref, cat_ref = refs[-3:]
    low = ranges_ref[0] * nblocks
    imported = cat_ref.shape[0] // BLK - nblocks

    def bias(g, j):
        listed = None
        if j < nblocks:
            for i in range(LOC):
                same = pattern_ref[low + g, i] == low + j
                listed = same if listed is None else listed | same
        elif imported != REM:
            for i in range(LOC, LOC + REM):
                same = pattern_ref[low + g, i] // nblocks == ranges_ref[1 + j - nblocks]
                listed = same if listed is None else listed | same
        return None if listed is None else jnp.where(listed, 0.0, LOW)

    biases = [[bias(g, j) for j in range(nblocks + imported)] for g in range(nblocks)]

    @pl.loop(0, pa_ref.shape[0])
    def _(h):
        cols = head_columns(h)
        gather_rows(cat_ref, pieces, cols)
        for g in range(nblocks):
            rows = slice(g * BLK, (g + 1) * BLK)
            scores = dot(q_ref[rows, cols], cat_ref[...], NT) * softmax_scale
            parts = []
            for j in range(nblocks + imported):
                part = scores[:, j * BLK : (j + 1) * BLK]
                if biases[g][j] is not None:
                    part = part + biases[g][j]
                parts.append(part)
            scores = jnp.concatenate(parts, axis=1)
            peak = jnp.max(scores, axis=1, keepdims=True)
            expo = jnp.exp(scores - peak)
            total = jnp.sum(expo, axis=1, keepdims=True)
            prob = (expo * (1.0 / total)).astype(pa_ref.dtype)
            pa_ref[h, rows] = prob[:, :split]
            pb_ref[h, rows] = prob[:, split:]


def attend_kernel(p_ref, *refs):
    pieces = refs[:-2]
    o_ref, cat_ref = refs[-2:]

    @pl.loop(0, p_ref.shape[0])
    def _(h):
        cols = head_columns(h)
        gather_rows(cat_ref, pieces, cols)
        o_ref[:, cols] = dot(p_ref[h], cat_ref[...], NN)


def attend_rest_kernel(p_ref, o_in, grad_ref, gain_ref, *refs):
    pieces = refs[:-5]
    o_ref, stat_ref, cat_ref, square_ref, cross_ref = refs[-5:]
    square_ref[...] = jnp.zeros_like(square_ref)
    cross_ref[...] = jnp.zeros_like(cross_ref)

    @pl.loop(0, p_ref.shape[0])
    def _(h):
        cols = head_columns(h)
        gather_rows(cat_ref, pieces, cols)
        out = o_in[:, cols] + dot(p_ref[h], cat_ref[...], NN)
        o_ref[:, cols] = out
        scaled = grad_ref[:, cols].astype(jnp.float32) * gain_ref[:, cols]
        square_ref[...] += out * out
        cross_ref[...] += scaled * out

    stat_ref[0:1] = jnp.sum(square_ref[...].T, axis=0, keepdims=True)
    stat_ref[1:2] = jnp.sum(cross_ref[...].T, axis=0, keepdims=True)
    stat_ref[2:] = jnp.zeros_like(stat_ref[2:])


def put_terms(scores, right, slots, first, cols, scale):
    for j, slot in enumerate(slots):
        part = slice(first + j * BLK, first + (j + 1) * BLK)
        slot[:, cols] = (dot(scores[:, part], right, TN) * scale).astype(slot.dtype)


def put_local(term, term_ref, local_ref, export_ref, start_ref, cols):
    term_ref[...] = term
    local_ref[:, cols] = term.astype(local_ref.dtype)
    start = pl.multiple_of(start_ref[0], BLK)
    export_ref[:, cols] = term_ref[pl.ds(start, BLK)]


def grad_out_kernel(stat_ref, o_ref, grad_ref, gain_ref, p_ref, *refs):
    normed_ref, d_ref, terms_ref, inverse_ref, factor_ref = refs
    tokens = o_ref.shape[0]
    stats = jnp.sum(stat_ref[...], axis=0)
    squares = jnp.broadcast_to(stats[0:1], (HEAD_SIZE, tokens)).T
    cross = jnp.broadcast_to(stats[1:2], (HEAD_SIZE, tokens)).T
    inverse = lax.rsqrt(squares / FEAT + epsilon)
    inverse_ref[...] = inverse
    factor_ref[...] = inverse * inverse * inverse * cross / FEAT

    @pl.loop(0, p_ref.shape[0])
    def _(h):
        cols = head_columns(h)
        out = o_ref[:, cols]
        inverse = inverse_ref[...]
        gain = gain_ref[:, cols]
        scaled = grad_ref[:, cols].astype(jnp.float32) * gain
        normed_ref[:, cols] = (out * inverse * gain).astype(normed_ref.dtype)
        d_attended = (inverse * scaled - out * factor_ref[...]).astype(d_ref.dtype)
        d_ref[:, cols] = d_attended
        terms_ref[:, cols] = dot(p_ref[h], d_attended, TN).astype(terms_ref.dtype)


def score_rows(d_ref, o_ref, value_cat, p_ref, h, rows, cols):
    d_attended = d_ref[rows, cols]
    delta = jnp.sum(d_attended.astype(jnp.float32) * o_ref[rows, cols], axis=1, keepdims=True)
    dprob = dot(d_attended, value_cat[...], NT)
    return (p_ref[h, rows].astype(jnp.float32) * (dprob - delta)).astype(jnp.bfloat16)


def middle_kernel(nblocks, n, start_ref, q_ref, o_ref, d_ref, pa_ref, pb_ref, *refs):
    key_in, value_in = refs[:n], refs[n : 2 * n]
    local_ref, export_ref, dq_ref, terms_ref = refs[2 * n : 2 * n + 4]
    slots = refs[2 * n + 4 : -4]
    key_cat, value_cat, score_ref, term_ref = refs[-4:]
    tokens = d_ref.shape[0]

    @pl.loop(0, pa_ref.shape[0])
    def _(h):
        cols = head_columns(h)
        gather_rows(key_cat, key_in, cols)
        gather_rows(value_cat, value_in, cols)
        put_terms(pa_ref[h], d_ref[:, cols], slots, tokens, cols, 1.0)
        term = dot(pa_ref[h, :, :tokens], d_ref[:, cols], TN)
        put_local(term, term_ref, local_ref, export_ref, start_ref, cols)
        for g in range(nblocks):
            rows = slice(g * BLK, (g + 1) * BLK)
            dscore = score_rows(d_ref, o_ref, value_cat, pb_ref, h, rows, cols)
            score_ref[rows] = dscore
            dq_ref[rows, cols] = dot(dscore, key_cat[...], NN)
        term = dot(score_ref[...], q_ref[:, cols], TN) * softmax_scale
        terms_ref[:, cols] = term.astype(terms_ref.dtype)


def key_kernel(nblocks, start_ref, q_ref, o_ref, d_ref, p_ref, dq_in, *refs):
    n = (len(refs) - 6) // 3
    key_cat, value_cat, score_ref, term_ref = refs[-4:]
    dq_ref, local_ref, export_ref = refs[2 * n : 2 * n + 3]
    slots = refs[2 * n + 3 : -4]
    tokens = q_ref.shape[0]

    @pl.loop(0, p_ref.shape[0])
    def _(h):
        cols = head_columns(h)
        gather_rows(key_cat, refs[:n], cols)
        gather_rows(value_cat, refs[n : 2 * n], cols)
        for g in range(nblocks):
            rows = slice(g * BLK, (g + 1) * BLK)
            dscore = score_rows(d_ref, o_ref, value_cat, p_ref, h, rows, cols)
            score_ref[rows] = dscore
            dq = dq_in[rows, cols] + dot(dscore, key_cat[...], NN)
            dq_ref[rows, cols] = (dq * softmax_scale).astype(dq_ref.dtype)
        put_terms(score_ref, q_ref[:, cols], slots, tokens, cols, softmax_scale)
        term = dot(score_ref[:, :tokens], q_ref[:, cols], TN) * softmax_scale
        put_local(term, term_ref, local_ref, export_ref, start_ref, cols)


def after(x, *earlier):
    return lax.optimization_barrier((x, earlier))[0]


def shards(queries, keys, values, gain, grad_out, pattern):
    n_seq = lax.axis_size("seq")
    far = n_seq // 2
    myself = lax.axis_index("seq")
    tokens, width = queries.shape
    heads = width // HEAD_SIZE
    nblocks = tokens // BLK
    a, b = myself // 2, myself % 2
    bf16, f32 = jnp.bfloat16, jnp.float32

    def move(x, to, among=None):
        among = range(far) if among is None else among
        return lax.ppermute(x, "seq", [(i * 2 + j, to(i) * 2 + j) for i in among for j in range(2)])

    def swap(x):
        return lax.ppermute(x, "seq", [(i, i ^ 1) for i in range(n_seq)])

    ranges = jnp.stack(
        [myself]
        + [(a ^ k) * 2 + b for k in range(1, far)]
        + [(a ^ k) * 2 + 1 - b for k in range(far)]
    )

    smem = pl.BlockSpec(memory_space=pltpu.SMEM)
    vmem = pl.BlockSpec(memory_space=pltpu.VMEM)
    shape = jax.ShapeDtypeStruct

    def call(name, kernel, inputs, out_shape, scratch=(), in_smem=(), out_smem=(), limit=10):
        single = not isinstance(out_shape, list)
        n_out = 1 if single else len(out_shape)
        out_specs = [smem if i in out_smem else vmem for i in range(n_out)]
        return pl.pallas_call(
            kernel,
            in_specs=[smem if i in in_smem else vmem for i in range(len(inputs))],
            out_specs=out_specs[0] if single else out_specs,
            out_shape=out_shape,
            scratch_shapes=[pltpu.VMEM(*s) for s in scratch],
            compiler_params=pltpu.CompilerParams(vmem_limit_bytes=limit * 1024 * 1024),
            cost_estimate=pl.CostEstimate(flops=10**11, bytes_accessed=10**8, transcendentals=0),
            name=name,
        )(*inputs)

    slot_shape = shape((BLK, width), bf16)
    key_own, value_own, both_own, start_vec = call(
        "pick",
        functools.partial(pick_kernel, nblocks),
        [myself.reshape(1), pattern, keys, values],
        [slot_shape, slot_shape, shape((2 * BLK, width), bf16), shape((1,), jnp.int32)],
        in_smem=(0,),
        out_smem=(3,),
    )
    start = start_vec[0]

    n_first, n_rest = far, far - 1
    first = tokens + n_first * BLK
    rest = n_rest * BLK

    def probabilities(key_near, key_mates):
        return call(
            "softmax",
            functools.partial(softmax_kernel, nblocks, first),
            [ranges, pattern, queries, keys, *key_near, *key_mates],
            [shape((heads, tokens, first), bf16), shape((heads, tokens, rest), bf16)],
            [((first + rest, HEAD_SIZE), bf16)],
            in_smem=(0, 1),
        )

    if far == 4:
        inner, outer = (1, 2), (0, 3)
        is_inner = (a == 1) | (a == 2)

        both = swap(both_own)
        k0, v0 = both[:BLK], both[BLK:]
        k1 = move(key_own, lambda i: i ^ 1)
        k2 = move(key_own, lambda i: i ^ 2)
        km = move(key_own, lambda i: i ^ 3, inner)
        kf = move(k2, lambda i: i ^ 1, inner)
        v1 = move(after(value_own, k1), lambda i: i ^ 1)
        v2 = move(after(value_own, k2), lambda i: i ^ 2)
        m1 = swap(k1)
        m2 = swap(after(k2, both))
        vm = move(after(value_own, km), lambda i: i ^ 3, inner)
        k3 = jnp.where(is_inner, after(km, m1), kf)
        m3 = swap(k3)
        n1 = swap(after(v1, m2))
        vf = move(v2, lambda i: i ^ 1, inner)
        n2 = swap(after(v2, m3))
        v3 = jnp.where(is_inner, vm, vf)
        n3 = swap(after(v3, n1))
        key_near, key_mates = [k1, k2, k3], [k0, m1, m2, m3]
        value_near, value_mates = [v1, v2, v3], [v0, n1, n2, n3]
        prob_first, prob_rest = probabilities(key_near, key_mates)
    else:
        key_near = [move(key_own, lambda i, k=k: i ^ k) for k in range(1, far)]
        value_near = [move(value_own, lambda i, k=k: i ^ k) for k in range(1, far)]
        key_mates = [swap(x) for x in [key_own] + key_near]
        value_mates = [swap(x) for x in [value_own] + value_near]
        prob_first, prob_rest = probabilities(key_near, key_mates)

    gain_row = gain.reshape(1, width)
    local_shapes = [shape((tokens, width), bf16), shape((BLK, width), f32)]

    attended = call(
        "attend",
        attend_kernel,
        [prob_first, values, *value_near, value_mates[0]],
        shape((tokens, width), f32),
        [((first, HEAD_SIZE), bf16)],
    )

    attended, stats = call(
        "attend_rest",
        attend_rest_kernel,
        [prob_rest, attended, grad_out, gain_row, *value_mates[1:]],
        [shape((tokens, width), f32), shape((8, tokens), f32)],
        [((rest, HEAD_SIZE), bf16), ((tokens, HEAD_SIZE), f32), ((tokens, HEAD_SIZE), f32)],
    )

    stats = lax.all_gather(stats, "head")

    normed, d_attended, value_rest = call(
        "grad_out",
        grad_out_kernel,
        [stats, attended, grad_out, gain_row, prob_rest],
        [shape((tokens, width), bf16)] * 2 + [shape((rest, width), bf16)],
        [((tokens, HEAD_SIZE), f32)] * 2,
    )
    value_rest = swap(value_rest)

    value_local, value_mine, dq_rest, key_rest, *value_first = call(
        "middle",
        functools.partial(middle_kernel, nblocks, n_rest),
        [
            start_vec,
            queries,
            attended,
            d_attended,
            prob_first,
            prob_rest,
            *key_mates[1:],
            *value_mates[1:],
        ],
        local_shapes
        + [shape((tokens, width), f32), shape((rest, width), bf16)]
        + [slot_shape] * n_first,
        [
            ((rest, HEAD_SIZE), bf16),
            ((rest, HEAD_SIZE), bf16),
            ((tokens, rest), bf16),
            ((tokens, HEAD_SIZE), f32),
        ],
        in_smem=(0,),
    )
    key_rest = swap(key_rest)

    grad_queries, key_local, key_mine, *key_first = call(
        "key_terms",
        functools.partial(key_kernel, nblocks),
        [
            start_vec,
            queries,
            attended,
            d_attended,
            prob_first,
            dq_rest,
            keys,
            *key_near,
            key_mates[0],
            values,
            *value_near,
            value_mates[0],
        ],
        [shape((tokens, width), bf16)] + local_shapes + [slot_shape] * n_first,
        [((first, HEAD_SIZE), bf16)] * 2 + [((tokens, first), bf16), ((tokens, HEAD_SIZE), f32)],
        in_smem=(0,),
    )

    def add(*terms):
        return sum(t.astype(f32) for t in terms)

    def send_back(near, mate, rest, mine):
        rest = [rest[k * BLK : (k + 1) * BLK] for k in range(n_rest)]
        if far == 4:
            c3 = add(near[2], rest[2]).astype(bf16)
            forwarded = move(c3, lambda i: i ^ 1, outer)
            came3 = move(c3, lambda i: i ^ 3, inner)
            c2 = add(near[1], rest[1], forwarded).astype(bf16)
            came2 = move(c2, lambda i: i ^ 2)
            c1 = add(near[0], rest[0]).astype(bf16)
            came1 = move(c1, lambda i: i ^ 1)
            came = [came1, came2, came3]
        else:
            came = [
                move(add(near[k - 1], rest[k - 1]).astype(bf16), lambda i, k=k: i ^ k)
                for k in range(1, far)
            ]
        return add(mine, swap(mate), *came).astype(bf16)

    grad_values = lax.dynamic_update_slice_in_dim(
        value_local,
        send_back(value_first[: far - 1], value_first[far - 1], value_rest, value_mine),
        start,
        0,
    )
    grad_keys = lax.dynamic_update_slice_in_dim(
        key_local,
        send_back(key_first[: far - 1], key_first[far - 1], key_rest, key_mine),
        start,
        0,
    )
    return normed, grad_queries, grad_keys, grad_values


def solution(mesh):
    split = P("seq", "head")
    return jax.shard_map(
        shards,
        mesh=mesh,
        in_specs=(split, split, split, P("head"), split, P()),
        out_specs=(split, split, split, split),
        check_vma=False,
    )
```

time: 433 us -> 164 us (0.38); the launches traced: 425 us -> 163 us
  matrix products: 139 us -> 0 us
  local copies, waits for them, and re-layouts: 133 us -> 13 us
  blocking collectives: 61.1 us -> 5.25 us
  Pallas kernels: 0 us -> 52.3 us
  other arithmetic: 40.2 us -> 6.33 us
  starting transfers between devices: 14.8 us -> 40.7 us
  waiting for transfers between devices: 34.8 us -> 42.7 us
    dot_general x14 -> x0, matrix products: 139 us -> none  [the longest x1 25.8 us: backward_group(): jnp.einsum('bjs,bjkw->skw', selector, key_terms, precision=lax.Precision....]
    reshape x9 -> x0, local copies, waits for them, and re-layouts: 63.4 us -> none  [the longest x2 33.6 us: backward_group(): value_terms = value_terms.reshape(per_group, REM, BLK, width)]
    all_to_all x1 -> x0, blocking collectives: 55.4 us -> none  [shards(): lax.all_to_all(key_send, 'seq', split_axis=0, concat_axis=0, tiled=True)]
    pallas_call x0 -> x7, Pallas kernels: none -> 52.3 us  [call(): pl.pallas_call(kernel, in_specs=[smem if i in in_smem else vmem for i in...]
    ppermute x0 -> x27, waiting for transfers between devices: none -> 42.7 us  [the longest x16 34.8 us: move(): lax.ppermute(x, 'seq', [(i * 2 + j, to(i) * 2 + j) for i in among for j i...]
    ppermute x0 -> x27, starting transfers between devices: none -> 40.7 us  [the longest x16 28.9 us: move(): lax.ppermute(x, 'seq', [(i * 2 + j, to(i) * 2 + j) for i in among for j i...]
    all_to_all x3 -> x0, waiting for transfers between devices: 34.8 us -> none  [the longest x1 21 us: shards(): lax.all_to_all(value_send, 'seq', split_axis=0, concat_axis=0, tiled=True)]
    unnamed x37 -> x47, local copies, waits for them, and re-layouts: 26.1 us -> 6.35 us
  transfers between devices with their start and end apart: 3 -> 27, of which waited for: 2 -> 11; matrix products, arithmetic and copies ran while one was open for 33% -> 6% of each run, Pallas kernels for 0% -> 27%
where the time goes in v2:
time: 164 us; the launch traced here: 163 us
  Pallas kernels  52.3 us (32%)
  waiting for transfers between devices  42.7 us (26%)
  starting transfers between devices  40.7 us (25%)
  local copies, waits for them, and re-layouts  13 us (8%)
  other arithmetic  6.33 us (4%)
  blocking collectives  5.25 us (3%)
  between operations  2.78 us (2%)
    pallas_call x7, Pallas kernels, call(): pl.pallas_call(kernel, in_specs=[smem if i in in_smem else vmem for i in...  52.3 us
    ppermute x16, waiting for transfers between devices, move(): lax.ppermute(x, 'seq', [(i * 2 + j, to(i) * 2 + j) for i in among for j i...  34.8 us
    ppermute x16, starting transfers between devices, move(): lax.ppermute(x, 'seq', [(i * 2 + j, to(i) * 2 + j) for i in among for j i...  28.9 us
    ppermute x11, starting transfers between devices, swap(): return lax.ppermute(x, 'seq', [(i, i ^ 1) for i in range(n_seq)])  11.8 us
    ppermute x11, waiting for transfers between devices, swap(): return lax.ppermute(x, 'seq', [(i, i ^ 1) for i in range(n_seq)])  7.89 us
    unnamed x47, local copies, waits for them, and re-layouts  6.35 us
    all_gather x1, blocking collectives, shards(): stats = lax.all_gather(stats, 'head')  5.25 us
  transfers between devices with their start and end apart: 27, of which 11 were waited for; matrix products, arithmetic and copies ran while one was open for 6% of the time, Pallas kernels for 27%

profile of v2, /device:TPU:0, one launch (start us, length us, event | category | flops | bytes accessed | tf_op | source)
XLA Modules:
  0.0 163.0 jit_solution(13687227570207709253)
XLA Ops:
  5.5 3.0 %collective-permute-start = (bf16[128,1024]{1,0:T(8,128)(2,1)}, bf16[128,1024]{1,0:T(8,128)(2,1)S(1)}, u32[]{:S(2)}, u32[]{:S(2)}) collective-permute-start(bf16[128,1024]{1,0:T(8,128)(2,1)} %get-tuple-element.38), channel_id=1, source_target_pairs={{0,8},{4,12},{8,0},{12,4},{16,24},{20,28},{24,16},{28,20},{1,9},{5... | collective-permute-start | bytes 786440 | tf_op jit(solution)/shard_map/ppermute | solution.py:236
  10.0 2.6 %collective-permute-start.1 = (bf16[128,1024]{1,0:T(8,128)(2,1)}, bf16[128,1024]{1,0:T(8,128)(2,1)S(1)}, u32[]{:S(2)}, u32[]{:S(2)}) collective-permute-start(bf16[128,1024]{1,0:T(8,128)(2,1)} %get-tuple-element.38), channel_id=1, source_target_pairs={{0,16},{4,20},{8,24},{12,28},{16,0},{20,4},{24,8},{28,12},{1,17},{... | collective-permute-start | bytes 786440 | tf_op jit(solution)/shard_map/ppermute | solution.py:236
  14.0 5.1 %collective-permute-done.refs_1_ = bf16[128,1024]{1,0:T(8,128)(2,1)S(1)} collective-permute-done((bf16[128,1024]{1,0:T(8,128)(2,1)}, bf16[128,1024]{1,0:T(8,128)(2,1)S(1)}, u32[]{:S(2)}, u32[]{:S(2)}) %collective-permute-start) | collective-permute-done | bytes 262176 | tf_op jit(solution)/shard_map/ppermute | solution.py:236
  19.1 2.2 %collective-permute-start.3 = (bf16[128,1024]{1,0:T(8,128)(2,1)S(1)}, bf16[128,1024]{1,0:T(8,128)(2,1)S(1)}, u32[]{:S(2)}, u32[]{:S(2)}) collective-permute-start(bf16[128,1024]{1,0:T(8,128)(2,1)S(1)} %collective-permute-done.refs_1_), channel_id=1, source_target_pairs={{0,4},{4,0},{8,12},{12,8},{16,20},{20,16},{24,28},{28,24},{1,5},{5... | collective-permute-start | bytes 786440 | tf_op jit(solution)/shard_map/ppermute | solution.py:239
  21.3 4.7 %collective-permute-done.1.refs_2_ = bf16[128,1024]{1,0:T(8,128)(2,1)S(1)} collective-permute-done((bf16[128,1024]{1,0:T(8,128)(2,1)}, bf16[128,1024]{1,0:T(8,128)(2,1)S(1)}, u32[]{:S(2)}, u32[]{:S(2)}) %collective-permute-start.1) | collective-permute-done | bytes 262176 | tf_op jit(solution)/shard_map/ppermute | solution.py:236
  27.3 4.3 %collective-permute-start.9 = (bf16[128,1024]{1,0:T(8,128)(2,1)}, bf16[128,1024]{1,0:T(8,128)(2,1)}, u32[]{:S(2)}, u32[]{:S(2)}) collective-permute-start(bf16[128,1024]{1,0:T(8,128)(2,1)} %copy-done.19), channel_id=1, source_target_pairs={{0,16},{4,20},{8,24},{12,28},{16,0},{20,4},{24,8},{28,12},{1,17},{... | collective-permute-start | bytes 786440 | tf_op jit(solution)/shard_map/ppermute | solution.py:236
  31.6 3.4 %collective-permute-start.8 = (bf16[128,1024]{1,0:T(8,128)(2,1)}, bf16[128,1024]{1,0:T(8,128)(2,1)}, u32[]{:S(2)}, u32[]{:S(2)}) collective-permute-start(bf16[128,1024]{1,0:T(8,128)(2,1)} %copy-done.19), channel_id=1, source_target_pairs={{0,8},{4,12},{8,0},{12,4},{16,24},{20,28},{24,16},{28,20},{1,9},{5... | collective-permute-start | bytes 786440 | tf_op jit(solution)/shard_map/ppermute | solution.py:236
  36.3 4.3 %collective-permute-done.4 = bf16[128,1024]{1,0:T(8,128)(2,1)} collective-permute-done((bf16[128,1024]{1,0:T(8,128)(2,1)S(1)}, bf16[128,1024]{1,0:T(8,128)(2,1)}, u32[]{:S(2)}, u32[]{:S(2)}) %collective-permute-start.4) | collective-permute-done | bytes 262176 | tf_op jit(solution)/shard_map/ppermute | solution.py:236
  47.0 2.9 %collective-permute-done.7.refs_7_.refs_2_ = bf16[128,1024]{1,0:T(8,128)(2,1)S(1)} collective-permute-done((bf16[128,1024]{1,0:T(8,128)(2,1)S(1)}, bf16[128,1024]{1,0:T(8,128)(2,1)S(1)}, u32[]{:S(2)}, u32[]{:S(2)}) %collective-permute-start.7) | collective-permute-done | bytes 262176 | tf_op jit(solution)/shard_map/ppermute | solution.py:239
  50.9 10.6 %softmax.1 = (bf16[8,512,1024]{2,1,0:T(8,128)(2,1)S(1)}, bf16[8,512,384]{2,1,0:T(8,128)(2,1)S(1)}) custom-call(s32[8]{0:T(128)S(1)} %stack.35.ranges_ref, s32[32,10]{1,0:T(8,128)S(1)} %copy.11.pattern_ref, bf16[512,1024]{1,0:T(8,128)(2,1)S(1)} %copy-done.9, bf16[512,1024]{1,0:T(8,128)(2,1)S(1)} %copy-done.12, ...), custom_call_target="tpu_custom_call" | custom-call | flops 99999997952 | bytes 100000000 | tf_op jit(solution)/shard_map/softmax/pallas_call | solution.py:255
  61.6 2.1 %collective-permute-start.14 = (bf16[128,1024]{1,0:T(8,128)(2,1)S(1)}, bf16[128,1024]{1,0:T(8,128)(2,1)S(1)}, u32[]{:S(2)}, u32[]{:S(2)}) collective-permute-start(bf16[128,1024]{1,0:T(8,128)(2,1)S(1)} %broadcast_select_fusion.refs_3_.refs_8_), channel_id=1, source_target_pairs={{0,4},{4,0},{8,12},{12,8},{16,20},{20,16},{24,28},{28,24},{1,5},{5... | collective-permute-start | bytes 786440 | tf_op jit(solution)/shard_map/ppermute | solution.py:239
  63.7 5.0 %attend.1.o_in = f32[512,1024]{1,0:T(8,128)S(1)} custom-call(bf16[8,512,1024]{2,1,0:T(8,128)(2,1)S(1)} %get-tuple-element.43.p_ref.pa_ref, bf16[512,1024]{1,0:T(8,128)(2,1)S(1)} %copy-done.14, bf16[128,1024]{1,0:T(8,128)(2,1)} %collective-permute-done.8.refs_1_.refs_6_, bf16[128,1024]{1,0:T(8,128)(2,1)} %collective-permute-done.9.refs_2_.refs_7_, ...), custom_call_target="tpu_custom_call" | custom-call | flops 99999997952 | bytes 100000000 | tf_op jit(solution)/shard_map/attend/pallas_call | solution.py:255
  68.8 3.8 %attend_rest.1 = (f32[512,1024]{1,0:T(8,128)S(1)}, f32[8,512]{1,0:T(8,128)S(1)}) custom-call(bf16[8,512,384]{2,1,0:T(8,128)(2,1)S(1)} %get-tuple-element.42.p_ref.pb_ref, f32[512,1024]{1,0:T(8,128)S(1)} %attend.1.o_in, bf16[512,1024]{1,0:T(8,128)(2,1)S(1)} %copy-done.8, f32[1,1024]{1,0:T(1,128)S(1)} %bitcast.12, ...), custom_call_target="tpu_custom_call" | custom-call | flops 99999997952 | bytes 100000000 | tf_op jit(solution)/shard_map/attend_rest/pallas_call | solution.py:255
  72.6 5.2 %all-gather = f32[32,512]{1,0:T(8,128)S(1)} all-gather(f32[8,512]{1,0:T(8,128)S(1)} %get-tuple-element.51), channel_id=2, replica_groups=mesh['seq'=8,'head'=4] {'head'}, dimensions={0}, use_global_device_ids=true | all-gather | bytes 81920 | tf_op jit(solution)/shard_map/all_gather | solution.py:342
  77.9 3.9 %grad_out.1 = (bf16[512,1024]{1,0:T(8,128)(2,1)}, bf16[512,1024]{1,0:T(8,128)(2,1)S(1)}, bf16[384,1024]{1,0:T(8,128)(2,1)S(1)}) custom-call(f32[4,8,512]{2,1,0:T(8,128)S(1)} %bitcast.11, f32[512,1024]{1,0:T(8,128)S(1)} %get-tuple-element.52.o_ref, bf16[512,1024]{1,0:T(8,128)(2,1)S(1)} %copy-done.8, f32[1,1024]{1,0:T(1,128)S(1)} %bitcast.13, ...), custom_call_target="tpu_custom_call" | custom-call | flops 99999997952 | bytes 100000000 | tf_op jit(solution)/shard_map/grad_out/pallas_call | solution.py:255
  83.1 13.4 %middle.1 = (bf16[512,1024]{1,0:T(8,128)(2,1)}, f32[128,1024]{1,0:T(8,128)S(1)}, f32[512,1024]{1,0:T(8,128)S(1)}, bf16[384,1024]{1,0:T(8,128)(2,1)S(1)}, bf16[12...) custom-call(s32[1]{0:T(128)} %get-tuple-element.54.start_ref, ...), custom_call_target="tpu_custom_call" | custom-call | flops 99999997952 | bytes 100000000 | tf_op jit(solution)/shard_map/middle/pallas_call | solution.py:255
  97.1 4.9 %collective-permute-done.22 = bf16[384,1024]{1,0:T(8,128)(2,1)S(1)} collective-permute-done((bf16[384,1024]{1,0:T(8,128)(2,1)S(1)}, bf16[384,1024]{1,0:T(8,128)(2,1)S(1)}, u32[]{:S(2)}, u32[]{:S(2)}) %collective-permute-start.22) | collective-permute-done | bytes 786464 | tf_op jit(solution)/shard_map/ppermute | solution.py:239
  104.7 14.7 %key_terms.1 = (bf16[512,1024]{1,0:T(8,128)(2,1)}, bf16[512,1024]{1,0:T(8,128)(2,1)}, f32[128,1024]{1,0:T(8,128)S(1)}, bf16[128,1024]{1,0:T(8,128)(2,1)S(1)}, bf...) custom-call(s32[1]{0:T(128)} %get-tuple-element.54.start_ref, ...), custom_call_target="tpu_custom_call" | custom-call | flops 99999997952 | bytes 100000000 | tf_op jit(solution)/shard_map/key_terms/pallas_call | solution.py:255
  130.9 1.9 %add_convert_fusion.5 = bf16[128,1024]{1,0:T(8,128)(2,1)} fusion(bf16[128,1024]{1,0:T(8,128)(2,1)} %copy-done.22, bf16[128,1024]{1,0:T(8,128)(2,1)S(1)} %get-tuple-element.63, bf16[384,1024]{1,0:T(8,128)(2,1)} %copy-done.21), kind=kLoop, calls=%fused_computation.5 | loop fusion | flops 786432 | bytes 1048576 | tf_op jit(solution)/shard_map/convert_element_type | solution.py:410
  134.4 3.5 %collective-permute-start.17 = (bf16[128,1024]{1,0:T(8,128)(2,1)}, bf16[128,1024]{1,0:T(8,128)(2,1)S(1)}, u32[]{:S(2)}, u32[]{:S(2)}) collective-permute-start(bf16[128,1024]{1,0:T(8,128)(2,1)} %get-tuple-element.74), channel_id=1, source_target_pairs={{0,8},{4,12},{8,0},{12,4},{16,24},{20,28},{24,16},{28,20},{1,9},{5... | collective-permute-start | bytes 786440 | tf_op jit(solution)/shard_map/ppermute | solution.py:236
  138.6 6.3 %collective-permute-done.25 = bf16[128,1024]{1,0:T(8,128)(2,1)S(1)} collective-permute-done((bf16[128,1024]{1,0:T(8,128)(2,1)S(1)}, bf16[128,1024]{1,0:T(8,128)(2,1)S(1)}, u32[]{:S(2)}, u32[]{:S(2)}) %collective-permute-start.25) | collective-permute-done | bytes 262176 | tf_op jit(solution)/shard_map/ppermute | solution.py:236
  145.1 2.8 %dynamic_update_slice.7 = bf16[512,1024]{1,0:T(8,128)(2,1)} dynamic-update-slice(bf16[512,1024]{1,0:T(8,128)(2,1)} %get-tuple-element.65, bf16[128,1024]{1,0:T(8,128)(2,1)S(1)} %add_convert_fusion, s32[]{:T(128)S(6)} %select_n.32, s32[]{:T(128)} %constant.31.clone.1) | dynamic-update-slice | bytes 524292 | tf_op jit(solution)/shard_map/dynamic_update_slice | solution.py:422
  147.9 11.3 %collective-permute-done.19 = bf16[128,1024]{1,0:T(8,128)(2,1)} collective-permute-done((bf16[128,1024]{1,0:T(8,128)(2,1)}, bf16[128,1024]{1,0:T(8,128)(2,1)}, u32[]{:S(2)}, u32[]{:S(2)}) %collective-permute-start.19) | collective-permute-done | bytes 262176 | tf_op jit(solution)/shard_map/ppermute | solution.py:236
  160.3 2.8 %dynamic_update_slice.6 = bf16[512,1024]{1,0:T(8,128)(2,1)} dynamic-update-slice(bf16[512,1024]{1,0:T(8,128)(2,1)} %get-tuple-element.58, bf16[128,1024]{1,0:T(8,128)(2,1)S(1)} %add_convert_fusion.4, s32[]{:T(128)S(6)} %select_n.32, s32[]{:T(128)} %constant.31.clone.1) | dynamic-update-slice | bytes 524292 | tf_op jit(solution)/shard_map/dynamic_update_slice | solution.py:428
  (97 shorter events, 35.6 us)
Async XLA Ops:
  5.5 13.6 %collective-permute-start = (bf16[128,1024]{1,0:T(8,128)(2,1)}, bf16[128,1024]{1,0:T(8,128)(2,1)S(1)}, u32[]{:S(2)}, u32[]{:S(2)}) collective-permute-start(bf16[128,1024]{1,0:T(8,128)(2,1)} %get-tuple-element.38), channel_id=1, source_target_pairs={{0,8},{4,12},{8,0},{12,4},{16,24},{20,28},{24,16},{28,20},{1,9},{5... | collective-permute-start | bytes 786440 | tf_op jit(solution)/shard_map/ppermute | solution.py:236
  8.5 27.3 %collective-permute-start.5 = (bf16[256,1024]{1,0:T(8,128)(2,1)S(1)}, bf16[256,1024]{1,0:T(8,128)(2,1)}, u32[]{:S(2)}, u32[]{:S(2)}) collective-permute-start(bf16[256,1024]{1,0:T(8,128)(2,1)S(1)} %get-tuple-element.40), channel_id=1, source_target_pairs={{0,4},{4,0},{8,12},{12,8},{16,20},{20,16},{24,28},{28,24},{1,5},{5... | collective-permute-start | bytes 1572872 | tf_op jit(solution)/shard_map/ppermute | solution.py:239
  10.0 16.0 %collective-permute-start.1 = (bf16[128,1024]{1,0:T(8,128)(2,1)}, bf16[128,1024]{1,0:T(8,128)(2,1)S(1)}, u32[]{:S(2)}, u32[]{:S(2)}) collective-permute-start(bf16[128,1024]{1,0:T(8,128)(2,1)} %get-tuple-element.38), channel_id=1, source_target_pairs={{0,16},{4,20},{8,24},{12,28},{16,0},{20,4},{24,8},{28,12},{1,17},{... | collective-permute-start | bytes 786440 | tf_op jit(solution)/shard_map/ppermute | solution.py:236
  12.6 19.0 %collective-permute-start.2 = (bf16[128,1024]{1,0:T(8,128)(2,1)}, bf16[128,1024]{1,0:T(8,128)(2,1)}, u32[]{:S(2)}, u32[]{:S(2)}) collective-permute-start(bf16[128,1024]{1,0:T(8,128)(2,1)} %get-tuple-element.38), channel_id=1, source_target_pairs={{8,16},{12,20},{16,8},{20,12},{9,17},{13,21},{17,9},{21,13},{10,18... | collective-permute-start | bytes 786440 | tf_op jit(solution)/shard_map/ppermute | solution.py:236
  19.1 16.0 %collective-permute-start.3 = (bf16[128,1024]{1,0:T(8,128)(2,1)S(1)}, bf16[128,1024]{1,0:T(8,128)(2,1)S(1)}, u32[]{:S(2)}, u32[]{:S(2)}) collective-permute-start(bf16[128,1024]{1,0:T(8,128)(2,1)S(1)} %collective-permute-done.refs_1_), channel_id=1, source_target_pairs={{0,4},{4,0},{8,12},{12,8},{16,20},{20,16},{24,28},{28,24},{1,5},{5... | collective-permute-start | bytes 786440 | tf_op jit(solution)/shard_map/ppermute | solution.py:239
  26.0 14.6 %collective-permute-start.4 = (bf16[128,1024]{1,0:T(8,128)(2,1)S(1)}, bf16[128,1024]{1,0:T(8,128)(2,1)}, u32[]{:S(2)}, u32[]{:S(2)}) collective-permute-start(bf16[128,1024]{1,0:T(8,128)(2,1)S(1)} %collective-permute-done.1.refs_2_), channel_id=1, source_target_pairs={{8,0},{12,4},{16,24},{20,28},{9,1},{13,5},{17,25},{21,29},{10,2},{... | collective-permute-start | bytes 786440 | tf_op jit(solution)/shard_map/ppermute | solution.py:236
  27.3 15.7 %collective-permute-start.9 = (bf16[128,1024]{1,0:T(8,128)(2,1)}, bf16[128,1024]{1,0:T(8,128)(2,1)}, u32[]{:S(2)}, u32[]{:S(2)}) collective-permute-start(bf16[128,1024]{1,0:T(8,128)(2,1)} %copy-done.19), channel_id=1, source_target_pairs={{0,16},{4,20},{8,24},{12,28},{16,0},{20,4},{24,8},{28,12},{1,17},{... | collective-permute-start | bytes 786440 | tf_op jit(solution)/shard_map/ppermute | solution.py:236
  31.6 14.6 %collective-permute-start.8 = (bf16[128,1024]{1,0:T(8,128)(2,1)}, bf16[128,1024]{1,0:T(8,128)(2,1)}, u32[]{:S(2)}, u32[]{:S(2)}) collective-permute-start(bf16[128,1024]{1,0:T(8,128)(2,1)} %copy-done.19), channel_id=1, source_target_pairs={{0,8},{4,12},{8,0},{12,4},{16,24},{20,28},{24,16},{28,20},{1,9},{5... | collective-permute-start | bytes 786440 | tf_op jit(solution)/shard_map/ppermute | solution.py:236
  35.8 10.4 %collective-permute-start.6 = (bf16[128,1024]{1,0:T(8,128)(2,1)S(1)}, bf16[128,1024]{1,0:T(8,128)(2,1)S(1)}, u32[]{:S(2)}, u32[]{:S(2)}) collective-permute-start(bf16[128,1024]{1,0:T(8,128)(2,1)S(1)} %collective-permute-done.1.refs_2_), channel_id=1, source_target_pairs={{0,4},{4,0},{8,12},{12,8},{16,20},{20,16},{24,28},{28,24},{1,5},{5... | collective-permute-start | bytes 786440 | tf_op jit(solution)/shard_map/ppermute | solution.py:239
  41.8 19.7 %collective-permute-start.10 = (bf16[128,1024]{1,0:T(8,128)(2,1)}, bf16[128,1024]{1,0:T(8,128)(2,1)S(1)}, u32[]{:S(2)}, u32[]{:S(2)}) collective-permute-start(bf16[128,1024]{1,0:T(8,128)(2,1)} %copy-done.19), channel_id=1, source_target_pairs={{8,16},{12,20},{16,8},{20,12},{9,17},{13,21},{17,9},{21,13},{10,18... | collective-permute-start | bytes 786440 | tf_op jit(solution)/shard_map/ppermute | solution.py:236
  43.0 18.6 %collective-permute-start.11 = (bf16[128,1024]{1,0:T(8,128)(2,1)}, bf16[128,1024]{1,0:T(8,128)(2,1)S(1)}, u32[]{:S(2)}, u32[]{:S(2)}) collective-permute-start(bf16[128,1024]{1,0:T(8,128)(2,1)} %collective-permute-done.9.refs_2_.refs_7_), channel_id=1, source_target_pairs={{8,0},{12,4},{16,24},{20,28},{9,1},{13,5},{17,25},{21,29},{10,2},{... | collective-permute-start | bytes 786440 | tf_op jit(solution)/shard_map/ppermute | solution.py:236
  46.2 15.4 %collective-permute-start.12 = (bf16[128,1024]{1,0:T(8,128)(2,1)}, bf16[128,1024]{1,0:T(8,128)(2,1)S(1)}, u32[]{:S(2)}, u32[]{:S(2)}) collective-permute-start(bf16[128,1024]{1,0:T(8,128)(2,1)} %collective-permute-done.8.refs_1_.refs_6_), channel_id=1, source_target_pairs={{0,4},{4,0},{8,12},{12,8},{16,20},{20,16},{24,28},{28,24},{1,5},{5... | collective-permute-start | bytes 786440 | tf_op jit(solution)/shard_map/ppermute | solution.py:239
  49.9 18.8 %collective-permute-start.13 = (bf16[128,1024]{1,0:T(8,128)(2,1)}, bf16[128,1024]{1,0:T(8,128)(2,1)}, u32[]{:S(2)}, u32[]{:S(2)}) collective-permute-start(bf16[128,1024]{1,0:T(8,128)(2,1)} %collective-permute-done.9.refs_2_.refs_7_), channel_id=1, source_target_pairs={{0,4},{4,0},{8,12},{12,8},{16,20},{20,16},{24,28},{28,24},{1,5},{5... | collective-permute-start | bytes 786440 | tf_op jit(solution)/shard_map/ppermute | solution.py:239
  81.7 20.4 %collective-permute-start.22 = (bf16[384,1024]{1,0:T(8,128)(2,1)S(1)}, bf16[384,1024]{1,0:T(8,128)(2,1)S(1)}, u32[]{:S(2)}, u32[]{:S(2)}) collective-permute-start(bf16[384,1024]{1,0:T(8,128)(2,1)S(1)} %get-tuple-element.69), channel_id=1, source_target_pairs={{0,4},{4,0},{8,12},{12,8},{16,20},{20,16},{24,28},{28,24},{1,5},{5... | collective-permute-start | bytes 2359304 | tf_op jit(solution)/shard_map/ppermute | solution.py:239
  96.4 23.0 %collective-permute-start.16 = (bf16[384,1024]{1,0:T(8,128)(2,1)S(1)}, bf16[384,1024]{1,0:T(8,128)(2,1)S(1)}, u32[]{:S(2)}, u32[]{:S(2)}) collective-permute-start(bf16[384,1024]{1,0:T(8,128)(2,1)S(1)} %get-tuple-element.62), channel_id=1, source_target_pairs={{0,4},{4,0},{8,12},{12,8},{16,20},{20,16},{24,28},{28,24},{1,5},{5... | collective-permute-start | bytes 2359304 | tf_op jit(solution)/shard_map/ppermute | solution.py:239
  103.0 22.3 %collective-permute-start.24 = (bf16[128,1024]{1,0:T(8,128)(2,1)}, bf16[128,1024]{1,0:T(8,128)(2,1)S(1)}, u32[]{:S(2)}, u32[]{:S(2)}) collective-permute-start(bf16[128,1024]{1,0:T(8,128)(2,1)} %get-tuple-element.73), channel_id=1, source_target_pairs={{0,8},{4,12},{24,16},{28,20},{1,9},{5,13},{25,17},{29,21},{2,10},{... | collective-permute-start | bytes 786440 | tf_op jit(solution)/shard_map/ppermute | solution.py:236
  121.8 10.9 %collective-permute-start.21 = (bf16[128,1024]{1,0:T(8,128)(2,1)}, bf16[128,1024]{1,0:T(8,128)(2,1)S(1)}, u32[]{:S(2)}, u32[]{:S(2)}) collective-permute-start(bf16[128,1024]{1,0:T(8,128)(2,1)} %get-tuple-element.67), channel_id=1, source_target_pairs={{0,4},{4,0},{8,12},{12,8},{16,20},{20,16},{24,28},{28,24},{1,5},{5... | collective-permute-start | bytes 786440 | tf_op jit(solution)/shard_map/ppermute | solution.py:239
  123.2 14.6 %collective-permute-start.26 = (bf16[128,1024]{1,0:T(8,128)(2,1)}, bf16[128,1024]{1,0:T(8,128)(2,1)S(1)}, u32[]{:S(2)}, u32[]{:S(2)}) collective-permute-start(bf16[128,1024]{1,0:T(8,128)(2,1)} %get-tuple-element.73), channel_id=1, source_target_pairs={{8,16},{12,20},{16,8},{20,12},{9,17},{13,21},{17,9},{21,13},{10,18... | collective-permute-start | bytes 786440 | tf_op jit(solution)/shard_map/ppermute | solution.py:236
  123.8 10.5 %collective-permute-start.23 = (bf16[128,1024]{1,0:T(8,128)(2,1)S(1)}, bf16[128,1024]{1,0:T(8,128)(2,1)S(1)}, u32[]{:S(2)}, u32[]{:S(2)}) collective-permute-start(bf16[128,1024]{1,0:T(8,128)(2,1)S(1)} %get-tuple-element.72), channel_id=1, source_target_pairs={{0,8},{4,12},{8,0},{12,4},{16,24},{20,28},{24,16},{28,20},{1,9},{5... | collective-permute-start | bytes 786440 | tf_op jit(solution)/shard_map/ppermute | solution.py:236
  125.4 19.5 %collective-permute-start.25 = (bf16[128,1024]{1,0:T(8,128)(2,1)S(1)}, bf16[128,1024]{1,0:T(8,128)(2,1)S(1)}, u32[]{:S(2)}, u32[]{:S(2)}) collective-permute-start(bf16[128,1024]{1,0:T(8,128)(2,1)S(1)} %add_convert_fusion.1), channel_id=1, source_target_pairs={{0,16},{4,20},{8,24},{12,28},{16,0},{20,4},{24,8},{28,12},{1,17},{... | collective-permute-start | bytes 786440 | tf_op jit(solution)/shard_map/ppermute | solution.py:236
  129.5 18.3 %collective-permute-start.15 = (bf16[128,1024]{1,0:T(8,128)(2,1)S(1)}, bf16[128,1024]{1,0:T(8,128)(2,1)S(1)}, u32[]{:S(2)}, u32[]{:S(2)}) collective-permute-start(bf16[128,1024]{1,0:T(8,128)(2,1)S(1)} %get-tuple-element.60), channel_id=1, source_target_pairs={{0,4},{4,0},{8,12},{12,8},{16,20},{20,16},{24,28},{28,24},{1,5},{5... | collective-permute-start | bytes 786440 | tf_op jit(solution)/shard_map/ppermute | solution.py:239
  132.7 15.1 %collective-permute-start.20 = (bf16[128,1024]{1,0:T(8,128)(2,1)}, bf16[128,1024]{1,0:T(8,128)(2,1)S(1)}, u32[]{:S(2)}, u32[]{:S(2)}) collective-permute-start(bf16[128,1024]{1,0:T(8,128)(2,1)} %get-tuple-element.75), channel_id=1, source_target_pairs={{8,16},{12,20},{16,8},{20,12},{9,17},{13,21},{17,9},{21,13},{10,18... | collective-permute-start | bytes 786440 | tf_op jit(solution)/shard_map/ppermute | solution.py:236
  134.4 13.5 %collective-permute-start.17 = (bf16[128,1024]{1,0:T(8,128)(2,1)}, bf16[128,1024]{1,0:T(8,128)(2,1)S(1)}, u32[]{:S(2)}, u32[]{:S(2)}) collective-permute-start(bf16[128,1024]{1,0:T(8,128)(2,1)} %get-tuple-element.74), channel_id=1, source_target_pairs={{0,8},{4,12},{8,0},{12,4},{16,24},{20,28},{24,16},{28,20},{1,9},{5... | collective-permute-start | bytes 786440 | tf_op jit(solution)/shard_map/ppermute | solution.py:236
  137.8 21.3 %collective-permute-start.19 = (bf16[128,1024]{1,0:T(8,128)(2,1)}, bf16[128,1024]{1,0:T(8,128)(2,1)}, u32[]{:S(2)}, u32[]{:S(2)}) collective-permute-start(bf16[128,1024]{1,0:T(8,128)(2,1)} %add_convert_fusion.5), channel_id=1, source_target_pairs={{0,16},{4,20},{8,24},{12,28},{16,0},{20,4},{24,8},{28,12},{1,17},{... | collective-permute-start | bytes 786440 | tf_op jit(solution)/shard_map/ppermute | solution.py:236
  (26 other events, 330.3 us)

commit v3 on v2

v3 whole, which is shorter than its diff:
```python
import functools

import jax
import jax.numpy as jnp
from jax import lax
from jax.experimental import pallas as pl
from jax.experimental.pallas import tpu as pltpu
from jax.sharding import PartitionSpec as P

HEAD_SIZE = 128
BLK = 128
LOC = 3
REM = 7
FEAT = 4096
LOW = -1e30

epsilon = 1e-06
softmax_scale = 1.0 / HEAD_SIZE**0.5

NT = (((1,), (1,)), ((), ()))
NN = (((1,), (0,)), ((), ()))
TN = (((0,), (0,)), ((), ()))


def dot(a, b, dims):
    return lax.dot_general(a, b, dims, preferred_element_type=jnp.float32)


def head_columns(h):
    return pl.ds(pl.multiple_of(h * HEAD_SIZE, HEAD_SIZE), HEAD_SIZE)


def blocks(first, count=1):
    return slice(first * BLK, (first + count) * BLK)


def pick_kernel(
    nblocks, me_ref, pattern_hbm, key_hbm, value_hbm, own_ref, start_ref, pattern_ref, key_ref, value_ref, sems
):
    copies = [
        pltpu.make_async_copy(source, target, sems.at[i])
        for i, (source, target) in enumerate(
            [(pattern_hbm, pattern_ref), (key_hbm, key_ref), (value_hbm, value_ref)]
        )
    ]
    for copy in copies:
        copy.start()
    copies[0].wait()
    pattern = pattern_ref[...]
    low = me_ref[0] * nblocks
    row = lax.broadcasted_iota(jnp.int32, pattern.shape, 1)
    inside = (pattern >= low) & (pattern < low + nblocks)
    others = (row < low) | (row >= low + nblocks)
    offset = jnp.where(inside & others, pattern - low, 0).astype(jnp.float32)
    start = pl.multiple_of(jnp.max(offset).astype(jnp.int32) * BLK, BLK)
    start_ref[0] = start
    copies[1].wait()
    copies[2].wait()
    own_ref[:BLK] = key_ref[pl.ds(start, BLK)]
    own_ref[BLK:] = value_ref[pl.ds(start, BLK)]


def gather_rows(cat_ref, pieces, cols):
    at = 0
    for piece, rows in pieces:
        size = rows.stop - rows.start
        cat_ref[at : at + size] = piece[rows, cols]
        at += size


def keys_of(slots):
    return [(slot, blocks(0)) for slot in slots]


def values_of(slots):
    return [(slot, blocks(1)) for slot in slots]


def is_listed(nblocks, ranges_ref, pattern_ref, g, local=None, place=None):
    low = ranges_ref[0] * nblocks
    listed = None
    for i in range(LOC) if place is None else range(LOC, LOC + REM):
        entry = pattern_ref[i, low + g]
        same = entry == low + local if place is None else entry // nblocks == ranges_ref[place]
        listed = same if listed is None else listed | same
    return jnp.where(listed, 0.0, LOW)


def biased(scores, biases):
    parts = [scores[:, blocks(j)] for j in range(len(biases))]
    parts = [p if bias is None else p + bias for p, bias in zip(parts, biases)]
    return jnp.concatenate(parts, axis=1)


def first_scores_kernel(nblocks, far_bias, ranges_ref, pattern_ref, q_ref, k_ref, *refs):
    slots = refs[:-4]
    p_ref, peak_ref, total_ref, cat_ref = refs[-4:]
    listed = functools.partial(is_listed, nblocks, ranges_ref, pattern_ref)
    biases = [
        [listed(g, local=j) for j in range(nblocks)]
        + [listed(g, place=1 + j) if far_bias else None for j in range(len(slots))]
        for g in range(nblocks)
    ]

    @pl.loop(0, p_ref.shape[0])
    def _(h):
        cols = head_columns(h)
        gather_rows(cat_ref, [(k_ref, blocks(0, nblocks))] + keys_of(slots), cols)
        for g in range(nblocks):
            rows = blocks(g)
            scores = dot(q_ref[rows, cols], cat_ref[...], NT) * softmax_scale
            scores = biased(scores, biases[g])
            peak = jnp.max(scores, axis=1, keepdims=True)
            expo = jnp.exp(scores - peak)
            total = jnp.sum(expo, axis=1, keepdims=True)
            p_ref[h, rows] = expo.astype(p_ref.dtype)
            peak_ref[h, rows] = jnp.broadcast_to(peak, (BLK, HEAD_SIZE))
            total_ref[h, rows] = jnp.broadcast_to(total, (BLK, HEAD_SIZE))


def first_attend_kernel(nblocks, p_ref, v_ref, *refs):
    slots = refs[:-2]
    o_ref, cat_ref = refs[-2:]

    @pl.loop(0, p_ref.shape[0])
    def _(h):
        cols = head_columns(h)
        gather_rows(cat_ref, [(v_ref, blocks(0, nblocks))] + values_of(slots), cols)
        o_ref[:, cols] = dot(p_ref[h], cat_ref[...], NN)


def second_kernel(
    nblocks,
    far_bias,
    n_first,
    ranges_ref,
    pattern_ref,
    q_ref,
    peak_ref,
    total_ref,
    o_in,
    grad_ref,
    gain_ref,
    *refs,
):
    slots = refs[:-8]
    p_ref, scale_ref, o_ref, stat_ref, key_cat, value_cat, square_ref, cross_ref = refs[-8:]
    listed = functools.partial(is_listed, nblocks, ranges_ref, pattern_ref)
    biases = [
        [listed(g, place=1 + n_first + j) if far_bias else None for j in range(len(slots))]
        for g in range(nblocks)
    ]
    square_ref[...] = jnp.zeros_like(square_ref)
    cross_ref[...] = jnp.zeros_like(cross_ref)

    @pl.loop(0, p_ref.shape[0])
    def _(h):
        cols = head_columns(h)
        gather_rows(key_cat, keys_of(slots), cols)
        gather_rows(value_cat, values_of(slots), cols)
        scores = dot(q_ref[:, cols], key_cat[...], NT) * softmax_scale
        if far_bias:
            parts = [biased(scores[blocks(g)], biases[g]) for g in range(nblocks)]
            scores = jnp.concatenate(parts, axis=0)
        old = peak_ref[h]
        peak = jnp.maximum(old, jnp.max(scores, axis=1, keepdims=True))
        shrink = jnp.exp(old - peak)
        expo = jnp.exp(scores - jnp.concatenate([peak] * len(slots), axis=1))
        total = total_ref[h] * shrink + jnp.sum(expo, axis=1, keepdims=True)
        inverse = 1.0 / total
        prob = (expo * jnp.concatenate([inverse] * len(slots), axis=1)).astype(p_ref.dtype)
        p_ref[h] = prob
        scale = shrink * inverse
        scale_ref[h] = scale
        out = o_in[:, cols] * scale + dot(prob, value_cat[...], NN)
        o_ref[:, cols] = out
        scaled = grad_ref[:, cols].astype(jnp.float32) * gain_ref[:, cols]
        square_ref[...] += out * out
        cross_ref[...] += scaled * out

    stat_ref[0:1] = jnp.sum(square_ref[...].T, axis=0, keepdims=True)
    stat_ref[1:2] = jnp.sum(cross_ref[...].T, axis=0, keepdims=True)
    stat_ref[2:] = jnp.zeros_like(stat_ref[2:])


def score_grad(d, delta, scale, value_cat, parts):
    dprob = dot(d, value_cat, NT)
    result = []
    for j, (prob, takes) in enumerate(parts):
        part = prob.astype(jnp.float32) * (dprob[:, blocks(j)] - delta)
        result.append((part * scale if takes else part).astype(jnp.bfloat16))
    return jnp.concatenate(result, axis=1)


def put_slots(slots, prob_parts, d, d_scaled, dscore, q, cols):
    for j, (slot, (prob, takes)) in enumerate(zip(slots, prob_parts)):
        key_term = dot(dscore[:, blocks(j)], q, TN) * softmax_scale
        slot[:BLK, cols] = key_term.astype(slot.dtype)
        slot[BLK:, cols] = dot(prob, d_scaled if takes else d, TN).astype(slot.dtype)


def take(places, pa_ref, pb_ref, h):
    return [
        (pb_ref[h, :, blocks(j)], False) if part else (pa_ref[h, :, blocks(j)], True)
        for part, j in places
    ]


def grad_out_kernel(
    places,
    q_ref,
    stat_ref,
    o_ref,
    grad_ref,
    gain_ref,
    scale_ref,
    pa_ref,
    pb_ref,
    *refs,
):
    n = len(places)
    normed_ref, d_ref, scaled_d_ref, delta_ref, dq_ref = refs[n : n + 5]
    outs = refs[n + 5 : 2 * n + 5]
    inverse_ref, factor_ref, key_cat, value_cat = refs[2 * n + 5 :]
    tokens = o_ref.shape[0]
    stats = jnp.sum(stat_ref[...], axis=0)
    squares = jnp.broadcast_to(stats[0:1], (HEAD_SIZE, tokens)).T
    cross = jnp.broadcast_to(stats[1:2], (HEAD_SIZE, tokens)).T
    inverse = lax.rsqrt(squares / FEAT + epsilon)
    inverse_ref[...] = inverse
    factor_ref[...] = inverse * inverse * inverse * cross / FEAT

    @pl.loop(0, pa_ref.shape[0])
    def _(h):
        cols = head_columns(h)
        gather_rows(key_cat, keys_of(refs[:n]), cols)
        gather_rows(value_cat, values_of(refs[:n]), cols)
        out = o_ref[:, cols]
        inverse = inverse_ref[...]
        gain = gain_ref[:, cols]
        scaled = grad_ref[:, cols].astype(jnp.float32) * gain
        normed_ref[:, cols] = (out * inverse * gain).astype(normed_ref.dtype)
        d_attended = inverse * scaled - out * factor_ref[...]
        d = d_attended.astype(d_ref.dtype)
        d_scaled = (d_attended * scale_ref[h]).astype(d_ref.dtype)
        d_ref[:, cols] = d
        scaled_d_ref[:, cols] = d_scaled
        delta = jnp.sum(d.astype(jnp.float32) * out, axis=1, keepdims=True)
        delta = jnp.broadcast_to(delta, out.shape)
        delta_ref[h] = delta
        parts = take(places, pa_ref, pb_ref, h)
        dscore = score_grad(d, delta, scale_ref[h], value_cat[...], parts)
        dq_ref[:, cols] = dot(dscore, key_cat[...], NN)
        put_slots(outs, parts, d, d_scaled, dscore, q_ref[:, cols], cols)


def slots_kernel(places, q_ref, d_ref, scaled_d_ref, delta_ref, scale_ref, pa_ref, pb_ref, dq_in, *refs):
    n = len(places)
    dq_ref = refs[n]
    outs = refs[n + 1 : 2 * n + 1]
    key_cat, value_cat = refs[2 * n + 1 :]

    @pl.loop(0, pa_ref.shape[0])
    def _(h):
        cols = head_columns(h)
        gather_rows(key_cat, keys_of(refs[:n]), cols)
        gather_rows(value_cat, values_of(refs[:n]), cols)
        parts = take(places, pa_ref, pb_ref, h)
        d = d_ref[:, cols]
        dscore = score_grad(d, delta_ref[h], scale_ref[h], value_cat[...], parts)
        dq_ref[:, cols] = dq_in[:, cols] + dot(dscore, key_cat[...], NN)
        put_slots(outs, parts, d, scaled_d_ref[:, cols], dscore, q_ref[:, cols], cols)


def local_kernel(
    nblocks,
    start_ref,
    q_ref,
    k_ref,
    v_ref,
    d_ref,
    scaled_d_ref,
    delta_ref,
    scale_ref,
    pa_ref,
    dq_in,
    dq_ref,
    key_local_ref,
    value_local_ref,
    export_ref,
    key_term,
    value_term,
):
    start = pl.multiple_of(start_ref[0], BLK)
    tokens = q_ref.shape[0]

    @pl.loop(0, pa_ref.shape[0])
    def _(h):
        cols = head_columns(h)
        parts = [(pa_ref[h, :, blocks(j)], True) for j in range(nblocks)]
        dscore = score_grad(d_ref[:, cols], delta_ref[h], scale_ref[h], v_ref[:, cols], parts)
        dq = dq_in[:, cols] + dot(dscore, k_ref[:, cols], NN)
        dq_ref[:, cols] = (dq * softmax_scale).astype(dq_ref.dtype)
        key_term[...] = dot(dscore, q_ref[:, cols], TN) * softmax_scale
        value_term[...] = dot(pa_ref[h, :, :tokens], scaled_d_ref[:, cols], TN)
        key_local_ref[:, cols] = key_term[...].astype(key_local_ref.dtype)
        value_local_ref[:, cols] = value_term[...].astype(value_local_ref.dtype)
        export_ref[:BLK, cols] = key_term[pl.ds(start, BLK)]
        export_ref[BLK:, cols] = value_term[pl.ds(start, BLK)]


def finish_kernel(start_ref, mine_ref, *refs):
    came = refs[:-4]
    key_out, value_out = refs[-2:]
    total = mine_ref[...]
    for term in came:
        total = total + term[...].astype(jnp.float32)
    key_out[...] = total[:BLK].astype(key_out.dtype)
    value_out[...] = total[BLK:].astype(value_out.dtype)


def after(x, *earlier):
    return lax.optimization_barrier((x, earlier))[0]


def shards(queries, keys, values, gain, grad_out, pattern):
    n_seq = lax.axis_size("seq")
    far = n_seq // 2
    myself = lax.axis_index("seq")
    tokens, width = queries.shape
    heads = width // HEAD_SIZE
    nblocks = tokens // BLK
    a, b = myself // 2, myself % 2
    bf16, f32 = jnp.bfloat16, jnp.float32
    pattern = pattern.T
    inner, outer = (1, 2), (0, 3)

    def move(x, to, among=None):
        among = range(far) if among is None else among
        return lax.ppermute(x, "seq", [(i * 2 + j, to(i) * 2 + j) for i in among for j in range(2)])

    def swap(x):
        return lax.ppermute(x, "seq", [(i, i ^ 1) for i in range(n_seq)])

    half = far // 2
    is_inner = (a == 1) | (a == 2)
    sources = [a ^ k for k in range(1, far)]
    if far == 4:
        sources[1:] = [jnp.where(is_inner, a ^ 3, a ^ 2), jnp.where(is_inner, a ^ 2, a ^ 3)]
    near_ranges = [s * 2 + b for s in sources]
    mate_ranges = [s * 2 + 1 - b for s in [a] + sources]
    ranges = jnp.stack(
        [myself] + near_ranges[:-1] + mate_ranges[:half] + near_ranges[-1:] + mate_ranges[half:]
    )
    far_bias = n_seq - 1 != REM

    smem = pl.BlockSpec(memory_space=pltpu.SMEM)
    vmem = pl.BlockSpec(memory_space=pltpu.VMEM)
    shape = jax.ShapeDtypeStruct

    def call(name, kernel, inputs, out_shape, scratch=(), in_smem=(), out_smem=(), cost=10**8):
        single = not isinstance(out_shape, list)
        n_out = 1 if single else len(out_shape)
        out_specs = [smem if i in out_smem else vmem for i in range(n_out)]
        return pl.pallas_call(
            kernel,
            in_specs=[smem if i in in_smem else vmem for i in range(len(inputs))],
            out_specs=out_specs[0] if single else out_specs,
            out_shape=out_shape,
            scratch_shapes=[pltpu.VMEM(*s) for s in scratch],
            compiler_params=pltpu.CompilerParams(vmem_limit_bytes=12 * 1024 * 1024),
            cost_estimate=pl.CostEstimate(flops=cost * 1000, bytes_accessed=cost, transcendentals=0),
            name=name,
        )(*inputs)

    hbm = pl.BlockSpec(memory_space=pltpu.MemorySpace.HBM)
    own, start_vec = pl.pallas_call(
        functools.partial(pick_kernel, nblocks),
        in_specs=[smem, hbm, hbm, hbm],
        out_specs=[vmem, smem],
        out_shape=[shape((2 * BLK, width), bf16), shape((1,), jnp.int32)],
        scratch_shapes=[
            pltpu.VMEM(pattern.shape, jnp.int32),
            pltpu.VMEM((tokens, width), bf16),
            pltpu.VMEM((tokens, width), bf16),
            pltpu.SemaphoreType.DMA((3,)),
        ],
        name="pick",
    )(myself.reshape(1), pattern, keys, values)

    if far == 4:
        m0 = swap(own)
        s1 = move(own, lambda i: i ^ 1)
        mid1 = move(own, lambda i: i ^ 3, inner)
        m1 = swap(after(s1, m0))
        mid2 = move(s1, lambda i: i ^ 3, inner)
        end2 = move(mid1, lambda i: i ^ 1, inner)
        s2 = jnp.where(is_inner, mid1, end2)
        m2 = swap(after(s2, m1))
        end3 = move(mid2, lambda i: i ^ 1, inner)
        s3 = jnp.where(is_inner, mid2, end3)
        m3 = swap(after(s3, m2))
        near, mates = [s1, s2, s3], [m0, m1, m2, m3]
    else:
        near = [move(own, lambda i, k=k: i ^ k) for k in range(1, far)]
        mates = [swap(x) for x in [own] + near]
    slots_a = near[:-1] + mates[:half]
    slots_b = near[-1:] + mates[half:]
    cols_a = tokens + len(slots_a) * BLK
    cols_b = len(slots_b) * BLK
    gain_row = gain.reshape(1, width)
    rows_shape = shape((heads, tokens, HEAD_SIZE), f32)
    wide16, wide32 = shape((tokens, width), bf16), shape((tokens, width), f32)

    prob_a, peak_a, total_a = call(
        "first_scores",
        functools.partial(first_scores_kernel, nblocks, far_bias),
        [ranges, pattern, queries, keys, *slots_a],
        [shape((heads, tokens, cols_a), bf16), rows_shape, rows_shape],
        [((cols_a, HEAD_SIZE), bf16)],
        in_smem=(0, 1),
    )
    attended = call(
        "first_attend",
        functools.partial(first_attend_kernel, nblocks),
        [prob_a, values, *slots_a],
        wide32,
        [((cols_a, HEAD_SIZE), bf16)],
    )
    prob_b, scale_a, attended, stats = call(
        "second",
        functools.partial(second_kernel, nblocks, far_bias, len(slots_a)),
        [ranges, pattern, queries, peak_a, total_a, attended, grad_out, gain_row, *slots_b],
        [shape((heads, tokens, cols_b), bf16), rows_shape, wide32, shape((8, tokens), f32)],
        [((cols_b, HEAD_SIZE), bf16)] * 2 + [((tokens, HEAD_SIZE), f32)] * 2,
        in_smem=(0, 1),
    )

    stats = lax.all_gather(stats, "head")

    near_places = [(0, nblocks + k) for k in range(far - 2)] + [(1, 0)]
    mate_places = [(0, nblocks + far - 2 + k) for k in range(half)]
    mate_places += [(1, 1 + k) for k in range(far - half)]
    pair = shape((2 * BLK, width), bf16)

    def cats(n):
        return [((n * BLK, HEAD_SIZE), bf16)] * 2

    normed, d_attended, d_scaled, delta, dq, mate_last = call(
        "grad_out",
        functools.partial(grad_out_kernel, mate_places[-1:]),
        [queries, stats, attended, grad_out, gain_row, scale_a, prob_a, prob_b, mates[-1]],
        [wide16, wide16, wide16, rows_shape, wide32, pair],
        [((tokens, HEAD_SIZE), f32)] * 2 + cats(1),
    )

    def slot_terms(name, places, slots, dq):
        n = len(slots)
        return call(
            name,
            functools.partial(slots_kernel, places),
            [queries, d_attended, d_scaled, delta, scale_a, prob_a, prob_b, dq, *slots],
            [wide32] + [pair] * n,
            cats(n),
        )

    def add(*terms):
        return sum(t.astype(f32) for t in terms).astype(bf16)

    y_last = swap(mate_last)
    if far == 4:
        dq, mate2, mate1, near3, near2 = slot_terms(
            "terms_far",
            [mate_places[2], mate_places[1], near_places[2], near_places[1]],
            [mates[2], mates[1], near[2], near[1]],
            dq,
        )
        y2 = swap(mate2)
        y1 = swap(after(mate1, y_last))
        c3 = add(near3, y_last)
        end3 = move(c3, lambda i: i ^ 1, outer)
        dq, near1, mate0 = slot_terms(
            "terms_near", [near_places[0], mate_places[0]], [near[0], mates[0]], after(dq, c3)
        )
        mid3 = move(add(c3, end3), lambda i: i ^ 3, inner)
        c2 = add(after(near2, near1), y2)
        end2 = move(c2, lambda i: i ^ 1, outer)
        dq = after(dq, y2, end3)
    else:
        dq, mate0, near_last = slot_terms(
            "terms_ends",
            [mate_places[0], near_places[-1]],
            [mates[0], near[-1]],
            dq,
        )
        came = [swap(mate0), move(add(near_last, y_last), lambda i: i ^ (far - 1))]
        for k in range(1, far - 1):
            dq, mate_k, near_k = slot_terms(
                "terms",
                [mate_places[k], near_places[k - 1]],
                [mates[k], near[k - 1]],
                dq,
            )
            came.append(move(add(near_k, swap(mate_k)), lambda i, k=k: i ^ k))

    grad_queries, key_local, value_local, mine = call(
        "terms_local",
        functools.partial(local_kernel, nblocks),
        [start_vec, queries, keys, values, d_attended, d_scaled, delta, scale_a, prob_a, dq],
        [wide16, wide16, wide16, shape((2 * BLK, width), f32)],
        [((tokens, HEAD_SIZE), f32)] * 2,
        in_smem=(0,),
    )
    if far == 4:
        mid2 = move(add(c2, end2), lambda i: i ^ 3, inner)
        c1 = add(after(near1, mine), y1, mid3)
        y0 = swap(after(mate0, y1))
        came = [move(c1, lambda i: i ^ 1), mid2, y0]
    at = 2 + len(came)
    block = pl.BlockSpec((BLK, width), lambda i, place: (place[0], 0))
    grad_keys, grad_values = pl.pallas_call(
        finish_kernel,
        grid_spec=pltpu.PrefetchScalarGridSpec(
            num_scalar_prefetch=1,
            grid=(1,),
            in_specs=[vmem] * (1 + len(came)) + [hbm, hbm],
            out_specs=[block, block],
        ),
        out_shape=[wide16, wide16],
        input_output_aliases={at: 0, at + 1: 1},
        name="finish",
    )(start_vec // BLK, mine, *came, key_local, value_local)
    return normed, grad_queries, grad_keys, grad_values


def solution(mesh):
    split = P("seq", "head")
    return jax.shard_map(
        shards,
        mesh=mesh,
        in_specs=(split, split, split, P("head"), split, P()),
        out_specs=(split, split, split, split),
        check_vma=False,
    )
```

time: 164 us -> 142 us (0.87)
  local copies, waits for them, and re-layouts: 13 us -> 1.9 us
  starting transfers between devices: 40.7 us -> 31.7 us
  other arithmetic: 6.33 us -> 3.27 us
    ppermute x16 -> x10, waiting for transfers between devices: 34.8 us -> 26.9 us  [move(): lax.ppermute(x, 'seq', [(i * 2 + j, to(i) * 2 + j) for i in among for j i...]
    ppermute x11 -> x8, waiting for transfers between devices: 7.89 us -> 15.6 us  [swap(): return lax.ppermute(x, 'seq', [(i, i ^ 1) for i in range(n_seq)])]
    ppermute x16 -> x10, starting transfers between devices: 28.9 us -> 23.3 us  [move(): lax.ppermute(x, 'seq', [(i * 2 + j, to(i) * 2 + j) for i in among for j i...]
    dynamic_update_slice x2 -> x0, local copies, waits for them, and re-layouts: 5.51 us -> none  [the longest x1 2.75 us: shards(): lax.dynamic_update_slice_in_dim(key_local, send_back(key_first[:far - 1],...]
    pallas_call x0 -> x2, Pallas kernels: none -> 5.16 us  [the longest x1 2.6 us: shards(): pl.pallas_call(finish_kernel, grid_spec=pltpu.PrefetchScalarGridSpec(num_...]
    unnamed x47 -> x26, local copies, waits for them, and re-layouts: 6.35 us -> 1.81 us
    pallas_call x7, Pallas kernels: 52.3 us -> 47.9 us  [call(): pl.pallas_call(kernel, in_specs=[smem if i in in_smem else vmem for i in...]
    ppermute x11 -> x8, starting transfers between devices: 11.8 us -> 8.41 us  [swap(): return lax.ppermute(x, 'seq', [(i, i ^ 1) for i in range(n_seq)])]
  transfers between devices with their start and end apart: 27 -> 18, of which waited for: 11 -> 9; matrix products, arithmetic and copies ran while one was open for 6% -> 2% of each run, Pallas kernels for 27% -> 25%
where the time goes in v3:
time: 142 us; the launch traced here: 141 us
  Pallas kernels  53.1 us (37%)
  waiting for transfers between devices  42.5 us (30%)
  starting transfers between devices  31.7 us (22%)
  blocking collectives  5.25 us (4%)
  between operations  3.69 us (3%)
  other arithmetic  3.27 us (2%)
  local copies, waits for them, and re-layouts  1.9 us (1%)
    pallas_call x7, Pallas kernels, call(): pl.pallas_call(kernel, in_specs=[smem if i in in_smem else vmem for i in...  47.9 us
    ppermute x10, waiting for transfers between devices, move(): lax.ppermute(x, 'seq', [(i * 2 + j, to(i) * 2 + j) for i in among for j i...  26.9 us
    ppermute x10, starting transfers between devices, move(): lax.ppermute(x, 'seq', [(i * 2 + j, to(i) * 2 + j) for i in among for j i...  23.3 us
    ppermute x8, waiting for transfers between devices, swap(): return lax.ppermute(x, 'seq', [(i, i ^ 1) for i in range(n_seq)])  15.6 us
    ppermute x8, starting transfers between devices, swap(): return lax.ppermute(x, 'seq', [(i, i ^ 1) for i in range(n_seq)])  8.41 us
    all_gather x1, blocking collectives, shards(): stats = lax.all_gather(stats, 'head')  5.25 us
  transfers between devices with their start and end apart: 18, of which 9 were waited for; matrix products, arithmetic and copies ran while one was open for 2% of the time, Pallas kernels for 25%

profile of v3, /device:TPU:0, one launch (start us, length us, event | category | flops | bytes accessed | tf_op | source)
XLA Modules:
  0.0 141.3 jit_solution(17306941094900544059)
XLA Ops:
  0.7 2.6 %pick.1 = (bf16[256,1024]{1,0:T(8,128)(2,1)}, s32[1]{0:T(128)}) custom-call(s32[1]{0:T(128)} %bitcast.me_ref, s32[10,32]{1,0:T(8,128)} %bitcast.12, bf16[512,1024]{1,0:T(8,128)(2,1)} %k_ref.3, bf16[512,1024]{1,0:T(8,128)(2,1)} %v_ref.3), custom_call_target="tpu_custom_call" | custom-call | tf_op jit(solution)/shard_map/pick/pallas_call | solution.py:377
  4.7 5.1 %collective-permute-start = (bf16[256,1024]{1,0:T(8,128)(2,1)}, bf16[256,1024]{1,0:T(8,128)(2,1)S(1)}, u32[]{:S(2)}, u32[]{:S(2)}) collective-permute-start(bf16[256,1024]{1,0:T(8,128)(2,1)} %get-tuple-element.42), channel_id=1, source_target_pairs={{0,8},{4,12},{8,0},{12,4},{16,24},{20,28},{24,16},{28,20},{1,9},{5... | collective-permute-start | bytes 1572872 | tf_op jit(solution)/shard_map/ppermute | solution.py:340
  9.8 1.5 %collective-permute-start.3 = (bf16[256,1024]{1,0:T(8,128)(2,1)}, bf16[256,1024]{1,0:T(8,128)(2,1)S(1)}, u32[]{:S(2)}, u32[]{:S(2)}) collective-permute-start(bf16[256,1024]{1,0:T(8,128)(2,1)} %get-tuple-element.42), channel_id=1, source_target_pairs={{0,4},{4,0},{8,12},{12,8},{16,20},{20,16},{24,28},{28,24},{1,5},{5... | collective-permute-start | bytes 1572872 | tf_op jit(solution)/shard_map/ppermute | solution.py:343
  12.6 9.0 %collective-permute-done.refs_0_ = bf16[256,1024]{1,0:T(8,128)(2,1)S(1)} collective-permute-done((bf16[256,1024]{1,0:T(8,128)(2,1)}, bf16[256,1024]{1,0:T(8,128)(2,1)S(1)}, u32[]{:S(2)}, u32[]{:S(2)}) %collective-permute-start) | collective-permute-done | bytes 524320 | tf_op jit(solution)/shard_map/ppermute | solution.py:340
  26.2 8.6 %collective-permute-done.2 = bf16[256,1024]{1,0:T(8,128)(2,1)} collective-permute-done((bf16[256,1024]{1,0:T(8,128)(2,1)}, bf16[256,1024]{1,0:T(8,128)(2,1)}, u32[]{:S(2)}, u32[]{:S(2)}) %collective-permute-start.2) | collective-permute-done | bytes 524320 | tf_op jit(solution)/shard_map/ppermute | solution.py:340
  35.9 1.6 %collective-permute-start.7 = (bf16[256,1024]{1,0:T(8,128)(2,1)S(1)}, bf16[256,1024]{1,0:T(8,128)(2,1)S(1)}, u32[]{:S(2)}, u32[]{:S(2)}) collective-permute-start(bf16[256,1024]{1,0:T(8,128)(2,1)S(1)} %broadcast_select_fusion.1.refs_1_.refs_3_), channel_id=1, source_target_pairs={{0,4},{4,0},{8,12},{12,8},{16,20},{20,16},{24,28},{28,24},{1,5},{5... | collective-permute-start | bytes 1572872 | tf_op jit(solution)/shard_map/ppermute | solution.py:343
  38.8 8.2 %first_scores.1 = (bf16[8,512,1024]{2,1,0:T(8,128)(2,1)S(1)}, f32[8,512,128]{2,1,0:T(8,128)S(1)}, f32[8,512,128]{2,1,0:T(8,128)S(1)}) custom-call(s32[8]{0:T(128)S(1)} %stack.35.ranges_ref, s32[10,32]{1,0:T(8,128)S(1)} %bitcast.13, bf16[512,1024]{1,0:T(8,128)(2,1)S(1)} %copy-done.8, bf16[512,1024]{1,0:T(8,128)(2,1)S(1)} %copy-done.1, ...), custom_call_target="tpu_custom_call" | custom-call | flops 99999997952 | bytes 100000000 | tf_op jit(solution)/shard_map/first_scores/pallas_call | solution.py:365
  47.0 4.6 %collective-permute-done.6 = bf16[256,1024]{1,0:T(8,128)(2,1)S(1)} collective-permute-done((bf16[256,1024]{1,0:T(8,128)(2,1)}, bf16[256,1024]{1,0:T(8,128)(2,1)S(1)}, u32[]{:S(2)}, u32[]{:S(2)}) %collective-permute-start.6) | collective-permute-done | bytes 524320 | tf_op jit(solution)/shard_map/ppermute | solution.py:340
  52.3 5.0 %first_attend.1.o_in = f32[512,1024]{1,0:T(8,128)S(1)} custom-call(bf16[8,512,1024]{2,1,0:T(8,128)(2,1)S(1)} %get-tuple-element.46.p_ref.pa_ref, bf16[512,1024]{1,0:T(8,128)(2,1)S(1)} %copy-done.2, bf16[256,1024]{1,0:T(8,128)(2,1)S(1)} %collective-permute-done.refs_0_, bf16[256,1024]{1,0:T(8,128)(2,1)S(1)} %broadcast_select_fusion.1.refs_1_.refs_3_, ...), custom_call_target="tpu_custom_call" | custom-call | flops 99999997952 | bytes 100000000 | tf_op jit(solution)/shard_map/first_attend/pallas_call | solution.py:365
  57.3 5.4 %collective-permute-done.8.refs_2_.refs_0_ = bf16[256,1024]{1,0:T(8,128)(2,1)S(1)} collective-permute-done((bf16[256,1024]{1,0:T(8,128)(2,1)S(1)}, bf16[256,1024]{1,0:T(8,128)(2,1)S(1)}, u32[]{:S(2)}, u32[]{:S(2)}) %collective-permute-start.8) | collective-permute-done | bytes 524320 | tf_op jit(solution)/shard_map/ppermute | solution.py:343
  62.7 7.1 %second.1 = (bf16[8,512,384]{2,1,0:T(8,128)(2,1)S(1)}, f32[8,512,128]{2,1,0:T(8,128)S(1)}, f32[512,1024]{1,0:T(8,128)S(1)}, f32[8,512]{1,0:T(8,128)S(1)}) custom-call(s32[8]{0:T(128)S(1)} %stack.35.ranges_ref, s32[10,32]{1,0:T(8,128)S(1)} %bitcast.14, bf16[512,1024]{1,0:T(8,128)(2,1)S(1)} %copy-done.8, f32[8,512,128]{2,1,0:T(8,128)S(1)} %get-tuple-element.44.peak_ref, ...), custom_call_target="tpu_custom_call" | custom-call | flops 99999997952 | bytes 100000000 | tf_op jit(solution)/shard_map/second/pallas_call | solution.py:365
  69.8 5.2 %all-gather = f32[32,512]{1,0:T(8,128)S(1)} all-gather(f32[8,512]{1,0:T(8,128)S(1)} %get-tuple-element.49), channel_id=2, replica_groups=mesh['seq'=8,'head'=4] {'head'}, dimensions={0}, use_global_device_ids=true | all-gather | bytes 81920 | tf_op jit(solution)/shard_map/all_gather | solution.py:439
  75.1 5.0 %grad_out.1 = (bf16[512,1024]{1,0:T(8,128)(2,1)}, bf16[512,1024]{1,0:T(8,128)(2,1)S(1)}, bf16[512,1024]{1,0:T(8,128)(2,1)S(1)}, f32[8,512,128]{2,1,0:T(8,128)S(1...) custom-call(bf16[512,1024]{1,0:T(8,128)(2,1)S(1)} %copy-done.8, f32[4,8,512]{2,1,0:T(8,128)S(1)} %bitcast.11, ...), custom_call_target="tpu_custom_call" | custom-call | flops 99999997952 | bytes 100000000 | tf_op jit(solution)/shard_map/grad_out/pallas_call | solution.py:365
  80.7 8.6 %terms_far.1 = (f32[512,1024]{1,0:T(8,128)S(1)}, bf16[256,1024]{1,0:T(8,128)(2,1)S(1)}, bf16[256,1024]{1,0:T(8,128)(2,1)}, bf16[256,1024]{1,0:T(8,128)(2,1)S(1)}, bf16[256,1024]{1,0:T(8,128)(2,1)S(1)}) custom-call(bf16[512,1024]{1,0:T(8,128)(2,1)S(1)} %copy-done.8, bf16[512,1024]{1,0:T(8,128)(2,1)S(1)} %get-tuple-element.55.d_ref, ...), custom_call_target="tpu_custom_call" | custom-call | flops 99999997952 | bytes 100000000 | tf_op jit(solution)/shard_map/terms_far/pallas_call | solution.py:365
  90.7 4.2 %collective-permute-done.9 = bf16[256,1024]{1,0:T(8,128)(2,1)S(1)} collective-permute-done((bf16[256,1024]{1,0:T(8,128)(2,1)S(1)}, bf16[256,1024]{1,0:T(8,128)(2,1)S(1)}, u32[]{:S(2)}, u32[]{:S(2)}) %collective-permute-start.9) | collective-permute-done | bytes 524320 | tf_op jit(solution)/shard_map/ppermute | solution.py:343
  95.1 2.6 %collective-permute-start.11 = (bf16[256,1024]{1,0:T(8,128)(2,1)S(1)}, bf16[256,1024]{1,0:T(8,128)(2,1)S(1)}, u32[]{:S(2)}, u32[]{:S(2)}) collective-permute-start(bf16[256,1024]{1,0:T(8,128)(2,1)S(1)} %add_convert_fusion.4), channel_id=1, source_target_pairs={{0,8},{4,12},{24,16},{28,20},{1,9},{5,13},{25,17},{29,21},{2,10},{... | collective-permute-start | bytes 1572872 | tf_op jit(solution)/shard_map/ppermute | solution.py:340
  98.3 5.1 %terms_near.1 = (f32[512,1024]{1,0:T(8,128)S(1)}, bf16[256,1024]{1,0:T(8,128)(2,1)S(1)}, bf16[256,1024]{1,0:T(8,128)(2,1)S(1)}) custom-call(bf16[512,1024]{1,0:T(8,128)(2,1)S(1)} %copy-done.8, bf16[512,1024]{1,0:T(8,128)(2,1)S(1)} %get-tuple-element.55.d_ref, bf16[512,1024]{1,0:T(8,128)(2,1)S(1)} %get-tuple-element.56.scaled_d_ref, ...), custom_call_target="tpu_custom_call" | custom-call | flops 99999997952 | bytes 100000000 | tf_op jit(solution)/shard_map/terms_near/pallas_call | solution.py:365
  103.4 2.7 %collective-permute-done.10 = bf16[256,1024]{1,0:T(8,128)(2,1)S(1)} collective-permute-done((bf16[256,1024]{1,0:T(8,128)(2,1)S(1)}, bf16[256,1024]{1,0:T(8,128)(2,1)S(1)}, u32[]{:S(2)}, u32[]{:S(2)}) %collective-permute-start.10) | collective-permute-done | bytes 524320 | tf_op jit(solution)/shard_map/ppermute | solution.py:343
  106.3 2.6 %collective-permute-start.15 = (bf16[256,1024]{1,0:T(8,128)(2,1)S(1)}, bf16[256,1024]{1,0:T(8,128)(2,1)S(1)}, u32[]{:S(2)}, u32[]{:S(2)}) collective-permute-start(bf16[256,1024]{1,0:T(8,128)(2,1)S(1)} %add_convert_fusion.1), channel_id=1, source_target_pairs={{0,8},{4,12},{24,16},{28,20},{1,9},{5,13},{25,17},{29,21},{2,10},{... | collective-permute-start | bytes 1572872 | tf_op jit(solution)/shard_map/ppermute | solution.py:340
  109.9 8.9 %terms_local.1 = (bf16[512,1024]{1,0:T(8,128)(2,1)}, bf16[512,1024]{1,0:T(8,128)(2,1)}, bf16[512,1024]{1,0:T(8,128)(2,1)}, f32[256,1024]{1,0:T(8,128)S(1)}) custom-call(s32[1]{0:T(128)} %get-tuple-element.54.start_ref, bf16[512,1024]{1,0:T(8,128)(2,1)S(1)} %copy-done.8, bf16[512,1024]{1,0:T(8,128)(2,1)S(1)} %copy-done.1, bf16[512,1024]{1,0:T(8,128)(2,1)S(1)} %copy-done.3, ...), custom_call_target="tpu_custom_call" | custom-call | flops 99999997952 | bytes 100000000 | tf_op jit(solution)/shard_map/terms_local/pallas_call | solution.py:365
  122.5 6.0 %collective-permute-start.14 = (bf16[256,1024]{1,0:T(8,128)(2,1)S(1)}, bf16[256,1024]{1,0:T(8,128)(2,1)S(1)}, u32[]{:S(2)}, u32[]{:S(2)}) collective-permute-start(bf16[256,1024]{1,0:T(8,128)(2,1)S(1)} %add_convert_fusion.2), channel_id=1, source_target_pairs={{0,8},{4,12},{8,0},{12,4},{16,24},{20,28},{24,16},{28,20},{1,9},{5... | collective-permute-start | bytes 1572872 | tf_op jit(solution)/shard_map/ppermute | solution.py:340
  131.4 1.9 %collective-permute-done.17.refs_2_ = bf16[256,1024]{1,0:T(8,128)(2,1)S(1)} collective-permute-done((bf16[256,1024]{1,0:T(8,128)(2,1)S(1)}, bf16[256,1024]{1,0:T(8,128)(2,1)S(1)}, u32[]{:S(2)}, u32[]{:S(2)}) %collective-permute-start.17) | collective-permute-done | bytes 524320 | tf_op jit(solution)/shard_map/ppermute | solution.py:343
  133.2 4.7 %collective-permute-done.14.refs_0_ = bf16[256,1024]{1,0:T(8,128)(2,1)S(1)} collective-permute-done((bf16[256,1024]{1,0:T(8,128)(2,1)S(1)}, bf16[256,1024]{1,0:T(8,128)(2,1)S(1)}, u32[]{:S(2)}, u32[]{:S(2)}) %collective-permute-start.14) | collective-permute-done | bytes 524320 | tf_op jit(solution)/shard_map/ppermute | solution.py:340
  138.7 2.6 %finish.1 = (bf16[512,1024]{1,0:T(8,128)(2,1)}, bf16[512,1024]{1,0:T(8,128)(2,1)}) custom-call(s32[1]{0:T(128)S(6)} %select_n.41.start_ref, f32[256,1024]{1,0:T(8,128)} %copy-done, bf16[256,1024]{1,0:T(8,128)(2,1)} %copy-done.12, bf16[256,1024]{1,0:T(8,128)(2,1)} %copy-done.10, ...), custom_call_target="tpu_custom_call", output_to_operand_aliasing={{0}: (5, {}), {1}: (6, {})} | custom-call | tf_op jit(solution)/shard_map/finish/pallas_call | solution.py:521
  (56 shorter events, 18.8 us)
Async XLA Ops:
  0.6 38.2 %copy-start.6 = (s32[32,10]{0,1:T(8,128)S(1)}, s32[32,10]{0,1:T(8,128)}, u32[]{:S(2)}) copy-start(s32[32,10]{0,1:T(8,128)} %param.11) | copy-start | bytes 3844
  0.6 38.2 %copy-start.1 = (bf16[512,1024]{1,0:T(8,128)(2,1)S(1)}, bf16[512,1024]{1,0:T(8,128)(2,1)}, u32[]{:S(2)}) copy-start(bf16[512,1024]{1,0:T(8,128)(2,1)} %k_ref.3) | copy-start | bytes 3145732
  0.7 38.2 %copy-start.8 = (bf16[512,1024]{1,0:T(8,128)(2,1)S(1)}, bf16[512,1024]{1,0:T(8,128)(2,1)}, u32[]{:S(2)}) copy-start(bf16[512,1024]{1,0:T(8,128)(2,1)} %q_ref.11) | copy-start | bytes 3145732
  3.2 8.1 %collective-permute-start.1 = (bf16[256,1024]{1,0:T(8,128)(2,1)}, bf16[256,1024]{1,0:T(8,128)(2,1)}, u32[]{:S(2)}, u32[]{:S(2)}) collective-permute-start(bf16[256,1024]{1,0:T(8,128)(2,1)} %get-tuple-element.42), channel_id=1, source_target_pairs={{8,16},{12,20},{16,8},{20,12},{9,17},{13,21},{17,9},{21,13},{10,18... | collective-permute-start | bytes 1572872 | tf_op jit(solution)/shard_map/ppermute | solution.py:340
  4.7 17.0 %collective-permute-start = (bf16[256,1024]{1,0:T(8,128)(2,1)}, bf16[256,1024]{1,0:T(8,128)(2,1)S(1)}, u32[]{:S(2)}, u32[]{:S(2)}) collective-permute-start(bf16[256,1024]{1,0:T(8,128)(2,1)} %get-tuple-element.42), channel_id=1, source_target_pairs={{0,8},{4,12},{8,0},{12,4},{16,24},{20,28},{24,16},{28,20},{1,9},{5... | collective-permute-start | bytes 1572872 | tf_op jit(solution)/shard_map/ppermute | solution.py:340
  9.8 13.3 %collective-permute-start.3 = (bf16[256,1024]{1,0:T(8,128)(2,1)}, bf16[256,1024]{1,0:T(8,128)(2,1)S(1)}, u32[]{:S(2)}, u32[]{:S(2)}) collective-permute-start(bf16[256,1024]{1,0:T(8,128)(2,1)} %get-tuple-element.42), channel_id=1, source_target_pairs={{0,4},{4,0},{8,12},{12,8},{16,20},{20,16},{24,28},{28,24},{1,5},{5... | collective-permute-start | bytes 1572872 | tf_op jit(solution)/shard_map/ppermute | solution.py:343
  11.3 23.4 %collective-permute-start.2 = (bf16[256,1024]{1,0:T(8,128)(2,1)}, bf16[256,1024]{1,0:T(8,128)(2,1)}, u32[]{:S(2)}, u32[]{:S(2)}) collective-permute-start(bf16[256,1024]{1,0:T(8,128)(2,1)} %collective-permute-done.1), channel_id=1, source_target_pairs={{8,0},{12,4},{16,24},{20,28},{9,1},{13,5},{17,25},{21,29},{10,2},{... | collective-permute-start | bytes 1572872 | tf_op jit(solution)/shard_map/ppermute | solution.py:340
  23.1 12.8 %collective-permute-start.4 = (bf16[256,1024]{1,0:T(8,128)(2,1)S(1)}, bf16[256,1024]{1,0:T(8,128)(2,1)}, u32[]{:S(2)}, u32[]{:S(2)}) collective-permute-start(bf16[256,1024]{1,0:T(8,128)(2,1)S(1)} %collective-permute-done.refs_0_), channel_id=1, source_target_pairs={{0,4},{4,0},{8,12},{12,8},{16,20},{20,16},{24,28},{28,24},{1,5},{5... | collective-permute-start | bytes 1572872 | tf_op jit(solution)/shard_map/ppermute | solution.py:343
  24.7 12.8 %collective-permute-start.5 = (bf16[256,1024]{1,0:T(8,128)(2,1)S(1)}, bf16[256,1024]{1,0:T(8,128)(2,1)}, u32[]{:S(2)}, u32[]{:S(2)}) collective-permute-start(bf16[256,1024]{1,0:T(8,128)(2,1)S(1)} %collective-permute-done.refs_0_), channel_id=1, source_target_pairs={{8,16},{12,20},{16,8},{20,12},{9,17},{13,21},{17,9},{21,13},{10,18... | collective-permute-start | bytes 1572872 | tf_op jit(solution)/shard_map/ppermute | solution.py:340
  35.9 16.4 %copy-start.4 = (bf16[256,1024]{1,0:T(8,128)(2,1)}, bf16[256,1024]{1,0:T(8,128)(2,1)S(1)}, u32[]{:S(2)}) copy-start(bf16[256,1024]{1,0:T(8,128)(2,1)S(1)} %broadcast_select_fusion.1.refs_1_.refs_3_) | copy-start | bytes 1572868
  35.9 16.4 %copy-start.2 = (bf16[512,1024]{1,0:T(8,128)(2,1)S(1)}, bf16[512,1024]{1,0:T(8,128)(2,1)}, u32[]{:S(2)}) copy-start(bf16[512,1024]{1,0:T(8,128)(2,1)} %v_ref.3) | copy-start | bytes 3145732
  35.9 15.8 %collective-permute-start.7 = (bf16[256,1024]{1,0:T(8,128)(2,1)S(1)}, bf16[256,1024]{1,0:T(8,128)(2,1)S(1)}, u32[]{:S(2)}, u32[]{:S(2)}) collective-permute-start(bf16[256,1024]{1,0:T(8,128)(2,1)S(1)} %broadcast_select_fusion.1.refs_1_.refs_3_), channel_id=1, source_target_pairs={{0,4},{4,0},{8,12},{12,8},{16,20},{20,16},{24,28},{28,24},{1,5},{5... | collective-permute-start | bytes 1572872 | tf_op jit(solution)/shard_map/ppermute | solution.py:343
  37.5 14.1 %collective-permute-start.6 = (bf16[256,1024]{1,0:T(8,128)(2,1)}, bf16[256,1024]{1,0:T(8,128)(2,1)S(1)}, u32[]{:S(2)}, u32[]{:S(2)}) collective-permute-start(bf16[256,1024]{1,0:T(8,128)(2,1)} %collective-permute-done.5), channel_id=1, source_target_pairs={{8,0},{12,4},{16,24},{20,28},{9,1},{13,5},{17,25},{21,29},{10,2},{... | collective-permute-start | bytes 1572872 | tf_op jit(solution)/shard_map/ppermute | solution.py:340
  51.7 11.0 %collective-permute-start.8 = (bf16[256,1024]{1,0:T(8,128)(2,1)S(1)}, bf16[256,1024]{1,0:T(8,128)(2,1)S(1)}, u32[]{:S(2)}, u32[]{:S(2)}) collective-permute-start(bf16[256,1024]{1,0:T(8,128)(2,1)S(1)} %broadcast_select_fusion.refs_0_.refs_2_), channel_id=1, source_target_pairs={{0,4},{4,0},{8,12},{12,8},{16,20},{20,16},{24,28},{28,24},{1,5},{5... | collective-permute-start | bytes 1572872 | tf_op jit(solution)/shard_map/ppermute | solution.py:343
  52.3 10.4 %copy-start.9 = (f32[1024]{0:T(1024)S(1)}, f32[1024]{0:T(1024)}, u32[]{:S(2)}) copy-start(f32[1024]{0:T(1024)} %param.9) | copy-start | bytes 12292
  80.1 14.7 %collective-permute-start.9 = (bf16[256,1024]{1,0:T(8,128)(2,1)S(1)}, bf16[256,1024]{1,0:T(8,128)(2,1)S(1)}, u32[]{:S(2)}, u32[]{:S(2)}) collective-permute-start(bf16[256,1024]{1,0:T(8,128)(2,1)S(1)} %get-tuple-element.61), channel_id=1, source_target_pairs={{0,4},{4,0},{8,12},{12,8},{16,20},{20,16},{24,28},{28,24},{1,5},{5... | collective-permute-start | bytes 1572872 | tf_op jit(solution)/shard_map/ppermute | solution.py:343
  89.2 16.9 %collective-permute-start.10 = (bf16[256,1024]{1,0:T(8,128)(2,1)S(1)}, bf16[256,1024]{1,0:T(8,128)(2,1)S(1)}, u32[]{:S(2)}, u32[]{:S(2)}) collective-permute-start(bf16[256,1024]{1,0:T(8,128)(2,1)S(1)} %get-tuple-element.64), channel_id=1, source_target_pairs={{0,4},{4,0},{8,12},{12,8},{16,20},{20,16},{24,28},{28,24},{1,5},{5... | collective-permute-start | bytes 1572872 | tf_op jit(solution)/shard_map/ppermute | solution.py:343
  95.1 13.9 %collective-permute-start.11 = (bf16[256,1024]{1,0:T(8,128)(2,1)S(1)}, bf16[256,1024]{1,0:T(8,128)(2,1)S(1)}, u32[]{:S(2)}, u32[]{:S(2)}) collective-permute-start(bf16[256,1024]{1,0:T(8,128)(2,1)S(1)} %add_convert_fusion.4), channel_id=1, source_target_pairs={{0,8},{4,12},{24,16},{28,20},{1,9},{5,13},{25,17},{29,21},{2,10},{... | collective-permute-start | bytes 1572872 | tf_op jit(solution)/shard_map/ppermute | solution.py:340
  97.7 22.9 %collective-permute-start.12 = (bf16[256,1024]{1,0:T(8,128)(2,1)}, bf16[256,1024]{1,0:T(8,128)(2,1)}, u32[]{:S(2)}, u32[]{:S(2)}) collective-permute-start(bf16[256,1024]{1,0:T(8,128)(2,1)} %get-tuple-element.71), channel_id=1, source_target_pairs={{0,4},{4,0},{8,12},{12,8},{16,20},{20,16},{24,28},{28,24},{1,5},{5... | collective-permute-start | bytes 1572872 | tf_op jit(solution)/shard_map/ppermute | solution.py:343
  106.3 13.4 %collective-permute-start.15 = (bf16[256,1024]{1,0:T(8,128)(2,1)S(1)}, bf16[256,1024]{1,0:T(8,128)(2,1)S(1)}, u32[]{:S(2)}, u32[]{:S(2)}) collective-permute-start(bf16[256,1024]{1,0:T(8,128)(2,1)S(1)} %add_convert_fusion.1), channel_id=1, source_target_pairs={{0,8},{4,12},{24,16},{28,20},{1,9},{5,13},{25,17},{29,21},{2,10},{... | collective-permute-start | bytes 1572872 | tf_op jit(solution)/shard_map/ppermute | solution.py:340
  109.2 12.1 %collective-permute-start.13 = (bf16[256,1024]{1,0:T(8,128)(2,1)S(1)}, bf16[256,1024]{1,0:T(8,128)(2,1)S(1)}, u32[]{:S(2)}, u32[]{:S(2)}) collective-permute-start(bf16[256,1024]{1,0:T(8,128)(2,1)S(1)} %add_convert_fusion.3), channel_id=1, source_target_pairs={{8,16},{12,20},{16,8},{20,12},{9,17},{13,21},{17,9},{21,13},{10,18... | collective-permute-start | bytes 1572872 | tf_op jit(solution)/shard_map/ppermute | solution.py:340
  119.9 11.4 %collective-permute-start.16 = (bf16[256,1024]{1,0:T(8,128)(2,1)S(1)}, bf16[256,1024]{1,0:T(8,128)(2,1)S(1)}, u32[]{:S(2)}, u32[]{:S(2)}) collective-permute-start(bf16[256,1024]{1,0:T(8,128)(2,1)S(1)} %add_convert_fusion), channel_id=1, source_target_pairs={{8,16},{12,20},{16,8},{20,12},{9,17},{13,21},{17,9},{21,13},{10,18... | collective-permute-start | bytes 1572872 | tf_op jit(solution)/shard_map/ppermute | solution.py:340
  120.6 12.6 %collective-permute-start.17 = (bf16[256,1024]{1,0:T(8,128)(2,1)S(1)}, bf16[256,1024]{1,0:T(8,128)(2,1)S(1)}, u32[]{:S(2)}, u32[]{:S(2)}) collective-permute-start(bf16[256,1024]{1,0:T(8,128)(2,1)S(1)} %get-tuple-element.75), channel_id=1, source_target_pairs={{0,4},{4,0},{8,12},{12,8},{16,20},{20,16},{24,28},{28,24},{1,5},{5... | collective-permute-start | bytes 1572872 | tf_op jit(solution)/shard_map/ppermute | solution.py:343
  122.5 15.4 %collective-permute-start.14 = (bf16[256,1024]{1,0:T(8,128)(2,1)S(1)}, bf16[256,1024]{1,0:T(8,128)(2,1)S(1)}, u32[]{:S(2)}, u32[]{:S(2)}) collective-permute-start(bf16[256,1024]{1,0:T(8,128)(2,1)S(1)} %add_convert_fusion.2), channel_id=1, source_target_pairs={{0,8},{4,12},{8,0},{12,4},{16,24},{20,28},{24,16},{28,20},{1,9},{5... | collective-permute-start | bytes 1572872 | tf_op jit(solution)/shard_map/ppermute | solution.py:340
  (7 other events, 35.5 us)

commit v4 on v3

--- a/solution.py
+++ b/solution.py
@@ -102,7 +102,7 @@
         for g in range(nblocks)
     ]
 
-    @pl.loop(0, p_ref.shape[0])
+    @pl.loop(0, p_ref.shape[0], unroll=4)
     def _(h):
         cols = head_columns(h)
         gather_rows(cat_ref, [(k_ref, blocks(0, nblocks))] + keys_of(slots), cols)
@@ -122,119 +122,163 @@
     slots = refs[:-2]
     o_ref, cat_ref = refs[-2:]
 
-    @pl.loop(0, p_ref.shape[0])
+    @pl.loop(0, p_ref.shape[0], unroll=4)
     def _(h):
         cols = head_columns(h)
         gather_rows(cat_ref, [(v_ref, blocks(0, nblocks))] + values_of(slots), cols)
         o_ref[:, cols] = dot(p_ref[h], cat_ref[...], NN)
 
 
-def second_kernel(
+def later_biases(nblocks, far_bias, at, count, ranges_ref, pattern_ref):
+    if not far_bias:
+        return None
+    listed = functools.partial(is_listed, nblocks, ranges_ref, pattern_ref)
+    return [[listed(g, place=at + j) for j in range(count)] for g in range(nblocks)]
+
+
+def later_scores(q, keys, biases):
+    scores = dot(q, keys, NT) * softmax_scale
+    if biases is None:
+        return scores
+    parts = [biased(scores[blocks(g)], biases[g]) for g in range(len(biases))]
+    return jnp.concatenate(parts, axis=0)
+
+
+def wide(x, like):
+    return x if like.shape == x.shape else jnp.concatenate([x] * (like.shape[1] // BLK), axis=1)
+
+
+def second_kernel(nblocks, far_bias, at, ranges_ref, pattern_ref, q_ref, peak_in, total_in, o_in, *refs):
+    slots = refs[:-7]
+    p_ref, shrink_ref, peak_ref, total_ref, o_ref, key_cat, value_cat = refs[-7:]
+    biases = later_biases(nblocks, far_bias, at, len(slots), ranges_ref, pattern_ref)
+
+    @pl.loop(0, p_ref.shape[0], unroll=4)
+    def _(h):
+        cols = head_columns(h)
+        gather_rows(key_cat, keys_of(slots), cols)
+        gather_rows(value_cat, values_of(slots), cols)
+        scores = later_scores(q_ref[:, cols], key_cat[...], biases)
+        old = peak_in[h]
+        peak = jnp.maximum(old, jnp.max(scores, axis=1, keepdims=True))
+        shrink = jnp.exp(old - peak)
+        expo = jnp.exp(scores - wide(peak, scores))
+        expo16 = expo.astype(p_ref.dtype)
+        p_ref[h] = expo16
+        shrink_ref[h] = shrink
+        peak_ref[h] = peak
+        total_ref[h] = total_in[h] * shrink + jnp.sum(expo, axis=1, keepdims=True)
+        o_ref[:, cols] = o_in[:, cols] * shrink + dot(expo16, value_cat[...], NN)
+
+
+def third_kernel(
     nblocks,
     far_bias,
-    n_first,
+    at,
     ranges_ref,
     pattern_ref,
     q_ref,
     peak_ref,
     total_ref,
+    shrink_ref,
     o_in,
     grad_ref,
     gain_ref,
-    *refs,
+    slot_ref,
+    p_ref,
+    scale_a_ref,
+    scale_b_ref,
+    o_ref,
+    stat_ref,
+    square_ref,
+    cross_ref,
 ):
-    slots = refs[:-8]
-    p_ref, scale_ref, o_ref, stat_ref, key_cat, value_cat, square_ref, cross_ref = refs[-8:]
-    listed = functools.partial(is_listed, nblocks, ranges_ref, pattern_ref)
-    biases = [
-        [listed(g, place=1 + n_first + j) if far_bias else None for j in range(len(slots))]
-        for g in range(nblocks)
-    ]
+    biases = later_biases(nblocks, far_bias, at, 1, ranges_ref, pattern_ref)
     square_ref[...] = jnp.zeros_like(square_ref)
     cross_ref[...] = jnp.zeros_like(cross_ref)
 
-    @pl.loop(0, p_ref.shape[0])
+    @pl.loop(0, p_ref.shape[0], unroll=True)
     def _(h):
         cols = head_columns(h)
-        gather_rows(key_cat, keys_of(slots), cols)
-        gather_rows(value_cat, values_of(slots), cols)
-        scores = dot(q_ref[:, cols], key_cat[...], NT) * softmax_scale
-        if far_bias:
-            parts = [biased(scores[blocks(g)], biases[g]) for g in range(nblocks)]
-            scores = jnp.concatenate(parts, axis=0)
+        scores = later_scores(q_ref[:, cols], slot_ref[blocks(0), cols], biases)
         old = peak_ref[h]
         peak = jnp.maximum(old, jnp.max(scores, axis=1, keepdims=True))
         shrink = jnp.exp(old - peak)
-        expo = jnp.exp(scores - jnp.concatenate([peak] * len(slots), axis=1))
+        expo = jnp.exp(scores - peak)
         total = total_ref[h] * shrink + jnp.sum(expo, axis=1, keepdims=True)
         inverse = 1.0 / total
-        prob = (expo * jnp.concatenate([inverse] * len(slots), axis=1)).astype(p_ref.dtype)
+        prob = (expo * inverse).astype(p_ref.dtype)
         p_ref[h] = prob
         scale = shrink * inverse
-        scale_ref[h] = scale
-        out = o_in[:, cols] * scale + dot(prob, value_cat[...], NN)
+        scale_b_ref[h] = scale
+        scale_a_ref[h] = scale * shrink_ref[h]
+        out = o_in[:, cols] * scale + dot(prob, slot_ref[blocks(1), cols], NN)
         o_ref[:, cols] = out
         scaled = grad_ref[:, cols].astype(jnp.float32) * gain_ref[:, cols]
         square_ref[...] += out * out
         cross_ref[...] += scaled * out
 
-    stat_ref[0:1] = jnp.sum(square_ref[...].T, axis=0, keepdims=True)
-    stat_ref[1:2] = jnp.sum(cross_ref[...].T, axis=0, keepdims=True)
-    stat_ref[2:] = jnp.zeros_like(stat_ref[2:])
-
-
-def score_grad(d, delta, scale, value_cat, parts):
+    squares = jnp.sum(square_ref[...].T, axis=0, keepdims=True)
+    cross = jnp.sum(cross_ref[...].T, axis=0, keepdims=True)
+    for g in range(nblocks):
+        stat_ref[g : g + 1] = squares[:, blocks(g)]
+        stat_ref[nblocks + g : nblocks + g + 1] = cross[:, blocks(g)]
+
+
+def score_grad(d, delta, scales, value_cat, parts):
     dprob = dot(d, value_cat, NT)
     result = []
-    for j, (prob, takes) in enumerate(parts):
-        part = prob.astype(jnp.float32) * (dprob[:, blocks(j)] - delta)
-        result.append((part * scale if takes else part).astype(jnp.bfloat16))
+    for j, (prob, part) in enumerate(parts):
+        term = prob.astype(jnp.float32) * (dprob[:, blocks(j)] - delta)
+        term = term if scales[part] is None else term * scales[part]
+        result.append(term.astype(jnp.bfloat16))
     return jnp.concatenate(result, axis=1)
 
 
-def put_slots(slots, prob_parts, d, d_scaled, dscore, q, cols):
-    for j, (slot, (prob, takes)) in enumerate(zip(slots, prob_parts)):
+def put_slots(slots, prob_parts, d_parts, dscore, q, cols):
+    for j, (slot, (prob, part)) in enumerate(zip(slots, prob_parts)):
         key_term = dot(dscore[:, blocks(j)], q, TN) * softmax_scale
         slot[:BLK, cols] = key_term.astype(slot.dtype)
-        slot[BLK:, cols] = dot(prob, d_scaled if takes else d, TN).astype(slot.dtype)
-
-
-def take(places, pa_ref, pb_ref, h):
-    return [
-        (pb_ref[h, :, blocks(j)], False) if part else (pa_ref[h, :, blocks(j)], True)
-        for part, j in places
-    ]
+        slot[BLK:, cols] = dot(prob, d_parts[part], TN).astype(slot.dtype)
+
+
+def take(places, p_refs, h):
+    return [(p_refs[part][h, :, blocks(j)], part) for part, j in places]
 
 
 def grad_out_kernel(
-    places,
+    place,
     q_ref,
     stat_ref,
     o_ref,
     grad_ref,
     gain_ref,
-    scale_ref,
-    pa_ref,
-    pb_ref,
-    *refs,
+    scale_a_ref,
+    scale_b_ref,
+    p_ref,
+    slot_ref,
+    normed_ref,
+    d_ref,
+    d_a_ref,
+    d_b_ref,
+    delta_ref,
+    dq_ref,
+    out_ref,
+    inverse_ref,
+    factor_ref,
 ):
-    n = len(places)
-    normed_ref, d_ref, scaled_d_ref, delta_ref, dq_ref = refs[n : n + 5]
-    outs = refs[n + 5 : 2 * n + 5]
-    inverse_ref, factor_ref, key_cat, value_cat = refs[2 * n + 5 :]
     tokens = o_ref.shape[0]
     stats = jnp.sum(stat_ref[...], axis=0)
-    squares = jnp.broadcast_to(stats[0:1], (HEAD_SIZE, tokens)).T
-    cross = jnp.broadcast_to(stats[1:2], (HEAD_SIZE, tokens)).T
+    rows = [jnp.broadcast_to(stats[g : g + 1], (HEAD_SIZE, BLK)).T for g in range(stats.shape[0])]
+    squares = jnp.concatenate(rows[: tokens // BLK], axis=0)
+    cross = jnp.concatenate(rows[tokens // BLK :], axis=0)
     inverse = lax.rsqrt(squares / FEAT + epsilon)
     inverse_ref[...] = inverse
     factor_ref[...] = inverse * inverse * inverse * cross / FEAT
 
-    @pl.loop(0, pa_ref.shape[0])
+    @pl.loop(0, p_ref.shape[0], unroll=True)
     def _(h):
         cols = head_columns(h)
-        gather_rows(key_cat, keys_of(refs[:n]), cols)
-        gather_rows(value_cat, values_of(refs[:n]), cols)
         out = o_ref[:, cols]
         inverse = inverse_ref[...]
         gain = gain_ref[:, cols]
@@ -242,34 +286,36 @@
         normed_ref[:, cols] = (out * inverse * gain).astype(normed_ref.dtype)
         d_attended = inverse * scaled - out * factor_ref[...]
         d = d_attended.astype(d_ref.dtype)
-        d_scaled = (d_attended * scale_ref[h]).astype(d_ref.dtype)
         d_ref[:, cols] = d
-        scaled_d_ref[:, cols] = d_scaled
+        d_a_ref[:, cols] = (d_attended * scale_a_ref[h]).astype(d_ref.dtype)
+        d_b_ref[:, cols] = (d_attended * scale_b_ref[h]).astype(d_ref.dtype)
         delta = jnp.sum(d.astype(jnp.float32) * out, axis=1, keepdims=True)
         delta = jnp.broadcast_to(delta, out.shape)
         delta_ref[h] = delta
-        parts = take(places, pa_ref, pb_ref, h)
-        dscore = score_grad(d, delta, scale_ref[h], value_cat[...], parts)
-        dq_ref[:, cols] = dot(dscore, key_cat[...], NN)
-        put_slots(outs, parts, d, d_scaled, dscore, q_ref[:, cols], cols)
-
-
-def slots_kernel(places, q_ref, d_ref, scaled_d_ref, delta_ref, scale_ref, pa_ref, pb_ref, dq_in, *refs):
+        parts = take([place], (None, None, p_ref), h)
+        dscore = score_grad(d, delta, (None, None, None), slot_ref[blocks(1), cols], parts)
+        dq_ref[:, cols] = dot(dscore, slot_ref[blocks(0), cols], NN)
+        put_slots([out_ref], parts, (None, None, d), dscore, q_ref[:, cols], cols)
+
+
+def slots_kernel(
+    places, q_ref, d_ref, d_a_ref, d_b_ref, delta_ref, scale_a_ref, scale_b_ref, pa_ref, pb_ref, dq_in, *refs
+):
     n = len(places)
     dq_ref = refs[n]
     outs = refs[n + 1 : 2 * n + 1]
     key_cat, value_cat = refs[2 * n + 1 :]
 
-    @pl.loop(0, pa_ref.shape[0])
+    @pl.loop(0, pa_ref.shape[0], unroll=4)
     def _(h):
         cols = head_columns(h)
         gather_rows(key_cat, keys_of(refs[:n]), cols)
         gather_rows(value_cat, values_of(refs[:n]), cols)
-        parts = take(places, pa_ref, pb_ref, h)
-        d = d_ref[:, cols]
-        dscore = score_grad(d, delta_ref[h], scale_ref[h], value_cat[...], parts)
+        parts = take(places, (pa_ref, pb_ref), h)
+        scales = (scale_a_ref[h], scale_b_ref[h])
+        dscore = score_grad(d_ref[:, cols], delta_ref[h], scales, value_cat[...], parts)
         dq_ref[:, cols] = dq_in[:, cols] + dot(dscore, key_cat[...], NN)
-        put_slots(outs, parts, d, scaled_d_ref[:, cols], dscore, q_ref[:, cols], cols)
+        put_slots(outs, parts, (d_a_ref[:, cols], d_b_ref[:, cols]), dscore, q_ref[:, cols], cols)
 
 
 def local_kernel(
@@ -294,11 +340,11 @@
     start = pl.multiple_of(start_ref[0], BLK)
     tokens = q_ref.shape[0]
 
-    @pl.loop(0, pa_ref.shape[0])
+    @pl.loop(0, pa_ref.shape[0], unroll=True)
     def _(h):
         cols = head_columns(h)
-        parts = [(pa_ref[h, :, blocks(j)], True) for j in range(nblocks)]
-        dscore = score_grad(d_ref[:, cols], delta_ref[h], scale_ref[h], v_ref[:, cols], parts)
+        parts = [(pa_ref[h, :, blocks(j)], 0) for j in range(nblocks)]
+        dscore = score_grad(d_ref[:, cols], delta_ref[h], (scale_ref[h],), v_ref[:, cols], parts)
         dq = dq_in[:, cols] + dot(dscore, k_ref[:, cols], NN)
         dq_ref[:, cols] = (dq * softmax_scale).astype(dq_ref.dtype)
         key_term[...] = dot(dscore, q_ref[:, cols], TN) * softmax_scale
@@ -405,7 +451,7 @@
         near = [move(own, lambda i, k=k: i ^ k) for k in range(1, far)]
         mates = [swap(x) for x in [own] + near]
     slots_a = near[:-1] + mates[:half]
-    slots_b = near[-1:] + mates[half:]
+    slots_b = near[-1:] + mates[half:-1]
     cols_a = tokens + len(slots_a) * BLK
     cols_b = len(slots_b) * BLK
     gain_row = gain.reshape(1, width)
@@ -427,12 +473,21 @@
         wide32,
         [((cols_a, HEAD_SIZE), bf16)],
     )
-    prob_b, scale_a, attended, stats = call(
+    prob_b, shrink, peak_b, total_b, attended = call(
         "second",
-        functools.partial(second_kernel, nblocks, far_bias, len(slots_a)),
-        [ranges, pattern, queries, peak_a, total_a, attended, grad_out, gain_row, *slots_b],
-        [shape((heads, tokens, cols_b), bf16), rows_shape, wide32, shape((8, tokens), f32)],
-        [((cols_b, HEAD_SIZE), bf16)] * 2 + [((tokens, HEAD_SIZE), f32)] * 2,
+        functools.partial(second_kernel, nblocks, far_bias, 1 + len(slots_a)),
+        [ranges, pattern, queries, peak_a, total_a, attended, *slots_b],
+        [shape((heads, tokens, cols_b), bf16), rows_shape, rows_shape, rows_shape, wide32],
+        [((cols_b, HEAD_SIZE), bf16)] * 2,
+        in_smem=(0, 1),
+        cost=1000,
+    )
+    prob_c, scale_a, scale_b, attended, stats = call(
+        "third",
+        functools.partial(third_kernel, nblocks, far_bias, 1 + len(slots_a) + len(slots_b)),
+        [ranges, pattern, queries, peak_b, total_b, shrink, attended, grad_out, gain_row, mates[-1]],
+        [shape((heads, tokens, BLK), bf16), rows_shape, rows_shape, wide32, shape((2 * nblocks, BLK), f32)],
+        [((tokens, HEAD_SIZE), f32)] * 2,
         in_smem=(0, 1),
     )
 
@@ -440,18 +495,18 @@
 
     near_places = [(0, nblocks + k) for k in range(far - 2)] + [(1, 0)]
     mate_places = [(0, nblocks + far - 2 + k) for k in range(half)]
-    mate_places += [(1, 1 + k) for k in range(far - half)]
+    mate_places += [(1, 1 + k) for k in range(far - half - 1)] + [(2, 0)]
     pair = shape((2 * BLK, width), bf16)
 
     def cats(n):
         return [((n * BLK, HEAD_SIZE), bf16)] * 2
 
-    normed, d_attended, d_scaled, delta, dq, mate_last = call(
+    normed, d_attended, d_a, d_b, delta, dq, mate_last = call(
         "grad_out",
-        functools.partial(grad_out_kernel, mate_places[-1:]),
-        [queries, stats, attended, grad_out, gain_row, scale_a, prob_a, prob_b, mates[-1]],
-        [wide16, wide16, wide16, rows_shape, wide32, pair],
-        [((tokens, HEAD_SIZE), f32)] * 2 + cats(1),
+        functools.partial(grad_out_kernel, mate_places[-1]),
+        [queries, stats, attended, grad_out, gain_row, scale_a, scale_b, prob_c, mates[-1]],
+        [wide16, wide16, wide16, wide16, rows_shape, wide32, pair],
+        [((tokens, HEAD_SIZE), f32)] * 2,
     )
 
     def slot_terms(name, places, slots, dq):
@@ -459,7 +514,7 @@
         return call(
             name,
             functools.partial(slots_kernel, places),
-            [queries, d_attended, d_scaled, delta, scale_a, prob_a, prob_b, dq, *slots],
+            [queries, d_attended, d_a, d_b, delta, scale_a, scale_b, prob_a, prob_b, dq, *slots],
             [wide32] + [pair] * n,
             cats(n),
         )
@@ -476,16 +531,14 @@
             dq,
         )
         y2 = swap(mate2)
-        y1 = swap(after(mate1, y_last))
-        c3 = add(near3, y_last)
+        y1 = swap(mate1)
+        dq, near1, mate0 = slot_terms(
+            "terms_near", [near_places[0], mate_places[0]], [near[0], mates[0]], dq
+        )
+        c3 = add(after(near3, near1), y_last)
         end3 = move(c3, lambda i: i ^ 1, outer)
-        dq, near1, mate0 = slot_terms(
-            "terms_near", [near_places[0], mate_places[0]], [near[0], mates[0]], after(dq, c3)
-        )
-        mid3 = move(add(c3, end3), lambda i: i ^ 3, inner)
-        c2 = add(after(near2, near1), y2)
-        end2 = move(c2, lambda i: i ^ 1, outer)
-        dq = after(dq, y2, end3)
+        far3 = move(add(c3, end3), lambda i: i ^ 2, inner)
+        dq = after(dq, c3)
     else:
         dq, mate0, near_last = slot_terms(
             "terms_ends",
@@ -506,16 +559,20 @@
     grad_queries, key_local, value_local, mine = call(
         "terms_local",
         functools.partial(local_kernel, nblocks),
-        [start_vec, queries, keys, values, d_attended, d_scaled, delta, scale_a, prob_a, dq],
+        [start_vec, queries, keys, values, d_attended, d_a, delta, scale_a, prob_a, dq],
         [wide16, wide16, wide16, shape((2 * BLK, width), f32)],
         [((tokens, HEAD_SIZE), f32)] * 2,
         in_smem=(0,),
+        cost=1000,
     )
     if far == 4:
-        mid2 = move(add(c2, end2), lambda i: i ^ 3, inner)
-        c1 = add(after(near1, mine), y1, mid3)
+        c2 = add(after(near2, mine), y2)
+        end2 = move(c2, lambda i: i ^ 1, outer)
+        c1 = add(near1, y1)
+        near_came = move(c1, lambda i: i ^ 1)
+        mid2 = move(add(c2, after(end2, far3)), lambda i: i ^ 3, inner)
         y0 = swap(after(mate0, y1))
-        came = [move(c1, lambda i: i ^ 1), mid2, y0]
+        came = [far3, mid2, y0, near_came]
     at = 2 + len(came)
     block = pl.BlockSpec((BLK, width), lambda i, place: (place[0], 0))
     grad_keys, grad_values = pl.pallas_call(

time: 142 us -> 136 us (0.958)
  Pallas kernels: 53.1 us -> 45.5 us
  waiting for transfers between devices: 42.5 us -> 50.1 us
  starting transfers between devices: 31.7 us -> 27.1 us
    ppermute x10, waiting for transfers between devices: 26.9 us -> 36.8 us  [move(): lax.ppermute(x, 'seq', [(i * 2 + j, to(i) * 2 + j) for i in among for j i...]
    pallas_call x7 -> x8, Pallas kernels: 47.9 us -> 40.1 us  [call(): pl.pallas_call(kernel, in_specs=[smem if i in in_smem else vmem for i in...]
    ppermute x10, starting transfers between devices: 23.3 us -> 18.7 us  [move(): lax.ppermute(x, 'seq', [(i * 2 + j, to(i) * 2 + j) for i in among for j i...]
    ppermute x8, waiting for transfers between devices: 15.6 us -> 13.3 us  [swap(): return lax.ppermute(x, 'seq', [(i, i ^ 1) for i in range(n_seq)])]
  transfers between devices with their start and end apart: 18 -> 18, of which waited for: 9 -> 12; matrix products, arithmetic and copies ran while one was open for 2% -> 2% of each run, Pallas kernels for 25% -> 24%
where the time goes in v4:
time: 136 us
  waiting for transfers between devices  50.1 us (37%)
  Pallas kernels  45.5 us (33%)
  starting transfers between devices  27.1 us (20%)
  blocking collectives  5.37 us (4%)
  between operations  3.47 us (3%)
  other arithmetic  3.19 us (2%)
    pallas_call x8, Pallas kernels, call(): pl.pallas_call(kernel, in_specs=[smem if i in in_smem else vmem for i in...  40.1 us
    ppermute x10, waiting for transfers between devices, move(): lax.ppermute(x, 'seq', [(i * 2 + j, to(i) * 2 + j) for i in among for j i...  36.8 us
    ppermute x10, starting transfers between devices, move(): lax.ppermute(x, 'seq', [(i * 2 + j, to(i) * 2 + j) for i in among for j i...  18.7 us
    ppermute x8, waiting for transfers between devices, swap(): return lax.ppermute(x, 'seq', [(i, i ^ 1) for i in range(n_seq)])  13.3 us
    ppermute x8, starting transfers between devices, swap(): return lax.ppermute(x, 'seq', [(i, i ^ 1) for i in range(n_seq)])  8.37 us
    all_gather x1, blocking collectives, shards(): stats = lax.all_gather(stats, 'head')  5.37 us
    pallas_call x1, Pallas kernels, shards(): pl.pallas_call(finish_kernel, grid_spec=pltpu.PrefetchScalarGridSpec(num_...  2.83 us
  transfers between devices with their start and end apart: 18, of which 12 were waited for; matrix products, arithmetic and copies ran while one was open for 2% of the time, Pallas kernels for 24%

profile of v4, /device:TPU:0, one launch (start us, length us, event | category | flops | bytes accessed | tf_op | source)
XLA Modules:
  0.0 135.8 jit_solution(2135646084701433774)
XLA Ops:
  0.7 2.6 %pick.1 = (bf16[256,1024]{1,0:T(8,128)(2,1)}, s32[1]{0:T(128)}) custom-call(s32[1]{0:T(128)} %bitcast.me_ref, s32[10,32]{1,0:T(8,128)} %bitcast.11, bf16[512,1024]{1,0:T(8,128)(2,1)} %k_ref.3, bf16[512,1024]{1,0:T(8,128)(2,1)} %v_ref.3), custom_call_target="tpu_custom_call" | custom-call | tf_op jit(solution)/shard_map/pick/pallas_call | solution.py:423
  4.7 5.1 %collective-permute-start = (bf16[256,1024]{1,0:T(8,128)(2,1)}, bf16[256,1024]{1,0:T(8,128)(2,1)S(1)}, u32[]{:S(2)}, u32[]{:S(2)}) collective-permute-start(bf16[256,1024]{1,0:T(8,128)(2,1)} %get-tuple-element.48), channel_id=1, source_target_pairs={{0,8},{4,12},{8,0},{12,4},{16,24},{20,28},{24,16},{28,20},{1,9},{5... | collective-permute-start | bytes 1572872 | tf_op jit(solution)/shard_map/ppermute | solution.py:386
  12.6 9.0 %collective-permute-done.refs_0_ = bf16[256,1024]{1,0:T(8,128)(2,1)S(1)} collective-permute-done((bf16[256,1024]{1,0:T(8,128)(2,1)}, bf16[256,1024]{1,0:T(8,128)(2,1)S(1)}, u32[]{:S(2)}, u32[]{:S(2)}) %collective-permute-start) | collective-permute-done | bytes 524320 | tf_op jit(solution)/shard_map/ppermute | solution.py:386
  26.2 8.6 %collective-permute-done.2 = bf16[256,1024]{1,0:T(8,128)(2,1)} collective-permute-done((bf16[256,1024]{1,0:T(8,128)(2,1)}, bf16[256,1024]{1,0:T(8,128)(2,1)}, u32[]{:S(2)}, u32[]{:S(2)}) %collective-permute-start.2) | collective-permute-done | bytes 524320 | tf_op jit(solution)/shard_map/ppermute | solution.py:386
  38.8 7.0 %first_scores.1 = (bf16[8,512,1024]{2,1,0:T(8,128)(2,1)S(1)}, f32[8,512,128]{2,1,0:T(8,128)S(1)}, f32[8,512,128]{2,1,0:T(8,128)S(1)}) custom-call(s32[8]{0:T(128)S(1)} %stack.35.ranges_ref, s32[10,32]{1,0:T(8,128)S(1)} %bitcast.12, bf16[512,1024]{1,0:T(8,128)(2,1)S(1)} %copy-done.2, bf16[512,1024]{1,0:T(8,128)(2,1)S(1)} %copy-done.3, ...), custom_call_target="tpu_custom_call" | custom-call | flops 99999997952 | bytes 100000000 | tf_op jit(solution)/shard_map/first_scores/pallas_call | solution.py:411
  45.8 5.8 %collective-permute-done.6 = bf16[256,1024]{1,0:T(8,128)(2,1)S(1)} collective-permute-done((bf16[256,1024]{1,0:T(8,128)(2,1)}, bf16[256,1024]{1,0:T(8,128)(2,1)S(1)}, u32[]{:S(2)}, u32[]{:S(2)}) %collective-permute-start.6) | collective-permute-done | bytes 524320 | tf_op jit(solution)/shard_map/ppermute | solution.py:386
  52.3 4.0 %first_attend.1.o_in = f32[512,1024]{1,0:T(8,128)S(1)} custom-call(bf16[8,512,1024]{2,1,0:T(8,128)(2,1)S(1)} %get-tuple-element.52.p_ref.pa_ref, bf16[512,1024]{1,0:T(8,128)(2,1)S(1)} %copy-done.4, bf16[256,1024]{1,0:T(8,128)(2,1)S(1)} %collective-permute-done.refs_0_, bf16[256,1024]{1,0:T(8,128)(2,1)S(1)} %broadcast_select_fusion.1.refs_1_.refs_3_, ...), custom_call_target="tpu_custom_call" | custom-call | flops 99999997952 | bytes 100000000 | tf_op jit(solution)/shard_map/first_attend/pallas_call | solution.py:411
  56.4 3.3 %second.1 = (bf16[8,512,256]{2,1,0:T(8,128)(2,1)S(1)}, f32[8,512,128]{2,1,0:T(8,128)S(1)}, f32[8,512,128]{2,1,0:T(8,128)S(1)}, f32[8,512,128]{2,1,0:T(8,128)S(1)}, f32[512,1024]{1,0:T(8,128)S(1)}) custom-call(s32[8]{0:T(128)S(1)} %stack.35.ranges_ref, s32[10,32]{1,0:T(8,128)S(1)} %bitcast.13, bf16[512,1024]{1,0:T(8,128)(2,1)S(1)} %copy-done.2, ...), custom_call_target="tpu_custom_call" | custom-call | flops 1000000 | bytes 1000 | tf_op jit(solution)/shard_map/second/pallas_call | solution.py:411
  59.7 3.1 %collective-permute-done.8.slot_ref = bf16[256,1024]{1,0:T(8,128)(2,1)S(1)} collective-permute-done((bf16[256,1024]{1,0:T(8,128)(2,1)S(1)}, bf16[256,1024]{1,0:T(8,128)(2,1)S(1)}, u32[]{:S(2)}, u32[]{:S(2)}) %collective-permute-start.8) | collective-permute-done | bytes 524320 | tf_op jit(solution)/shard_map/ppermute | solution.py:389
  62.8 3.5 %third.1 = (bf16[8,512,128]{2,1,0:T(8,128)(2,1)S(1)}, f32[8,512,128]{2,1,0:T(8,128)S(1)}, f32[8,512,128]{2,1,0:T(8,128)S(1)}, f32[512,1024]{1,0:T(8,128)S(1)}, f32[8,128]{1,0:T(8,128)S(1)}) custom-call(s32[8]{0:T(128)S(1)} %stack.35.ranges_ref, s32[10,32]{1,0:T(8,128)S(1)} %bitcast.14, bf16[512,1024]{1,0:T(8,128)(2,1)S(1)} %copy-done.2, ...), custom_call_target="tpu_custom_call" | custom-call | flops 99999997952 | bytes 100000000 | tf_op jit(solution)/shard_map/third/pallas_call | solution.py:411
  66.3 5.4 %all-gather = f32[32,128]{1,0:T(8,128)S(1)} all-gather(f32[8,128]{1,0:T(8,128)S(1)} %get-tuple-element.59), channel_id=2, replica_groups=mesh['seq'=8,'head'=4] {'head'}, dimensions={0}, use_global_device_ids=true | all-gather | bytes 20480 | tf_op jit(solution)/shard_map/all_gather | solution.py:494
  71.7 4.3 %grad_out.1 = (bf16[512,1024]{1,0:T(8,128)(2,1)}, bf16[512,1024]{1,0:T(8,128)(2,1)S(1)}, bf16[512,1024]{1,0:T(8,128)(2,1)S(1)}, bf16[512,1024]{1,0:T(8,128)(2,1)...) custom-call(bf16[512,1024]{1,0:T(8,128)(2,1)S(1)} %copy-done.2, ...), custom_call_target="tpu_custom_call" | custom-call | flops 99999997952 | bytes 100000000 | tf_op jit(solution)/shard_map/grad_out/pallas_call | solution.py:411
  76.4 7.1 %terms_far.1 = (f32[512,1024]{1,0:T(8,128)S(1)}, bf16[256,1024]{1,0:T(8,128)(2,1)S(1)}, bf16[256,1024]{1,0:T(8,128)(2,1)S(1)}, bf16[256,1024]{1,0:T(8,128)(2,1)S(1)}, bf16[256,1024]{1,0:T(8,128)(2,1)S(1)}) custom-call(bf16[512,1024]{1,0:T(8,128)(2,1)S(1)} %copy-done.2, bf16[512,1024]{1,0:T(8,128)(2,1)S(1)} %get-tuple-element.66.d_ref, ...), custom_call_target="tpu_custom_call" | custom-call | flops 99999997952 | bytes 100000000 | tf_op jit(solution)/shard_map/terms_far/pallas_call | solution.py:411
  85.1 3.6 %terms_near.1 = (f32[512,1024]{1,0:T(8,128)S(1)}, bf16[256,1024]{1,0:T(8,128)(2,1)S(1)}, bf16[256,1024]{1,0:T(8,128)(2,1)S(1)}) custom-call(bf16[512,1024]{1,0:T(8,128)(2,1)S(1)} %copy-done.2, bf16[512,1024]{1,0:T(8,128)(2,1)S(1)} %get-tuple-element.66.d_ref, bf16[512,1024]{1,0:T(8,128)(2,1)S(1)} %get-tuple-element.67.d_a_ref.scaled_d_ref, ...), custom_call_target="tpu_custom_call" | custom-call | flops 99999997952 | bytes 100000000 | tf_op jit(solution)/shard_map/terms_near/pallas_call | solution.py:411
  88.8 2.2 %collective-permute-done.9 = bf16[256,1024]{1,0:T(8,128)(2,1)} collective-permute-done((bf16[256,1024]{1,0:T(8,128)(2,1)}, bf16[256,1024]{1,0:T(8,128)(2,1)}, u32[]{:S(2)}, u32[]{:S(2)}) %collective-permute-start.9) | collective-permute-done | bytes 524320 | tf_op jit(solution)/shard_map/ppermute | solution.py:389
  92.2 3.2 %collective-permute-start.10 = (bf16[256,1024]{1,0:T(8,128)(2,1)S(1)}, bf16[256,1024]{1,0:T(8,128)(2,1)S(1)}, u32[]{:S(2)}, u32[]{:S(2)}) collective-permute-start(bf16[256,1024]{1,0:T(8,128)(2,1)S(1)} %add_convert_fusion.4), channel_id=1, source_target_pairs={{0,8},{4,12},{24,16},{28,20},{1,9},{5,13},{25,17},{29,21},{2,10},{... | collective-permute-start | bytes 1572872 | tf_op jit(solution)/shard_map/ppermute | solution.py:386
  96.1 7.3 %terms_local.1 = (bf16[512,1024]{1,0:T(8,128)(2,1)}, bf16[512,1024]{1,0:T(8,128)(2,1)}, bf16[512,1024]{1,0:T(8,128)(2,1)}, f32[256,1024]{1,0:T(8,128)S(1)}) custom-call(s32[1]{0:T(128)} %get-tuple-element.65.start_ref, bf16[512,1024]{1,0:T(8,128)(2,1)S(1)} %copy-done.2, bf16[512,1024]{1,0:T(8,128)(2,1)S(1)} %copy-done.3, bf16[512,1024]{1,0:T(8,128)(2,1)S(1)} %copy-done.5, ...), custom_call_target="tpu_custom_call" | custom-call | flops 1000000 | bytes 1000 | tf_op jit(solution)/shard_map/terms_local/pallas_call | solution.py:411
  103.6 1.8 %collective-permute-start.13 = (bf16[256,1024]{1,0:T(8,128)(2,1)S(1)}, bf16[256,1024]{1,0:T(8,128)(2,1)S(1)}, u32[]{:S(2)}, u32[]{:S(2)}) collective-permute-start(bf16[256,1024]{1,0:T(8,128)(2,1)S(1)} %add_convert_fusion.2), channel_id=1, source_target_pairs={{0,8},{4,12},{24,16},{28,20},{1,9},{5,13},{25,17},{29,21},{2,10},{... | collective-permute-start | bytes 1572872 | tf_op jit(solution)/shard_map/ppermute | solution.py:386
  108.0 4.7 %collective-permute-done.15 = bf16[256,1024]{1,0:T(8,128)(2,1)S(1)} collective-permute-done((bf16[256,1024]{1,0:T(8,128)(2,1)S(1)}, bf16[256,1024]{1,0:T(8,128)(2,1)S(1)}, u32[]{:S(2)}, u32[]{:S(2)}) %collective-permute-start.15) | collective-permute-done | bytes 524320 | tf_op jit(solution)/shard_map/ppermute | solution.py:389
  114.6 3.1 %collective-permute-done.13 = bf16[256,1024]{1,0:T(8,128)(2,1)S(1)} collective-permute-done((bf16[256,1024]{1,0:T(8,128)(2,1)S(1)}, bf16[256,1024]{1,0:T(8,128)(2,1)S(1)}, u32[]{:S(2)}, u32[]{:S(2)}) %collective-permute-start.13) | collective-permute-done | bytes 524320 | tf_op jit(solution)/shard_map/ppermute | solution.py:386
  117.8 3.1 %collective-permute-done.11.refs_0_ = bf16[256,1024]{1,0:T(8,128)(2,1)S(1)} collective-permute-done((bf16[256,1024]{1,0:T(8,128)(2,1)S(1)}, bf16[256,1024]{1,0:T(8,128)(2,1)S(1)}, u32[]{:S(2)}, u32[]{:S(2)}) %collective-permute-start.11) | collective-permute-done | bytes 524320 | tf_op jit(solution)/shard_map/ppermute | solution.py:386
  124.3 1.8 %collective-permute-done.16.refs_2_ = bf16[256,1024]{1,0:T(8,128)(2,1)S(1)} collective-permute-done((bf16[256,1024]{1,0:T(8,128)(2,1)S(1)}, bf16[256,1024]{1,0:T(8,128)(2,1)S(1)}, u32[]{:S(2)}, u32[]{:S(2)}) %collective-permute-start.16) | collective-permute-done | bytes 524320 | tf_op jit(solution)/shard_map/ppermute | solution.py:389
  126.1 5.9 %collective-permute-done.17.refs_3_ = bf16[256,1024]{1,0:T(8,128)(2,1)S(1)} collective-permute-done((bf16[256,1024]{1,0:T(8,128)(2,1)S(1)}, bf16[256,1024]{1,0:T(8,128)(2,1)S(1)}, u32[]{:S(2)}, u32[]{:S(2)}) %collective-permute-start.17) | collective-permute-done | bytes 524320 | tf_op jit(solution)/shard_map/ppermute | solution.py:386
  133.0 2.8 %finish.1 = (bf16[512,1024]{1,0:T(8,128)(2,1)}, bf16[512,1024]{1,0:T(8,128)(2,1)}) custom-call(s32[1]{0:T(128)S(6)} %select_n.41.start_ref, f32[256,1024]{1,0:T(8,128)} %copy-done.8, bf16[256,1024]{1,0:T(8,128)(2,1)} %copy-done.16, bf16[256,1024]{1,0:T(8,128)(2,1)} %copy-done.19, ...), custom_call_target="tpu_custom_call", output_to_operand_aliasing={{0}: (6, {}), {1}: (7, {})} | custom-call | tf_op jit(solution)/shard_map/finish/pallas_call | solution.py:578
  (71 shorter events, 23.9 us)
Async XLA Ops:
  0.6 38.2 %copy-start.13 = (s32[32,10]{0,1:T(8,128)S(1)}, s32[32,10]{0,1:T(8,128)}, u32[]{:S(2)}) copy-start(s32[32,10]{0,1:T(8,128)} %param.11) | copy-start | bytes 3844
  0.6 38.2 %copy-start.3 = (bf16[512,1024]{1,0:T(8,128)(2,1)S(1)}, bf16[512,1024]{1,0:T(8,128)(2,1)}, u32[]{:S(2)}) copy-start(bf16[512,1024]{1,0:T(8,128)(2,1)} %k_ref.3) | copy-start | bytes 3145732
  0.7 38.2 %copy-start.2 = (bf16[512,1024]{1,0:T(8,128)(2,1)S(1)}, bf16[512,1024]{1,0:T(8,128)(2,1)}, u32[]{:S(2)}) copy-start(bf16[512,1024]{1,0:T(8,128)(2,1)} %q_ref.13) | copy-start | bytes 3145732
  3.2 8.1 %collective-permute-start.1 = (bf16[256,1024]{1,0:T(8,128)(2,1)}, bf16[256,1024]{1,0:T(8,128)(2,1)}, u32[]{:S(2)}, u32[]{:S(2)}) collective-permute-start(bf16[256,1024]{1,0:T(8,128)(2,1)} %get-tuple-element.48), channel_id=1, source_target_pairs={{8,16},{12,20},{16,8},{20,12},{9,17},{13,21},{17,9},{21,13},{10,18... | collective-permute-start | bytes 1572872 | tf_op jit(solution)/shard_map/ppermute | solution.py:386
  4.7 17.0 %collective-permute-start = (bf16[256,1024]{1,0:T(8,128)(2,1)}, bf16[256,1024]{1,0:T(8,128)(2,1)S(1)}, u32[]{:S(2)}, u32[]{:S(2)}) collective-permute-start(bf16[256,1024]{1,0:T(8,128)(2,1)} %get-tuple-element.48), channel_id=1, source_target_pairs={{0,8},{4,12},{8,0},{12,4},{16,24},{20,28},{24,16},{28,20},{1,9},{5... | collective-permute-start | bytes 1572872 | tf_op jit(solution)/shard_map/ppermute | solution.py:386
  9.8 13.3 %collective-permute-start.3 = (bf16[256,1024]{1,0:T(8,128)(2,1)}, bf16[256,1024]{1,0:T(8,128)(2,1)S(1)}, u32[]{:S(2)}, u32[]{:S(2)}) collective-permute-start(bf16[256,1024]{1,0:T(8,128)(2,1)} %get-tuple-element.48), channel_id=1, source_target_pairs={{0,4},{4,0},{8,12},{12,8},{16,20},{20,16},{24,28},{28,24},{1,5},{5... | collective-permute-start | bytes 1572872 | tf_op jit(solution)/shard_map/ppermute | solution.py:389
  11.3 23.4 %collective-permute-start.2 = (bf16[256,1024]{1,0:T(8,128)(2,1)}, bf16[256,1024]{1,0:T(8,128)(2,1)}, u32[]{:S(2)}, u32[]{:S(2)}) collective-permute-start(bf16[256,1024]{1,0:T(8,128)(2,1)} %collective-permute-done.1), channel_id=1, source_target_pairs={{8,0},{12,4},{16,24},{20,28},{9,1},{13,5},{17,25},{21,29},{10,2},{... | collective-permute-start | bytes 1572872 | tf_op jit(solution)/shard_map/ppermute | solution.py:386
  23.1 12.8 %collective-permute-start.4 = (bf16[256,1024]{1,0:T(8,128)(2,1)S(1)}, bf16[256,1024]{1,0:T(8,128)(2,1)}, u32[]{:S(2)}, u32[]{:S(2)}) collective-permute-start(bf16[256,1024]{1,0:T(8,128)(2,1)S(1)} %collective-permute-done.refs_0_), channel_id=1, source_target_pairs={{0,4},{4,0},{8,12},{12,8},{16,20},{20,16},{24,28},{28,24},{1,5},{5... | collective-permute-start | bytes 1572872 | tf_op jit(solution)/shard_map/ppermute | solution.py:389
  24.7 12.8 %collective-permute-start.5 = (bf16[256,1024]{1,0:T(8,128)(2,1)S(1)}, bf16[256,1024]{1,0:T(8,128)(2,1)}, u32[]{:S(2)}, u32[]{:S(2)}) collective-permute-start(bf16[256,1024]{1,0:T(8,128)(2,1)S(1)} %collective-permute-done.refs_0_), channel_id=1, source_target_pairs={{8,16},{12,20},{16,8},{20,12},{9,17},{13,21},{17,9},{21,13},{10,18... | collective-permute-start | bytes 1572872 | tf_op jit(solution)/shard_map/ppermute | solution.py:386
  35.9 16.4 %copy-start.11 = (bf16[256,1024]{1,0:T(8,128)(2,1)}, bf16[256,1024]{1,0:T(8,128)(2,1)S(1)}, u32[]{:S(2)}) copy-start(bf16[256,1024]{1,0:T(8,128)(2,1)S(1)} %broadcast_select_fusion.1.refs_1_.refs_3_) | copy-start | bytes 1572868
  35.9 16.4 %copy-start.4 = (bf16[512,1024]{1,0:T(8,128)(2,1)S(1)}, bf16[512,1024]{1,0:T(8,128)(2,1)}, u32[]{:S(2)}) copy-start(bf16[512,1024]{1,0:T(8,128)(2,1)} %v_ref.3) | copy-start | bytes 3145732
  35.9 15.8 %collective-permute-start.7 = (bf16[256,1024]{1,0:T(8,128)(2,1)S(1)}, bf16[256,1024]{1,0:T(8,128)(2,1)S(1)}, u32[]{:S(2)}, u32[]{:S(2)}) collective-permute-start(bf16[256,1024]{1,0:T(8,128)(2,1)S(1)} %broadcast_select_fusion.1.refs_1_.refs_3_), channel_id=1, source_target_pairs={{0,4},{4,0},{8,12},{12,8},{16,20},{20,16},{24,28},{28,24},{1,5},{5... | collective-permute-start | bytes 1572872 | tf_op jit(solution)/shard_map/ppermute | solution.py:389
  37.5 14.1 %collective-permute-start.6 = (bf16[256,1024]{1,0:T(8,128)(2,1)}, bf16[256,1024]{1,0:T(8,128)(2,1)S(1)}, u32[]{:S(2)}, u32[]{:S(2)}) collective-permute-start(bf16[256,1024]{1,0:T(8,128)(2,1)} %collective-permute-done.5), channel_id=1, source_target_pairs={{8,0},{12,4},{16,24},{20,28},{9,1},{13,5},{17,25},{21,29},{10,2},{... | collective-permute-start | bytes 1572872 | tf_op jit(solution)/shard_map/ppermute | solution.py:386
  51.7 11.0 %collective-permute-start.8 = (bf16[256,1024]{1,0:T(8,128)(2,1)S(1)}, bf16[256,1024]{1,0:T(8,128)(2,1)S(1)}, u32[]{:S(2)}, u32[]{:S(2)}) collective-permute-start(bf16[256,1024]{1,0:T(8,128)(2,1)S(1)} %broadcast_select_fusion.refs_0_.refs_2_), channel_id=1, source_target_pairs={{0,4},{4,0},{8,12},{12,8},{16,20},{20,16},{24,28},{28,24},{1,5},{5... | collective-permute-start | bytes 1572872 | tf_op jit(solution)/shard_map/ppermute | solution.py:389
  75.9 15.1 %collective-permute-start.9 = (bf16[256,1024]{1,0:T(8,128)(2,1)}, bf16[256,1024]{1,0:T(8,128)(2,1)}, u32[]{:S(2)}, u32[]{:S(2)}) collective-permute-start(bf16[256,1024]{1,0:T(8,128)(2,1)} %get-tuple-element.77), channel_id=1, source_target_pairs={{0,4},{4,0},{8,12},{12,8},{16,20},{20,16},{24,28},{28,24},{1,5},{5... | collective-permute-start | bytes 1572872 | tf_op jit(solution)/shard_map/ppermute | solution.py:389
  83.5 19.8 %collective-permute-start.12 = (bf16[256,1024]{1,0:T(8,128)(2,1)S(1)}, bf16[256,1024]{1,0:T(8,128)(2,1)S(1)}, u32[]{:S(2)}, u32[]{:S(2)}) collective-permute-start(bf16[256,1024]{1,0:T(8,128)(2,1)S(1)} %get-tuple-element.83), channel_id=1, source_target_pairs={{0,4},{4,0},{8,12},{12,8},{16,20},{20,16},{24,28},{28,24},{1,5},{5... | collective-permute-start | bytes 1572872 | tf_op jit(solution)/shard_map/ppermute | solution.py:389
  92.2 14.3 %collective-permute-start.10 = (bf16[256,1024]{1,0:T(8,128)(2,1)S(1)}, bf16[256,1024]{1,0:T(8,128)(2,1)S(1)}, u32[]{:S(2)}, u32[]{:S(2)}) collective-permute-start(bf16[256,1024]{1,0:T(8,128)(2,1)S(1)} %add_convert_fusion.4), channel_id=1, source_target_pairs={{0,8},{4,12},{24,16},{28,20},{1,9},{5,13},{25,17},{29,21},{2,10},{... | collective-permute-start | bytes 1572872 | tf_op jit(solution)/shard_map/ppermute | solution.py:386
  95.5 17.3 %collective-permute-start.15 = (bf16[256,1024]{1,0:T(8,128)(2,1)S(1)}, bf16[256,1024]{1,0:T(8,128)(2,1)S(1)}, u32[]{:S(2)}, u32[]{:S(2)}) collective-permute-start(bf16[256,1024]{1,0:T(8,128)(2,1)S(1)} %get-tuple-element.86), channel_id=1, source_target_pairs={{0,4},{4,0},{8,12},{12,8},{16,20},{20,16},{24,28},{28,24},{1,5},{5... | collective-permute-start | bytes 1572872 | tf_op jit(solution)/shard_map/ppermute | solution.py:389
  103.6 14.2 %collective-permute-start.13 = (bf16[256,1024]{1,0:T(8,128)(2,1)S(1)}, bf16[256,1024]{1,0:T(8,128)(2,1)S(1)}, u32[]{:S(2)}, u32[]{:S(2)}) collective-permute-start(bf16[256,1024]{1,0:T(8,128)(2,1)S(1)} %add_convert_fusion.2), channel_id=1, source_target_pairs={{0,8},{4,12},{24,16},{28,20},{1,9},{5,13},{25,17},{29,21},{2,10},{... | collective-permute-start | bytes 1572872 | tf_op jit(solution)/shard_map/ppermute | solution.py:386
  106.7 14.2 %collective-permute-start.11 = (bf16[256,1024]{1,0:T(8,128)(2,1)S(1)}, bf16[256,1024]{1,0:T(8,128)(2,1)S(1)}, u32[]{:S(2)}, u32[]{:S(2)}) collective-permute-start(bf16[256,1024]{1,0:T(8,128)(2,1)S(1)} %add_convert_fusion.3), channel_id=1, source_target_pairs={{8,24},{12,28},{16,0},{20,4},{9,25},{13,29},{17,1},{21,5},{10,26},... | collective-permute-start | bytes 1572872 | tf_op jit(solution)/shard_map/ppermute | solution.py:386
  112.7 13.3 %collective-permute-start.16 = (bf16[256,1024]{1,0:T(8,128)(2,1)S(1)}, bf16[256,1024]{1,0:T(8,128)(2,1)S(1)}, u32[]{:S(2)}, u32[]{:S(2)}) collective-permute-start(bf16[256,1024]{1,0:T(8,128)(2,1)S(1)} %get-tuple-element.87), channel_id=1, source_target_pairs={{0,4},{4,0},{8,12},{12,8},{16,20},{20,16},{24,28},{28,24},{1,5},{5... | collective-permute-start | bytes 1572872 | tf_op jit(solution)/shard_map/ppermute | solution.py:389
  113.5 18.6 %collective-permute-start.17 = (bf16[256,1024]{1,0:T(8,128)(2,1)S(1)}, bf16[256,1024]{1,0:T(8,128)(2,1)S(1)}, u32[]{:S(2)}, u32[]{:S(2)}) collective-permute-start(bf16[256,1024]{1,0:T(8,128)(2,1)S(1)} %add_convert_fusion), channel_id=1, source_target_pairs={{0,8},{4,12},{8,0},{12,4},{16,24},{20,28},{24,16},{28,20},{1,9},{5... | collective-permute-start | bytes 1572872 | tf_op jit(solution)/shard_map/ppermute | solution.py:386
  120.9 11.1 %copy-start.16 = (bf16[256,1024]{1,0:T(8,128)(2,1)}, bf16[256,1024]{1,0:T(8,128)(2,1)S(1)}, u32[]{:S(2)}) copy-start(bf16[256,1024]{1,0:T(8,128)(2,1)S(1)} %collective-permute-done.11.refs_0_) | copy-start | bytes 1572868
  121.1 10.9 %collective-permute-start.14 = (bf16[256,1024]{1,0:T(8,128)(2,1)S(1)}, bf16[256,1024]{1,0:T(8,128)(2,1)S(1)}, u32[]{:S(2)}, u32[]{:S(2)}) collective-permute-start(bf16[256,1024]{1,0:T(8,128)(2,1)S(1)} %add_convert_fusion.1), channel_id=1, source_target_pairs={{8,16},{12,20},{16,8},{20,12},{9,17},{13,21},{17,9},{21,13},{10,18... | collective-permute-start | bytes 1572872 | tf_op jit(solution)/shard_map/ppermute | solution.py:386
  (14 other events, 76.8 us)

commit v5 on v4

--- a/solution.py
+++ b/solution.py
@@ -153,7 +153,7 @@
     p_ref, shrink_ref, peak_ref, total_ref, o_ref, key_cat, value_cat = refs[-7:]
     biases = later_biases(nblocks, far_bias, at, len(slots), ranges_ref, pattern_ref)
 
-    @pl.loop(0, p_ref.shape[0], unroll=4)
+    @pl.loop(0, p_ref.shape[0], unroll=True)
     def _(h):
         cols = head_columns(h)
         gather_rows(key_cat, keys_of(slots), cols)
@@ -306,7 +306,7 @@
     outs = refs[n + 1 : 2 * n + 1]
     key_cat, value_cat = refs[2 * n + 1 :]
 
-    @pl.loop(0, pa_ref.shape[0], unroll=4)
+    @pl.loop(0, pa_ref.shape[0], unroll=True)
     def _(h):
         cols = head_columns(h)
         gather_rows(key_cat, keys_of(refs[:n]), cols)

time: 136 us -> 136 us (level)
  transfers between devices with their start and end apart: 18 -> 18, of which waited for: 12 -> 12; matrix products, arithmetic and copies ran while one was open for 2% -> 2% of each run, Pallas kernels for 24% -> 23%
where the time goes in v5:
time: 136 us
  waiting for transfers between devices  50.6 us (37%)
  Pallas kernels  45 us (33%)
  starting transfers between devices  27.1 us (20%)
  blocking collectives  5.37 us (4%)
  between operations  3.47 us (3%)
  other arithmetic  3.19 us (2%)
    pallas_call x8, Pallas kernels, call(): pl.pallas_call(kernel, in_specs=[smem if i in in_smem else vmem for i in...  39.6 us
    ppermute x10, waiting for transfers between devices, move(): lax.ppermute(x, 'seq', [(i * 2 + j, to(i) * 2 + j) for i in among for j i...  36.8 us
    ppermute x10, starting transfers between devices, move(): lax.ppermute(x, 'seq', [(i * 2 + j, to(i) * 2 + j) for i in among for j i...  18.7 us
    ppermute x8, waiting for transfers between devices, swap(): return lax.ppermute(x, 'seq', [(i, i ^ 1) for i in range(n_seq)])  13.8 us
    ppermute x8, starting transfers between devices, swap(): return lax.ppermute(x, 'seq', [(i, i ^ 1) for i in range(n_seq)])  8.37 us
    all_gather x1, blocking collectives, shards(): stats = lax.all_gather(stats, 'head')  5.37 us
    pallas_call x1, Pallas kernels, shards(): pl.pallas_call(finish_kernel, grid_spec=pltpu.PrefetchScalarGridSpec(num_...  2.83 us
  transfers between devices with their start and end apart: 18, of which 12 were waited for; matrix products, arithmetic and copies ran while one was open for 2% of the time, Pallas kernels for 23%

profile of v5, /device:TPU:0, one launch (start us, length us, event | category | flops | bytes accessed | tf_op | source)
XLA Modules:
  0.0 135.8 jit_solution(911135914177794639)
XLA Ops:
  0.7 2.6 %pick.1 = (bf16[256,1024]{1,0:T(8,128)(2,1)}, s32[1]{0:T(128)}) custom-call(s32[1]{0:T(128)} %bitcast.me_ref, s32[10,32]{1,0:T(8,128)} %bitcast.11, bf16[512,1024]{1,0:T(8,128)(2,1)} %k_ref.3, bf16[512,1024]{1,0:T(8,128)(2,1)} %v_ref.3), custom_call_target="tpu_custom_call" | custom-call | tf_op jit(solution)/shard_map/pick/pallas_call | solution.py:423
  4.7 5.1 %collective-permute-start = (bf16[256,1024]{1,0:T(8,128)(2,1)}, bf16[256,1024]{1,0:T(8,128)(2,1)S(1)}, u32[]{:S(2)}, u32[]{:S(2)}) collective-permute-start(bf16[256,1024]{1,0:T(8,128)(2,1)} %get-tuple-element.48), channel_id=1, source_target_pairs={{0,8},{4,12},{8,0},{12,4},{16,24},{20,28},{24,16},{28,20},{1,9},{5... | collective-permute-start | bytes 1572872 | tf_op jit(solution)/shard_map/ppermute | solution.py:386
  12.6 9.0 %collective-permute-done.refs_0_ = bf16[256,1024]{1,0:T(8,128)(2,1)S(1)} collective-permute-done((bf16[256,1024]{1,0:T(8,128)(2,1)}, bf16[256,1024]{1,0:T(8,128)(2,1)S(1)}, u32[]{:S(2)}, u32[]{:S(2)}) %collective-permute-start) | collective-permute-done | bytes 524320 | tf_op jit(solution)/shard_map/ppermute | solution.py:386
  26.2 8.6 %collective-permute-done.2 = bf16[256,1024]{1,0:T(8,128)(2,1)} collective-permute-done((bf16[256,1024]{1,0:T(8,128)(2,1)}, bf16[256,1024]{1,0:T(8,128)(2,1)}, u32[]{:S(2)}, u32[]{:S(2)}) %collective-permute-start.2) | collective-permute-done | bytes 524320 | tf_op jit(solution)/shard_map/ppermute | solution.py:386
  38.8 7.0 %first_scores.1 = (bf16[8,512,1024]{2,1,0:T(8,128)(2,1)S(1)}, f32[8,512,128]{2,1,0:T(8,128)S(1)}, f32[8,512,128]{2,1,0:T(8,128)S(1)}) custom-call(s32[8]{0:T(128)S(1)} %stack.35.ranges_ref, s32[10,32]{1,0:T(8,128)S(1)} %bitcast.12, bf16[512,1024]{1,0:T(8,128)(2,1)S(1)} %copy-done.2, bf16[512,1024]{1,0:T(8,128)(2,1)S(1)} %copy-done.3, ...), custom_call_target="tpu_custom_call" | custom-call | flops 99999997952 | bytes 100000000 | tf_op jit(solution)/shard_map/first_scores/pallas_call | solution.py:411
  45.8 5.8 %collective-permute-done.6 = bf16[256,1024]{1,0:T(8,128)(2,1)S(1)} collective-permute-done((bf16[256,1024]{1,0:T(8,128)(2,1)}, bf16[256,1024]{1,0:T(8,128)(2,1)S(1)}, u32[]{:S(2)}, u32[]{:S(2)}) %collective-permute-start.6) | collective-permute-done | bytes 524320 | tf_op jit(solution)/shard_map/ppermute | solution.py:386
  52.3 4.0 %first_attend.1.o_in = f32[512,1024]{1,0:T(8,128)S(1)} custom-call(bf16[8,512,1024]{2,1,0:T(8,128)(2,1)S(1)} %get-tuple-element.52.p_ref.pa_ref, bf16[512,1024]{1,0:T(8,128)(2,1)S(1)} %copy-done.4, bf16[256,1024]{1,0:T(8,128)(2,1)S(1)} %collective-permute-done.refs_0_, bf16[256,1024]{1,0:T(8,128)(2,1)S(1)} %broadcast_select_fusion.1.refs_1_.refs_3_, ...), custom_call_target="tpu_custom_call" | custom-call | flops 99999997952 | bytes 100000000 | tf_op jit(solution)/shard_map/first_attend/pallas_call | solution.py:411
  56.4 3.3 %second.1 = (bf16[8,512,256]{2,1,0:T(8,128)(2,1)S(1)}, f32[8,512,128]{2,1,0:T(8,128)S(1)}, f32[8,512,128]{2,1,0:T(8,128)S(1)}, f32[8,512,128]{2,1,0:T(8,128)S(1)}, f32[512,1024]{1,0:T(8,128)S(1)}) custom-call(s32[8]{0:T(128)S(1)} %stack.35.ranges_ref, s32[10,32]{1,0:T(8,128)S(1)} %bitcast.13, bf16[512,1024]{1,0:T(8,128)(2,1)S(1)} %copy-done.2, ...), custom_call_target="tpu_custom_call" | custom-call | flops 1000000 | bytes 1000 | tf_op jit(solution)/shard_map/second/pallas_call | solution.py:411
  59.6 3.1 %collective-permute-done.8.slot_ref = bf16[256,1024]{1,0:T(8,128)(2,1)S(1)} collective-permute-done((bf16[256,1024]{1,0:T(8,128)(2,1)S(1)}, bf16[256,1024]{1,0:T(8,128)(2,1)S(1)}, u32[]{:S(2)}, u32[]{:S(2)}) %collective-permute-start.8) | collective-permute-done | bytes 524320 | tf_op jit(solution)/shard_map/ppermute | solution.py:389
  62.8 3.5 %third.1 = (bf16[8,512,128]{2,1,0:T(8,128)(2,1)S(1)}, f32[8,512,128]{2,1,0:T(8,128)S(1)}, f32[8,512,128]{2,1,0:T(8,128)S(1)}, f32[512,1024]{1,0:T(8,128)S(1)}, f32[8,128]{1,0:T(8,128)S(1)}) custom-call(s32[8]{0:T(128)S(1)} %stack.35.ranges_ref, s32[10,32]{1,0:T(8,128)S(1)} %bitcast.14, bf16[512,1024]{1,0:T(8,128)(2,1)S(1)} %copy-done.2, ...), custom_call_target="tpu_custom_call" | custom-call | flops 99999997952 | bytes 100000000 | tf_op jit(solution)/shard_map/third/pallas_call | solution.py:411
  66.3 5.4 %all-gather = f32[32,128]{1,0:T(8,128)S(1)} all-gather(f32[8,128]{1,0:T(8,128)S(1)} %get-tuple-element.59), channel_id=2, replica_groups=mesh['seq'=8,'head'=4] {'head'}, dimensions={0}, use_global_device_ids=true | all-gather | bytes 20480 | tf_op jit(solution)/shard_map/all_gather | solution.py:494
  71.7 4.3 %grad_out.1 = (bf16[512,1024]{1,0:T(8,128)(2,1)}, bf16[512,1024]{1,0:T(8,128)(2,1)S(1)}, bf16[512,1024]{1,0:T(8,128)(2,1)S(1)}, bf16[512,1024]{1,0:T(8,128)(2,1)...) custom-call(bf16[512,1024]{1,0:T(8,128)(2,1)S(1)} %copy-done.2, ...), custom_call_target="tpu_custom_call" | custom-call | flops 99999997952 | bytes 100000000 | tf_op jit(solution)/shard_map/grad_out/pallas_call | solution.py:411
  76.4 6.8 %terms_far.1 = (f32[512,1024]{1,0:T(8,128)S(1)}, bf16[256,1024]{1,0:T(8,128)(2,1)S(1)}, bf16[256,1024]{1,0:T(8,128)(2,1)S(1)}, bf16[256,1024]{1,0:T(8,128)(2,1)S(1)}, bf16[256,1024]{1,0:T(8,128)(2,1)S(1)}) custom-call(bf16[512,1024]{1,0:T(8,128)(2,1)S(1)} %copy-done.2, bf16[512,1024]{1,0:T(8,128)(2,1)S(1)} %get-tuple-element.66.d_ref, ...), custom_call_target="tpu_custom_call" | custom-call | flops 99999997952 | bytes 100000000 | tf_op jit(solution)/shard_map/terms_far/pallas_call | solution.py:411
  84.9 3.4 %terms_near.1 = (f32[512,1024]{1,0:T(8,128)S(1)}, bf16[256,1024]{1,0:T(8,128)(2,1)S(1)}, bf16[256,1024]{1,0:T(8,128)(2,1)S(1)}) custom-call(bf16[512,1024]{1,0:T(8,128)(2,1)S(1)} %copy-done.2, bf16[512,1024]{1,0:T(8,128)(2,1)S(1)} %get-tuple-element.66.d_ref, bf16[512,1024]{1,0:T(8,128)(2,1)S(1)} %get-tuple-element.67.d_a_ref.scaled_d_ref, ...), custom_call_target="tpu_custom_call" | custom-call | flops 99999997952 | bytes 100000000 | tf_op jit(solution)/shard_map/terms_near/pallas_call | solution.py:411
  88.3 2.7 %collective-permute-done.9 = bf16[256,1024]{1,0:T(8,128)(2,1)} collective-permute-done((bf16[256,1024]{1,0:T(8,128)(2,1)}, bf16[256,1024]{1,0:T(8,128)(2,1)}, u32[]{:S(2)}, u32[]{:S(2)}) %collective-permute-start.9) | collective-permute-done | bytes 524320 | tf_op jit(solution)/shard_map/ppermute | solution.py:389
  92.2 3.2 %collective-permute-start.10 = (bf16[256,1024]{1,0:T(8,128)(2,1)S(1)}, bf16[256,1024]{1,0:T(8,128)(2,1)S(1)}, u32[]{:S(2)}, u32[]{:S(2)}) collective-permute-start(bf16[256,1024]{1,0:T(8,128)(2,1)S(1)} %add_convert_fusion.4), channel_id=1, source_target_pairs={{0,8},{4,12},{24,16},{28,20},{1,9},{5,13},{25,17},{29,21},{2,10},{... | collective-permute-start | bytes 1572872 | tf_op jit(solution)/shard_map/ppermute | solution.py:386
  96.1 7.3 %terms_local.1 = (bf16[512,1024]{1,0:T(8,128)(2,1)}, bf16[512,1024]{1,0:T(8,128)(2,1)}, bf16[512,1024]{1,0:T(8,128)(2,1)}, f32[256,1024]{1,0:T(8,128)S(1)}) custom-call(s32[1]{0:T(128)} %get-tuple-element.65.start_ref, bf16[512,1024]{1,0:T(8,128)(2,1)S(1)} %copy-done.2, bf16[512,1024]{1,0:T(8,128)(2,1)S(1)} %copy-done.3, bf16[512,1024]{1,0:T(8,128)(2,1)S(1)} %copy-done.5, ...), custom_call_target="tpu_custom_call" | custom-call | flops 1000000 | bytes 1000 | tf_op jit(solution)/shard_map/terms_local/pallas_call | solution.py:411
  103.6 1.8 %collective-permute-start.13 = (bf16[256,1024]{1,0:T(8,128)(2,1)S(1)}, bf16[256,1024]{1,0:T(8,128)(2,1)S(1)}, u32[]{:S(2)}, u32[]{:S(2)}) collective-permute-start(bf16[256,1024]{1,0:T(8,128)(2,1)S(1)} %add_convert_fusion.2), channel_id=1, source_target_pairs={{0,8},{4,12},{24,16},{28,20},{1,9},{5,13},{25,17},{29,21},{2,10},{... | collective-permute-start | bytes 1572872 | tf_op jit(solution)/shard_map/ppermute | solution.py:386
  108.0 4.7 %collective-permute-done.15 = bf16[256,1024]{1,0:T(8,128)(2,1)S(1)} collective-permute-done((bf16[256,1024]{1,0:T(8,128)(2,1)S(1)}, bf16[256,1024]{1,0:T(8,128)(2,1)S(1)}, u32[]{:S(2)}, u32[]{:S(2)}) %collective-permute-start.15) | collective-permute-done | bytes 524320 | tf_op jit(solution)/shard_map/ppermute | solution.py:389
  114.6 3.1 %collective-permute-done.13 = bf16[256,1024]{1,0:T(8,128)(2,1)S(1)} collective-permute-done((bf16[256,1024]{1,0:T(8,128)(2,1)S(1)}, bf16[256,1024]{1,0:T(8,128)(2,1)S(1)}, u32[]{:S(2)}, u32[]{:S(2)}) %collective-permute-start.13) | collective-permute-done | bytes 524320 | tf_op jit(solution)/shard_map/ppermute | solution.py:386
  117.8 3.1 %collective-permute-done.11.refs_0_ = bf16[256,1024]{1,0:T(8,128)(2,1)S(1)} collective-permute-done((bf16[256,1024]{1,0:T(8,128)(2,1)S(1)}, bf16[256,1024]{1,0:T(8,128)(2,1)S(1)}, u32[]{:S(2)}, u32[]{:S(2)}) %collective-permute-start.11) | collective-permute-done | bytes 524320 | tf_op jit(solution)/shard_map/ppermute | solution.py:386
  124.3 1.8 %collective-permute-done.16.refs_2_ = bf16[256,1024]{1,0:T(8,128)(2,1)S(1)} collective-permute-done((bf16[256,1024]{1,0:T(8,128)(2,1)S(1)}, bf16[256,1024]{1,0:T(8,128)(2,1)S(1)}, u32[]{:S(2)}, u32[]{:S(2)}) %collective-permute-start.16) | collective-permute-done | bytes 524320 | tf_op jit(solution)/shard_map/ppermute | solution.py:389
  126.1 5.9 %collective-permute-done.17.refs_3_ = bf16[256,1024]{1,0:T(8,128)(2,1)S(1)} collective-permute-done((bf16[256,1024]{1,0:T(8,128)(2,1)S(1)}, bf16[256,1024]{1,0:T(8,128)(2,1)S(1)}, u32[]{:S(2)}, u32[]{:S(2)}) %collective-permute-start.17) | collective-permute-done | bytes 524320 | tf_op jit(solution)/shard_map/ppermute | solution.py:386
  133.0 2.8 %finish.1 = (bf16[512,1024]{1,0:T(8,128)(2,1)}, bf16[512,1024]{1,0:T(8,128)(2,1)}) custom-call(s32[1]{0:T(128)S(6)} %select_n.41.start_ref, f32[256,1024]{1,0:T(8,128)} %copy-done.8, bf16[256,1024]{1,0:T(8,128)(2,1)} %copy-done.16, bf16[256,1024]{1,0:T(8,128)(2,1)} %copy-done.19, ...), custom_call_target="tpu_custom_call", output_to_operand_aliasing={{0}: (6, {}), {1}: (7, {})} | custom-call | tf_op jit(solution)/shard_map/finish/pallas_call | solution.py:578
  (71 shorter events, 23.9 us)
Async XLA Ops:
  0.6 38.2 %copy-start.13 = (s32[32,10]{0,1:T(8,128)S(1)}, s32[32,10]{0,1:T(8,128)}, u32[]{:S(2)}) copy-start(s32[32,10]{0,1:T(8,128)} %param.11) | copy-start | bytes 3844
  0.6 38.2 %copy-start.3 = (bf16[512,1024]{1,0:T(8,128)(2,1)S(1)}, bf16[512,1024]{1,0:T(8,128)(2,1)}, u32[]{:S(2)}) copy-start(bf16[512,1024]{1,0:T(8,128)(2,1)} %k_ref.3) | copy-start | bytes 3145732
  0.7 38.2 %copy-start.2 = (bf16[512,1024]{1,0:T(8,128)(2,1)S(1)}, bf16[512,1024]{1,0:T(8,128)(2,1)}, u32[]{:S(2)}) copy-start(bf16[512,1024]{1,0:T(8,128)(2,1)} %q_ref.13) | copy-start | bytes 3145732
  3.2 8.1 %collective-permute-start.1 = (bf16[256,1024]{1,0:T(8,128)(2,1)}, bf16[256,1024]{1,0:T(8,128)(2,1)}, u32[]{:S(2)}, u32[]{:S(2)}) collective-permute-start(bf16[256,1024]{1,0:T(8,128)(2,1)} %get-tuple-element.48), channel_id=1, source_target_pairs={{8,16},{12,20},{16,8},{20,12},{9,17},{13,21},{17,9},{21,13},{10,18... | collective-permute-start | bytes 1572872 | tf_op jit(solution)/shard_map/ppermute | solution.py:386
  4.7 17.0 %collective-permute-start = (bf16[256,1024]{1,0:T(8,128)(2,1)}, bf16[256,1024]{1,0:T(8,128)(2,1)S(1)}, u32[]{:S(2)}, u32[]{:S(2)}) collective-permute-start(bf16[256,1024]{1,0:T(8,128)(2,1)} %get-tuple-element.48), channel_id=1, source_target_pairs={{0,8},{4,12},{8,0},{12,4},{16,24},{20,28},{24,16},{28,20},{1,9},{5... | collective-permute-start | bytes 1572872 | tf_op jit(solution)/shard_map/ppermute | solution.py:386
  9.8 13.3 %collective-permute-start.3 = (bf16[256,1024]{1,0:T(8,128)(2,1)}, bf16[256,1024]{1,0:T(8,128)(2,1)S(1)}, u32[]{:S(2)}, u32[]{:S(2)}) collective-permute-start(bf16[256,1024]{1,0:T(8,128)(2,1)} %get-tuple-element.48), channel_id=1, source_target_pairs={{0,4},{4,0},{8,12},{12,8},{16,20},{20,16},{24,28},{28,24},{1,5},{5... | collective-permute-start | bytes 1572872 | tf_op jit(solution)/shard_map/ppermute | solution.py:389
  11.3 23.4 %collective-permute-start.2 = (bf16[256,1024]{1,0:T(8,128)(2,1)}, bf16[256,1024]{1,0:T(8,128)(2,1)}, u32[]{:S(2)}, u32[]{:S(2)}) collective-permute-start(bf16[256,1024]{1,0:T(8,128)(2,1)} %collective-permute-done.1), channel_id=1, source_target_pairs={{8,0},{12,4},{16,24},{20,28},{9,1},{13,5},{17,25},{21,29},{10,2},{... | collective-permute-start | bytes 1572872 | tf_op jit(solution)/shard_map/ppermute | solution.py:386
  23.1 12.8 %collective-permute-start.4 = (bf16[256,1024]{1,0:T(8,128)(2,1)S(1)}, bf16[256,1024]{1,0:T(8,128)(2,1)}, u32[]{:S(2)}, u32[]{:S(2)}) collective-permute-start(bf16[256,1024]{1,0:T(8,128)(2,1)S(1)} %collective-permute-done.refs_0_), channel_id=1, source_target_pairs={{0,4},{4,0},{8,12},{12,8},{16,20},{20,16},{24,28},{28,24},{1,5},{5... | collective-permute-start | bytes 1572872 | tf_op jit(solution)/shard_map/ppermute | solution.py:389
  24.7 12.8 %collective-permute-start.5 = (bf16[256,1024]{1,0:T(8,128)(2,1)S(1)}, bf16[256,1024]{1,0:T(8,128)(2,1)}, u32[]{:S(2)}, u32[]{:S(2)}) collective-permute-start(bf16[256,1024]{1,0:T(8,128)(2,1)S(1)} %collective-permute-done.refs_0_), channel_id=1, source_target_pairs={{8,16},{12,20},{16,8},{20,12},{9,17},{13,21},{17,9},{21,13},{10,18... | collective-permute-start | bytes 1572872 | tf_op jit(solution)/shard_map/ppermute | solution.py:386
  35.9 16.4 %copy-start.11 = (bf16[256,1024]{1,0:T(8,128)(2,1)}, bf16[256,1024]{1,0:T(8,128)(2,1)S(1)}, u32[]{:S(2)}) copy-start(bf16[256,1024]{1,0:T(8,128)(2,1)S(1)} %broadcast_select_fusion.1.refs_1_.refs_3_) | copy-start | bytes 1572868
  35.9 16.4 %copy-start.4 = (bf16[512,1024]{1,0:T(8,128)(2,1)S(1)}, bf16[512,1024]{1,0:T(8,128)(2,1)}, u32[]{:S(2)}) copy-start(bf16[512,1024]{1,0:T(8,128)(2,1)} %v_ref.3) | copy-start | bytes 3145732
  35.9 15.8 %collective-permute-start.7 = (bf16[256,1024]{1,0:T(8,128)(2,1)S(1)}, bf16[256,1024]{1,0:T(8,128)(2,1)S(1)}, u32[]{:S(2)}, u32[]{:S(2)}) collective-permute-start(bf16[256,1024]{1,0:T(8,128)(2,1)S(1)} %broadcast_select_fusion.1.refs_1_.refs_3_), channel_id=1, source_target_pairs={{0,4},{4,0},{8,12},{12,8},{16,20},{20,16},{24,28},{28,24},{1,5},{5... | collective-permute-start | bytes 1572872 | tf_op jit(solution)/shard_map/ppermute | solution.py:389
  37.5 14.1 %collective-permute-start.6 = (bf16[256,1024]{1,0:T(8,128)(2,1)}, bf16[256,1024]{1,0:T(8,128)(2,1)S(1)}, u32[]{:S(2)}, u32[]{:S(2)}) collective-permute-start(bf16[256,1024]{1,0:T(8,128)(2,1)} %collective-permute-done.5), channel_id=1, source_target_pairs={{8,0},{12,4},{16,24},{20,28},{9,1},{13,5},{17,25},{21,29},{10,2},{... | collective-permute-start | bytes 1572872 | tf_op jit(solution)/shard_map/ppermute | solution.py:386
  51.7 11.0 %collective-permute-start.8 = (bf16[256,1024]{1,0:T(8,128)(2,1)S(1)}, bf16[256,1024]{1,0:T(8,128)(2,1)S(1)}, u32[]{:S(2)}, u32[]{:S(2)}) collective-permute-start(bf16[256,1024]{1,0:T(8,128)(2,1)S(1)} %broadcast_select_fusion.refs_0_.refs_2_), channel_id=1, source_target_pairs={{0,4},{4,0},{8,12},{12,8},{16,20},{20,16},{24,28},{28,24},{1,5},{5... | collective-permute-start | bytes 1572872 | tf_op jit(solution)/shard_map/ppermute | solution.py:389
  75.9 15.1 %collective-permute-start.9 = (bf16[256,1024]{1,0:T(8,128)(2,1)}, bf16[256,1024]{1,0:T(8,128)(2,1)}, u32[]{:S(2)}, u32[]{:S(2)}) collective-permute-start(bf16[256,1024]{1,0:T(8,128)(2,1)} %get-tuple-element.77), channel_id=1, source_target_pairs={{0,4},{4,0},{8,12},{12,8},{16,20},{20,16},{24,28},{28,24},{1,5},{5... | collective-permute-start | bytes 1572872 | tf_op jit(solution)/shard_map/ppermute | solution.py:389
  83.3 20.1 %collective-permute-start.12 = (bf16[256,1024]{1,0:T(8,128)(2,1)S(1)}, bf16[256,1024]{1,0:T(8,128)(2,1)S(1)}, u32[]{:S(2)}, u32[]{:S(2)}) collective-permute-start(bf16[256,1024]{1,0:T(8,128)(2,1)S(1)} %get-tuple-element.83), channel_id=1, source_target_pairs={{0,4},{4,0},{8,12},{12,8},{16,20},{20,16},{24,28},{28,24},{1,5},{5... | collective-permute-start | bytes 1572872 | tf_op jit(solution)/shard_map/ppermute | solution.py:389
  92.2 14.3 %collective-permute-start.10 = (bf16[256,1024]{1,0:T(8,128)(2,1)S(1)}, bf16[256,1024]{1,0:T(8,128)(2,1)S(1)}, u32[]{:S(2)}, u32[]{:S(2)}) collective-permute-start(bf16[256,1024]{1,0:T(8,128)(2,1)S(1)} %add_convert_fusion.4), channel_id=1, source_target_pairs={{0,8},{4,12},{24,16},{28,20},{1,9},{5,13},{25,17},{29,21},{2,10},{... | collective-permute-start | bytes 1572872 | tf_op jit(solution)/shard_map/ppermute | solution.py:386
  95.5 17.3 %collective-permute-start.15 = (bf16[256,1024]{1,0:T(8,128)(2,1)S(1)}, bf16[256,1024]{1,0:T(8,128)(2,1)S(1)}, u32[]{:S(2)}, u32[]{:S(2)}) collective-permute-start(bf16[256,1024]{1,0:T(8,128)(2,1)S(1)} %get-tuple-element.86), channel_id=1, source_target_pairs={{0,4},{4,0},{8,12},{12,8},{16,20},{20,16},{24,28},{28,24},{1,5},{5... | collective-permute-start | bytes 1572872 | tf_op jit(solution)/shard_map/ppermute | solution.py:389
  103.6 14.2 %collective-permute-start.13 = (bf16[256,1024]{1,0:T(8,128)(2,1)S(1)}, bf16[256,1024]{1,0:T(8,128)(2,1)S(1)}, u32[]{:S(2)}, u32[]{:S(2)}) collective-permute-start(bf16[256,1024]{1,0:T(8,128)(2,1)S(1)} %add_convert_fusion.2), channel_id=1, source_target_pairs={{0,8},{4,12},{24,16},{28,20},{1,9},{5,13},{25,17},{29,21},{2,10},{... | collective-permute-start | bytes 1572872 | tf_op jit(solution)/shard_map/ppermute | solution.py:386
  106.7 14.2 %collective-permute-start.11 = (bf16[256,1024]{1,0:T(8,128)(2,1)S(1)}, bf16[256,1024]{1,0:T(8,128)(2,1)S(1)}, u32[]{:S(2)}, u32[]{:S(2)}) collective-permute-start(bf16[256,1024]{1,0:T(8,128)(2,1)S(1)} %add_convert_fusion.3), channel_id=1, source_target_pairs={{8,24},{12,28},{16,0},{20,4},{9,25},{13,29},{17,1},{21,5},{10,26},... | collective-permute-start | bytes 1572872 | tf_op jit(solution)/shard_map/ppermute | solution.py:386
  112.7 13.3 %collective-permute-start.16 = (bf16[256,1024]{1,0:T(8,128)(2,1)S(1)}, bf16[256,1024]{1,0:T(8,128)(2,1)S(1)}, u32[]{:S(2)}, u32[]{:S(2)}) collective-permute-start(bf16[256,1024]{1,0:T(8,128)(2,1)S(1)} %get-tuple-element.87), channel_id=1, source_target_pairs={{0,4},{4,0},{8,12},{12,8},{16,20},{20,16},{24,28},{28,24},{1,5},{5... | collective-permute-start | bytes 1572872 | tf_op jit(solution)/shard_map/ppermute | solution.py:389
  113.5 18.6 %collective-permute-start.17 = (bf16[256,1024]{1,0:T(8,128)(2,1)S(1)}, bf16[256,1024]{1,0:T(8,128)(2,1)S(1)}, u32[]{:S(2)}, u32[]{:S(2)}) collective-permute-start(bf16[256,1024]{1,0:T(8,128)(2,1)S(1)} %add_convert_fusion), channel_id=1, source_target_pairs={{0,8},{4,12},{8,0},{12,4},{16,24},{20,28},{24,16},{28,20},{1,9},{5... | collective-permute-start | bytes 1572872 | tf_op jit(solution)/shard_map/ppermute | solution.py:386
  120.9 11.1 %copy-start.16 = (bf16[256,1024]{1,0:T(8,128)(2,1)}, bf16[256,1024]{1,0:T(8,128)(2,1)S(1)}, u32[]{:S(2)}) copy-start(bf16[256,1024]{1,0:T(8,128)(2,1)S(1)} %collective-permute-done.11.refs_0_) | copy-start | bytes 1572868
  121.1 10.9 %collective-permute-start.14 = (bf16[256,1024]{1,0:T(8,128)(2,1)S(1)}, bf16[256,1024]{1,0:T(8,128)(2,1)S(1)}, u32[]{:S(2)}, u32[]{:S(2)}) collective-permute-start(bf16[256,1024]{1,0:T(8,128)(2,1)S(1)} %add_convert_fusion.1), channel_id=1, source_target_pairs={{8,16},{12,20},{16,8},{20,12},{9,17},{13,21},{17,9},{21,13},{10,18... | collective-permute-start | bytes 1572872 | tf_op jit(solution)/shard_map/ppermute | solution.py:386
  (14 other events, 77.3 us)
